TPU v7x, 128 devices: a whole 4x4x4 slice. The times are simulated.
128 devices in a mesh: cfg: 2 (over x_hi), seq: 16 (over x_lo, y, core), fsdp: 4 (over z).
Axes of the slice: x: 4 (x_hi: 2, x_lo: 2; x = x_hi * 2 + x_lo), y: 4, z: 4, core: 2. Of those that a mesh axis runs over, the one named last changes fastest.
Arguments:
- q_video: bfloat16 [4, 2048, 3072], P('fsdp', 'seq'), may hold values from -30 to 30
- k_video: bfloat16 [4, 2048, 3072], P('fsdp', 'seq'), may hold values from -6 to 6
- v_video: bfloat16 [4, 2048, 3072], P('fsdp', 'seq'), may hold values from -6 to 6
- k_text: bfloat16 [2, 4, 256, 3072], P('cfg', 'fsdp', 'seq'), may hold values from -6 to 6
- v_text: bfloat16 [2, 4, 256, 3072], P('cfg', 'fsdp', 'seq'), may hold values from -6 to 6
- text_len: int32 [2, 4], P(None, 'fsdp'), may hold values from 64 to 256
- guide_index: int32 [4], P('fsdp'), may hold values from 0 to 6
- gate: float32 [4, 3072], P('fsdp'), may hold values from 0.1 to 1.9
- adjoint: bfloat16 [2, 4, 2048, 3072], P('cfg', 'fsdp', 'seq'), may hold values from -12 to 12
- w_out: bfloat16 [3072, 3072], P(('cfg', 'seq', 'fsdp')), may hold values from -0.109375 to 0.109375
Outputs:
- grad_q_video: bfloat16 [4, 2048, 3072], P('fsdp', 'seq')
- grad_k_video: bfloat16 [4, 2048, 3072], P('fsdp', 'seq')
- grad_v_video: bfloat16 [4, 2048, 3072], P('fsdp', 'seq')
- grad_k_text: bfloat16 [2, 4, 256, 3072], P('cfg', 'fsdp', 'seq')
- grad_v_text: bfloat16 [2, 4, 256, 3072], P('cfg', 'fsdp', 'seq')
All inputs are finite; a program needn't handle non-finite values.
Results may differ from a plain program's by a relative error of at most 0.011.
Values may be sent and summed in bfloat16 or wider, within the bound.
No kernel may reach another device: no remote copies, remote signals or barrier semaphores. Data moves between devices by JAX's collectives and lax.ppermute only.
A program may use at most 128 MiB of HBM per device.

v0:
```python
import math

import jax
import jax.numpy as jnp
from jax import lax
from jax.sharding import PartitionSpec as P

HEADS = 24
HD = 128
TXT = 256


def padded_width(head_count, groups, head_dim):
    return -(-head_count // groups) * groups * head_dim


def pad_heads(matrix, full_width):
    missing = full_width - matrix.shape[-1]
    return jnp.pad(matrix, ((0, 0), (0, missing)))


def block_rows_for(row_total):
    block_rows = row_total
    while block_rows > 512 and block_rows % 2 == 0:
        block_rows = block_rows // 2
    return block_rows


def score_block(query_part, keys_video, keys_text, text_valid, factor):
    video_scores = (
        jnp.einsum("qd,kd->qk", query_part, keys_video, preferred_element_type=jnp.float32) * factor
    )
    text_scores = (
        jnp.einsum("qd,ptd->pqt", query_part, keys_text, preferred_element_type=jnp.float32)
        * factor
    )
    text_scores = jnp.where(text_valid[:, None, :], text_scores, -jnp.inf)
    return (video_scores, text_scores)


def forward_block(query_part, keys_video, vals_video, keys_text, vals_text, text_valid, factor):
    video_scores, text_scores = score_block(query_part, keys_video, keys_text, text_valid, factor)
    row_max = jnp.maximum(jnp.max(video_scores, axis=-1)[None, :], jnp.max(text_scores, axis=-1))
    video_exp = jnp.exp(video_scores[None] - row_max[:, :, None])
    text_exp = jnp.exp(text_scores - row_max[:, :, None])
    row_sum = jnp.sum(video_exp, axis=-1) + jnp.sum(text_exp, axis=-1)
    video_prob = video_exp / row_sum[:, :, None]
    text_prob = text_exp / row_sum[:, :, None]
    video_low = video_prob.astype(jnp.bfloat16)
    text_low = text_prob.astype(jnp.bfloat16)
    output = jnp.einsum("pqk,kd->pqd", video_low, vals_video, preferred_element_type=jnp.float32)
    output = output + jnp.einsum(
        "pqt,ptd->pqd", text_low, vals_text, preferred_element_type=jnp.float32
    )
    return ((video_prob, text_prob, video_low, text_low), (output, row_max, row_sum))


def recompute_block(query_part, keys_video, keys_text, text_valid, factor, row_max, row_sum):
    video_scores, text_scores = score_block(query_part, keys_video, keys_text, text_valid, factor)
    video_prob = jnp.exp(video_scores[None] - row_max[:, :, None]) / row_sum[:, :, None]
    text_prob = jnp.exp(text_scores - row_max[:, :, None]) / row_sum[:, :, None]
    return (video_prob, text_prob, video_prob.astype(jnp.bfloat16), text_prob.astype(jnp.bfloat16))


def gradient_block(
    query_part,
    adjoint_part,
    keys_video,
    vals_video,
    keys_text,
    vals_text,
    prob_parts,
    output,
    factor,
):
    video_prob, text_prob, video_low, text_low = prob_parts
    row_delta = jnp.sum(adjoint_part.astype(jnp.float32) * output, axis=-1)[:, :, None]
    video_grad = jnp.einsum(
        "pqd,kd->pqk", adjoint_part, vals_video, preferred_element_type=jnp.float32
    )
    text_grad = jnp.einsum(
        "pqd,ptd->pqt", adjoint_part, vals_text, preferred_element_type=jnp.float32
    )
    video_ds = (video_prob * (video_grad - row_delta)).astype(jnp.bfloat16)
    text_ds = (text_prob * (text_grad - row_delta)).astype(jnp.bfloat16)
    query_grad = jnp.einsum("pqk,kd->pqd", video_ds, keys_video, preferred_element_type=jnp.float32)
    query_grad = (
        query_grad
        + jnp.einsum("pqt,ptd->pqd", text_ds, keys_text, preferred_element_type=jnp.float32)
    ) * factor
    terms = (
        jnp.einsum("pqk,qd->pkd", video_ds, query_part, preferred_element_type=jnp.float32),
        jnp.einsum("pqk,pqd->pkd", video_low, adjoint_part, preferred_element_type=jnp.float32),
        jnp.einsum("pqt,qd->ptd", text_ds, query_part, preferred_element_type=jnp.float32),
        jnp.einsum("pqt,pqd->ptd", text_low, adjoint_part, preferred_element_type=jnp.float32),
    )
    return (query_grad.astype(jnp.bfloat16), terms)


def add_terms(running, terms):
    return tuple((before + update for before, update in zip(running, terms)))


def empty_sums(keys_video, keys_text):
    passes = keys_text.shape[0]
    video_zero = jnp.zeros((passes,) + keys_video.shape, jnp.float32)
    text_zero = jnp.zeros(keys_text.shape, jnp.float32)
    return (video_zero, video_zero, text_zero, text_zero)


def query_layout(queries):
    row_total, head_dim = queries.shape
    block_rows = block_rows_for(row_total)
    block_count = row_total // block_rows
    return (
        1.0 / math.sqrt(head_dim),
        block_rows,
        block_count,
        queries.reshape(block_count, block_rows, head_dim),
    )


def adjoint_layout(adjoint_heads, block_rows, block_count):
    passes, row_total, head_dim = adjoint_heads.shape
    return adjoint_heads.reshape(passes, block_count, block_rows, head_dim).swapaxes(0, 1)


def finish(totals, query_grads, factor):
    key_video, val_video, key_text, val_text = totals
    passes = key_video.shape[0]
    query_grad = query_grads.swapaxes(0, 1).reshape(passes, -1, query_grads.shape[-1])
    return (
        query_grad,
        (key_video * factor).astype(jnp.bfloat16),
        val_video.astype(jnp.bfloat16),
        (key_text * factor).astype(jnp.bfloat16),
        val_text.astype(jnp.bfloat16),
    )


def forward_sweep(queries, keys_video, vals_video, keys_text, vals_text, text_valid):
    factor, block_rows, block_count, query_blocks = query_layout(queries)

    def forward_step(running, query_part):
        prob_parts, stored = forward_block(
            query_part, keys_video, vals_video, keys_text, vals_text, text_valid, factor
        )
        return (running, stored)

    unused, stored = lax.scan(forward_step, jnp.zeros((), jnp.float32), query_blocks)
    return stored


def backward_sweep(
    queries, keys_video, vals_video, keys_text, vals_text, text_valid, adjoint_heads, stored
):
    factor, block_rows, block_count, query_blocks = query_layout(queries)
    adjoint_blocks = adjoint_layout(adjoint_heads, block_rows, block_count)

    def backward_step(running, pieces):
        query_part, adjoint_part, output, row_max, row_sum = pieces
        prob_parts = recompute_block(
            query_part, keys_video, keys_text, text_valid, factor, row_max, row_sum
        )
        query_grad, terms = gradient_block(
            query_part,
            adjoint_part,
            keys_video,
            vals_video,
            keys_text,
            vals_text,
            prob_parts,
            output,
            factor,
        )
        return (add_terms(running, terms), query_grad)

    pieces = (query_blocks, adjoint_blocks, stored[0], stored[1], stored[2])
    totals, query_grads = lax.scan(backward_step, empty_sums(keys_video, keys_text), pieces)
    return finish(totals, query_grads, factor)


def run_heads(queries, keys_video, vals_video, keys_text, vals_text, text_valid, adjoint_heads):
    video_axes = (1, 1, 1, 2, 2, None)
    stored = jax.vmap(forward_sweep, in_axes=video_axes)(
        queries, keys_video, vals_video, keys_text, vals_text, text_valid
    )
    results = jax.vmap(backward_sweep, in_axes=video_axes + (2, 0), out_axes=2)(
        queries, keys_video, vals_video, keys_text, vals_text, text_valid, adjoint_heads, stored
    )
    return results


def local(q_video, k_video, v_video, k_text, v_text, text_len, guide_index, gate, adjoint, w_out):
    model_width = q_video.shape[-1]
    cfg_index = lax.axis_index("cfg")
    guidance = 1.5 + guide_index[0].astype(jnp.float32)
    pass_weight = jnp.where(cfg_index == 0, guidance, 1.0 - guidance)
    scaled = (gate[0][None, :] * pass_weight * adjoint[0, 0].astype(jnp.float32)).astype(
        jnp.bfloat16
    )
    adjoint_out = jnp.einsum(
        "td,nd->tn",
        scaled,
        lax.all_gather(w_out, ("cfg", "seq", "fsdp"), axis=0, tiled=True),
        preferred_element_type=jnp.float32,
    ).astype(jnp.bfloat16)
    position = jnp.arange(TXT, dtype=jnp.int32)
    text_valid = position[None, :] < text_len[:, 0][:, None]
    groups = lax.axis_size("seq")
    full_width = padded_width(HEADS, groups, HD)
    slot_count = full_width // (groups * HD)
    query_sent = pad_heads(q_video[0], full_width)
    key_sent = pad_heads(k_video[0], full_width)
    value_sent = pad_heads(v_video[0], full_width)
    text_key_sent = pad_heads(k_text[0, 0], full_width)
    text_value_sent = pad_heads(v_text[0, 0], full_width)
    received = (
        lax.all_to_all(query_sent, "seq", split_axis=1, concat_axis=0, tiled=True),
        lax.all_to_all(key_sent, "seq", split_axis=1, concat_axis=0, tiled=True),
        lax.all_to_all(value_sent, "seq", split_axis=1, concat_axis=0, tiled=True),
        lax.all_to_all(text_key_sent, "seq", split_axis=1, concat_axis=0, tiled=True),
        lax.all_to_all(text_value_sent, "seq", split_axis=1, concat_axis=0, tiled=True),
    )
    video_total = received[0].shape[0]
    video_heads = [
        received_part.reshape(video_total, slot_count, HD) for received_part in received[:3]
    ]
    text_heads = [received_part.reshape(1, TXT, slot_count, HD) for received_part in received[3:]]
    own_valid = jnp.where(cfg_index == 0, text_valid[0], text_valid[1])[None, :]
    arrived = lax.all_to_all(
        pad_heads(adjoint_out, full_width), "seq", split_axis=1, concat_axis=0, tiled=True
    )
    adjoint_heads = arrived.reshape(1, video_total, slot_count, HD)
    head_grads = run_heads(
        video_heads[0],
        video_heads[1],
        video_heads[2],
        text_heads[0],
        text_heads[1],
        own_valid,
        adjoint_heads,
    )
    video_back = [
        grad_part[0].reshape(video_total, full_width // groups) for grad_part in head_grads[:3]
    ]
    text_back = [grad_part[0].reshape(TXT, full_width // groups) for grad_part in head_grads[3:]]
    returned = (
        lax.all_to_all(video_back[0], "seq", split_axis=0, concat_axis=1, tiled=True),
        lax.all_to_all(video_back[1], "seq", split_axis=0, concat_axis=1, tiled=True),
        lax.all_to_all(video_back[2], "seq", split_axis=0, concat_axis=1, tiled=True),
        lax.all_to_all(text_back[0], "seq", split_axis=0, concat_axis=1, tiled=True),
        lax.all_to_all(text_back[1], "seq", split_axis=0, concat_axis=1, tiled=True),
    )
    summed = (
        lax.psum(returned[0][:, :model_width], "cfg").astype(jnp.float32),
        lax.psum(returned[1][:, :model_width], "cfg").astype(jnp.float32),
        lax.psum(returned[2][:, :model_width], "cfg").astype(jnp.float32),
    )
    video_grads = [total_part.astype(jnp.bfloat16) for total_part in summed]
    text_grads = [returned[3][:, :model_width], returned[4][:, :model_width]]
    return (
        video_grads[0][None],
        video_grads[1][None],
        video_grads[2][None],
        text_grads[0][None, None],
        text_grads[1][None, None],
    )


def solution(mesh):
    placed = (
        P("fsdp", "seq", None),
        P("fsdp", "seq", None),
        P("fsdp", "seq", None),
        P("cfg", "fsdp", "seq", None),
        P("cfg", "fsdp", "seq", None),
        P(None, "fsdp"),
        P("fsdp"),
        P("fsdp", None),
        P("cfg", "fsdp", "seq", None),
        P(("cfg", "seq", "fsdp"), None),
    )
    return jax.shard_map(
        local,
        mesh=mesh,
        in_specs=placed,
        out_specs=(
            P("fsdp", "seq", None),
            P("fsdp", "seq", None),
            P("fsdp", "seq", None),
            P("cfg", "fsdp", "seq", None),
            P("cfg", "fsdp", "seq", None),
        ),
        check_vma=False,
    )
```

profile of v0, /device:TPU:0, one launch (start us, length us, event | category | flops | bytes accessed | tf_op | source)
XLA Modules:
  0.0 418.8 jit_solution(4297552746161061745)
XLA Ops:
  9.5 5.6 %all-to-all-start.2 = ((bf16[16,16,256]{2,0,1:T(8,128)(2,1)}), bf16[16,16,256]{2,0,1:T(8,128)(2,1)S(1)}, u32[]{:S(2)}, u32[]{:S(2)}) async-start(bf16[16,16,256]{2,0,1:T(8,128)(2,1)} %bitcast.239), calls=%async_computation.2 | async-start | bytes 262144 | tf_op jit(solution)/shard_map/all_to_all | solution.py:222
  16.6 5.1 %all-to-all-done.2 = bf16[16,16,256]{2,0,1:T(8,128)(2,1)S(1)} async-done(((bf16[16,16,256]{2,0,1:T(8,128)(2,1)}), bf16[16,16,256]{2,0,1:T(8,128)(2,1)S(1)}, u32[]{:S(2)}, u32[]{:S(2)}) %all-to-all-start.2) | async-done | bytes 131104 | tf_op jit(solution)/shard_map/all_to_all | solution.py:222
  21.8 3.5 all-to-all-start.4
  27.9 4.1 all-to-all-done.4
  32.0 3.7 all-to-all-start
  37.1 18.5 %all-to-all-done = bf16[128,16,256]{0,2,1:T(8,128)(2,1)S(1)} async-done(((bf16[128,16,256]{0,2,1:T(8,128)(2,1)}), bf16[128,16,256]{0,2,1:T(8,128)(2,1)S(1)}, u32[]{:S(2)}, u32[]{:S(2)}) %all-to-all-start) | async-done | bytes 1048608 | tf_op jit(solution)/shard_map/all_to_all | solution.py:219
  55.6 4.3 %all-to-all-start.1 = ((bf16[128,16,256]{0,2,1:T(8,128)(2,1)}), bf16[128,16,256]{0,2,1:T(8,128)(2,1)}, u32[]{:S(2)}, u32[]{:S(2)}) async-start(bf16[128,16,256]{0,2,1:T(8,128)(2,1)} %bitcast.17), calls=%async_computation.1 | async-start | bytes 2097152 | tf_op jit(solution)/shard_map/all_to_all | solution.py:220
  65.2 13.9 %all-to-all-done.1 = bf16[128,16,256]{0,2,1:T(8,128)(2,1)} async-done(((bf16[128,16,256]{0,2,1:T(8,128)(2,1)}), bf16[128,16,256]{0,2,1:T(8,128)(2,1)}, u32[]{:S(2)}, u32[]{:S(2)}) %all-to-all-start.1) | async-done | bytes 1048608 | tf_op jit(solution)/shard_map/all_to_all | solution.py:220
  79.1 4.4 %all-to-all-start.3 = ((bf16[128,16,256]{0,2,1:T(8,128)(2,1)}), bf16[128,16,256]{0,2,1:T(8,128)(2,1)}, u32[]{:S(2)}, u32[]{:S(2)}) async-start(bf16[128,16,256]{0,2,1:T(8,128)(2,1)} %bitcast.323), calls=%async_computation.3 | async-start | bytes 2097152 | tf_op jit(solution)/shard_map/all_to_all | solution.py:221
  101.4 10.1 %all-to-all-done.3 = bf16[128,16,256]{0,2,1:T(8,128)(2,1)} async-done(((bf16[128,16,256]{0,2,1:T(8,128)(2,1)}), bf16[128,16,256]{0,2,1:T(8,128)(2,1)}, u32[]{:S(2)}, u32[]{:S(2)}) %all-to-all-start.3) | async-done | bytes 1048608 | tf_op jit(solution)/shard_map/all_to_all | solution.py:221
  119.2 13.8 %convolution_convert_fusion = bf16[128,3072]{1,0:T(8,128)(2,1)} fusion(bf16[3072,3072]{1,0:T(8,128)(2,1)} %all-gather.2.cloned.1.call-done, bf16[1,1,128,3072]{3,2,1,0:T(8,128)(2,1)} %param.22, f32[3072]{0:T(1024)S(1)} %bitcast.352), kind=kOutput, calls=%fused_computation.91 | convolution fusion | flops 2417491968 | bytes 20459520 | tf_op jit(solution)/shard_map/td,nd->tn/dot_general | solution.py:202
  137.5 4.5 %all-to-all-start.5 = ((bf16[128,16,256]{0,2,1:T(8,128)(2,1)}), bf16[128,16,256]{0,2,1:T(8,128)(2,1)}, u32[]{:S(2)}, u32[]{:S(2)}) async-start(bf16[128,16,256]{0,2,1:T(8,128)(2,1)} %bitcast.321), calls=%async_computation.5 | async-start | bytes 2097152 | tf_op jit(solution)/shard_map/all_to_all | solution.py:231
  142.0 39.5 %while.33 = (s32[]{:T(128)}, f32[4,2,1,512,128]{4,3,1,2,0:T(8,128)}, f32[4,2,1,512]{3,1,2,0:T(2,128)}, f32[4,2,1,512]{3,1,2,0:T(2,128)S(1)}, bf16[4,2,512,128]{3...) while((s32[]{:T(128)}, ...), condition=%wide.region_5.6_spmd, body=%wide.region_0.5_spmd.sunk | while | flops 1229060096 | bytes 37561024 | solution.py:150
  189.0 67.4 %while.34 = (s32[]{:T(128)}, f32[2,1,2048,128]{3,2,0,1:T(8,128)}, f32[2,1,2048,128]{3,2,0,1:T(8,128)S(1)}, f32[2,1,256,128]{3,2,0,1:T(8,128)}, f32[2,1,256,128]{...) while((s32[]{:T(128)}, f32[2,1,2048,128]{3,2,0,1:T(8,128)}, ...), condition=%wide.region_8.9_spmd.clone, body=%wide.region_6.8_spmd.clone.sunk | while | flops 3039820800 | bytes 91665336 | solution.py:179
  259.3 5.5 %all-to-all-start.6 = ((bf16[16,128,256]{1,2,0:T(8,128)(2,1)}), bf16[16,128,256]{1,2,0:T(8,128)(2,1)}, u32[]{:S(2)}, u32[]{:S(2)}) async-start(bf16[16,128,256]{1,2,0:T(8,128)(2,1)} %copy.118), calls=%async_computation.6 | async-start | bytes 2097152 | tf_op jit(solution)/shard_map/all_to_all | solution.py:249
  270.7 10.7 %all-to-all-done.6 = bf16[16,128,256]{1,2,0:T(8,128)(2,1)} async-done(((bf16[16,128,256]{1,2,0:T(8,128)(2,1)}), bf16[16,128,256]{1,2,0:T(8,128)(2,1)}, u32[]{:S(2)}, u32[]{:S(2)}) %all-to-all-start.6) | async-done | bytes 1048608 | tf_op jit(solution)/shard_map/all_to_all | solution.py:249
  281.5 4.6 %all-to-all-start.7 = ((bf16[16,128,256]{1,2,0:T(8,128)(2,1)}), bf16[16,128,256]{1,2,0:T(8,128)(2,1)}, u32[]{:S(2)}, u32[]{:S(2)}) async-start(bf16[16,128,256]{1,2,0:T(8,128)(2,1)} %copy.120), calls=%async_computation.7 | async-start | bytes 2097152 | tf_op jit(solution)/shard_map/all_to_all | solution.py:250
  288.1 14.4 %all-to-all-done.7 = bf16[16,128,256]{1,2,0:T(8,128)(2,1)} async-done(((bf16[16,128,256]{1,2,0:T(8,128)(2,1)}), bf16[16,128,256]{1,2,0:T(8,128)(2,1)}, u32[]{:S(2)}, u32[]{:S(2)}) %all-to-all-start.7) | async-done | bytes 1048608 | tf_op jit(solution)/shard_map/all_to_all | solution.py:250
  302.4 3.7 all-to-all-start.8
  310.3 12.4 %all-to-all-done.8 = bf16[16,128,256]{1,2,0:T(8,128)(2,1)S(1)} async-done(((bf16[16,128,256]{1,2,0:T(8,128)(2,1)}), bf16[16,128,256]{1,2,0:T(8,128)(2,1)S(1)}, u32[]{:S(2)}, u32[]{:S(2)}) %all-to-all-start.8) | async-done | bytes 1048608 | tf_op jit(solution)/shard_map/all_to_all | solution.py:251
  328.9 5.8 %all-to-all-done.9 = bf16[16,16,256]{2,1,0:T(8,128)(2,1)S(1)} async-done(((bf16[16,16,256]{2,1,0:T(8,128)(2,1)}), bf16[16,16,256]{2,1,0:T(8,128)(2,1)S(1)}, u32[]{:S(2)}, u32[]{:S(2)}) %all-to-all-start.9) | async-done | bytes 131104 | tf_op jit(solution)/shard_map/all_to_all | solution.py:252
  334.7 3.5 all-to-all-start.10
  338.3 8.3 %all-to-all-done.10 = bf16[16,16,256]{2,1,0:T(8,128)(2,1)S(1)} async-done(((bf16[16,16,256]{2,1,0:T(8,128)(2,1)}), bf16[16,16,256]{2,1,0:T(8,128)(2,1)S(1)}, u32[]{:S(2)}, u32[]{:S(2)}) %all-to-all-start.10) | async-done | bytes 131104 | tf_op jit(solution)/shard_map/all_to_all | solution.py:253
  347.9 57.2 %all-reduce.9.cloned.1.call-done = (bf16[1,128,3072]{1,2,0:T(8,128)(2,1)}, bf16[1,128,3072]{1,2,0:T(8,128)(2,1)}, bf16[1,128,3072]{1,2,0:T(8,128)(2,1)}) async-done(((bf16[1,128,3072]{1,2,0:T(8,128)(2,1)}, bf16[1,128,3072]{1,2,0:T(8,128)(2,1)}, bf16[1,128,3072]{1,2,0:T(8,128)(2,1)}), (bf16[1,128,3072]{1,2,0:T(8,128)(2,1)}, bf16[1,128,3072]{1,2,0:T(8,128)(2,1)}, ...) | async-done | bytes 2359312 | tf_op jit(solution)/shard_map/psum | solution.py:256
  (242 shorter events, 185.3 us)
Async XLA Ops:
  7.2 28.5 %copy-start.11 = (bf16[1,128,3072]{2,1,0:T(8,128)(2,1)S(1)}, bf16[1,128,3072]{2,1,0:T(8,128)(2,1)}, u32[]{:S(2)}) copy-start(bf16[1,128,3072]{2,1,0:T(8,128)(2,1)} %param.15) | copy-start | bytes 2359300
  7.2 112.0 %all-gather.2.cloned.1.call-start = ((), (), s32[]{:S(2)}) async-start(), calls=%async_computation.11 | async-start | bytes 19021824 | tf_op jit(solution)/shard_map/all_gather | solution.py:205
  9.5 12.3 %all-to-all-start.2 = ((bf16[16,16,256]{2,0,1:T(8,128)(2,1)}), bf16[16,16,256]{2,0,1:T(8,128)(2,1)S(1)}, u32[]{:S(2)}, u32[]{:S(2)}) async-start(bf16[16,16,256]{2,0,1:T(8,128)(2,1)} %bitcast.239), calls=%async_computation.2 | async-start | bytes 262144 | tf_op jit(solution)/shard_map/all_to_all | solution.py:222
  21.8 10.2 %all-to-all-start.4 = ((bf16[16,16,256]{2,0,1:T(8,128)(2,1)}), bf16[16,16,256]{2,0,1:T(8,128)(2,1)S(1)}, u32[]{:S(2)}, u32[]{:S(2)}) async-start(bf16[16,16,256]{2,0,1:T(8,128)(2,1)} %bitcast.238), calls=%async_computation.4 | async-start | bytes 262144 | tf_op jit(solution)/shard_map/all_to_all | solution.py:223
  32.0 28.0 %copy-start.12 = (bf16[16,16,256]{2,0,1:T(8,128)(2,1)}, bf16[16,16,256]{2,0,1:T(8,128)(2,1)S(1)}, u32[]{:S(2)}) copy-start(bf16[16,16,256]{2,0,1:T(8,128)(2,1)S(1)} %all-to-all-done.4) | copy-start | bytes 393220
  32.0 23.6 %all-to-all-start = ((bf16[128,16,256]{0,2,1:T(8,128)(2,1)}), bf16[128,16,256]{0,2,1:T(8,128)(2,1)S(1)}, u32[]{:S(2)}, u32[]{:S(2)}) async-start(bf16[128,16,256]{0,2,1:T(8,128)(2,1)} %bitcast.11), calls=%async_computation | async-start | bytes 2097152 | tf_op jit(solution)/shard_map/all_to_all | solution.py:219
  37.1 46.4 %copy-start.14 = (s32[2,1]{0,1:T(1,128)S(1)}, s32[2,1]{0,1:T(1,128)}, u32[]{:S(2)}) copy-start(s32[2,1]{0,1:T(1,128)} %param.19) | copy-start | bytes 28
  55.6 23.5 %all-to-all-start.1 = ((bf16[128,16,256]{0,2,1:T(8,128)(2,1)}), bf16[128,16,256]{0,2,1:T(8,128)(2,1)}, u32[]{:S(2)}, u32[]{:S(2)}) async-start(bf16[128,16,256]{0,2,1:T(8,128)(2,1)} %bitcast.17), calls=%async_computation.1 | async-start | bytes 2097152 | tf_op jit(solution)/shard_map/all_to_all | solution.py:220
  79.1 32.4 %all-to-all-start.3 = ((bf16[128,16,256]{0,2,1:T(8,128)(2,1)}), bf16[128,16,256]{0,2,1:T(8,128)(2,1)}, u32[]{:S(2)}, u32[]{:S(2)}) async-start(bf16[128,16,256]{0,2,1:T(8,128)(2,1)} %bitcast.323), calls=%async_computation.3 | async-start | bytes 2097152 | tf_op jit(solution)/shard_map/all_to_all | solution.py:221
  133.0 9.0 %copy-start.13 = (f32[4,2,1,512]{3,1,2,0:T(2,128)S(1)}, f32[4,2,1,512]{3,1,2,0:T(2,128)}, u32[]{:S(2)}) copy-start(f32[4,2,1,512]{3,1,2,0:T(2,128)} %custom-call.6) | copy-start | bytes 49156
  137.5 44.0 %all-to-all-start.5 = ((bf16[128,16,256]{0,2,1:T(8,128)(2,1)}), bf16[128,16,256]{0,2,1:T(8,128)(2,1)}, u32[]{:S(2)}, u32[]{:S(2)}) async-start(bf16[128,16,256]{0,2,1:T(8,128)(2,1)} %bitcast.321), calls=%async_computation.5 | async-start | bytes 2097152 | tf_op jit(solution)/shard_map/all_to_all | solution.py:231
  189.0 3.6 copy-start.2
  189.0 4.0 copy-start.10
  205.8 3.6 copy-start.2
  205.8 4.0 copy-start.10
  222.7 4.0 copy-start.10
  239.5 4.0 copy-start.10
  259.3 22.1 %all-to-all-start.6 = ((bf16[16,128,256]{1,2,0:T(8,128)(2,1)}), bf16[16,128,256]{1,2,0:T(8,128)(2,1)}, u32[]{:S(2)}, u32[]{:S(2)}) async-start(bf16[16,128,256]{1,2,0:T(8,128)(2,1)} %copy.118), calls=%async_computation.6 | async-start | bytes 2097152 | tf_op jit(solution)/shard_map/all_to_all | solution.py:249
  281.5 20.9 %all-to-all-start.7 = ((bf16[16,128,256]{1,2,0:T(8,128)(2,1)}), bf16[16,128,256]{1,2,0:T(8,128)(2,1)}, u32[]{:S(2)}, u32[]{:S(2)}) async-start(bf16[16,128,256]{1,2,0:T(8,128)(2,1)} %copy.120), calls=%async_computation.7 | async-start | bytes 2097152 | tf_op jit(solution)/shard_map/all_to_all | solution.py:250
  288.1 35.5 %copy-start.8 = (f32[2,1,256,128]{3,2,0,1:T(8,128)S(1)}, f32[2,1,256,128]{3,2,0,1:T(8,128)}, u32[]{:S(2)}) copy-start(f32[2,1,256,128]{3,2,0,1:T(8,128)} %get-tuple-element.151) | copy-start | bytes 786436
  302.4 20.2 %all-to-all-start.8 = ((bf16[16,128,256]{1,2,0:T(8,128)(2,1)}), bf16[16,128,256]{1,2,0:T(8,128)(2,1)S(1)}, u32[]{:S(2)}, u32[]{:S(2)}) async-start(bf16[16,128,256]{1,2,0:T(8,128)(2,1)} %copy.122), calls=%async_computation.8 | async-start | bytes 2097152 | tf_op jit(solution)/shard_map/all_to_all | solution.py:251
  306.1 99.0 %all-reduce.9.cloned.1.call-start = ((), (), s32[]{:S(2)}) async-start(), calls=%async_computation.12 | async-start | bytes 4718592 | tf_op jit(solution)/shard_map/psum | solution.py:256
  324.5 10.2 %all-to-all-start.9 = ((bf16[16,16,256]{2,1,0:T(8,128)(2,1)}), bf16[16,16,256]{2,1,0:T(8,128)(2,1)S(1)}, u32[]{:S(2)}, u32[]{:S(2)}) async-start(bf16[16,16,256]{2,1,0:T(8,128)(2,1)} %all_to_all.172), calls=%async_computation.9 | async-start | bytes 262144 | tf_op jit(solution)/shard_map/all_to_all | solution.py:252
  334.7 11.9 %all-to-all-start.10 = ((bf16[16,16,256]{2,1,0:T(8,128)(2,1)}), bf16[16,16,256]{2,1,0:T(8,128)(2,1)S(1)}, u32[]{:S(2)}, u32[]{:S(2)}) async-start(bf16[16,16,256]{2,1,0:T(8,128)(2,1)} %all_to_all.176), calls=%async_computation.10 | async-start | bytes 262144 | tf_op jit(solution)/shard_map/all_to_all | solution.py:253
  (34 other events, 75.7 us)
Sparse Core Ops, SparseCore 0:
  11.1 102.5 all-gather.1
  323.7 81.3 all-reduce.8
where the time goes:
time: 422 us; the launch traced here: 419 us
  waiting for transfers between devices  161 us (38%)
  matrix products  96.3 us (23%)
  local copies, waits for them, and re-layouts  78.8 us (19%)
  starting transfers between devices  46.7 us (11%)
  other arithmetic  19.8 us (5%)
  between operations  15 us (4%)
    psum x1, waiting for transfers between devices, local(): lax.psum(returned[0][:, :model_width], 'cfg').astype(jnp.float32)  57.2 us
    all_to_all x1, waiting for transfers between devices, local(): lax.all_to_all(query_sent, 'seq', split_axis=1, concat_axis=0, tiled=True)  18.5 us
    dot_general x8, matrix products, score_block(): jnp.einsum('qd,kd->qk', query_part, keys_video, preferred_element_type=jn...  18.1 us
    unnamed x22, local copies, waits for them, and re-layouts  17.9 us
    all_to_all x1, waiting for transfers between devices, local(): lax.all_to_all(video_back[1], 'seq', split_axis=0, concat_axis=1, tiled=T...  14.4 us
    all_to_all x1, waiting for transfers between devices, local(): lax.all_to_all(key_sent, 'seq', split_axis=1, concat_axis=0, tiled=True)  13.9 us
    dot_general x1, matrix products, local(): jnp.einsum('td,nd->tn', scaled, lax.all_gather(w_out, ('cfg', 'seq', 'fsd...  13.8 us
    all_to_all x1, waiting for transfers between devices, local(): lax.all_to_all(video_back[2], 'seq', split_axis=0, concat_axis=1, tiled=T...  12.4 us
  transfers between devices with their start and end apart: 13, of which 11 were waited for; matrix products, arithmetic and copies ran while one was open for 21% of the time, Pallas kernels for 0%

commit v1 on v0

v1 whole, which is shorter than its diff:
```python
import math

import jax
import jax.numpy as jnp
from jax import lax
from jax.experimental import pallas as pl
from jax.experimental.pallas import tpu as pltpu
from jax.sharding import PartitionSpec as P

HD = 128
TOK = 128
TT = 16
XW = 768
XH = 384
WROWS = 96
SCALE = 1.0 / math.sqrt(HD)
EXP2 = SCALE * math.log2(math.e)
VIDK = 2048
TXTK = 256


def dot(a, b, dims):
    return lax.dot_general(a, b, (dims, ((), ())), preferred_element_type=jnp.float32)


NT = ((1,), (1,))
NN = ((1,), (0,))
TN = ((0,), (0,))


def attn_kernel(bias_ref, q_ref, do_ref, k_ref, v_ref, dq_ref, dk_ref, dv_ref, dk_acc, dv_acc, ds_ref):
    step = pl.program_id(0)
    last = pl.num_programs(0) - 1
    q = q_ref[...]
    v_video = v_ref[:VIDK]
    s = dot(q, k_ref[:VIDK], NT)
    mv = jnp.max(s, axis=1, keepdims=True)
    e = jnp.exp2((s - mv) * EXP2)
    lv = jnp.sum(e, axis=1, keepdims=True)
    eb = e.astype(jnp.bfloat16)
    ov = dot(eb, v_video, NN)
    g = jnp.zeros(q.shape, jnp.float32)
    delta = jnp.zeros(lv.shape, jnp.float32)
    pbs = []
    for p in range(2):
        rows = slice(VIDK + p * TXTK, VIDK + (p + 1) * TXTK)
        vt = v_ref[rows]
        st = dot(q, k_ref[rows], NT) + bias_ref[p:p + 1, :]
        m = jnp.maximum(mv, jnp.max(st, axis=1, keepdims=True))
        a = jnp.exp2((mv - m) * EXP2)
        et = jnp.exp2((st - m) * EXP2)
        inv = 1.0 / (a * lv + jnp.sum(et, axis=1, keepdims=True))
        w = a * inv
        pt = et * inv
        ptb = pt.astype(jnp.bfloat16)
        do = do_ref[:, p].reshape(q.shape)
        do32 = do.astype(jnp.float32)
        o = w * ov + dot(ptb, vt, NN)
        dl = jnp.sum(do32 * o, axis=1, keepdims=True)
        g = g + w * do32
        delta = delta + w * dl
        dst = pt * (dot(do, vt, NT) - dl)
        ds_ref[:, rows] = dst.astype(jnp.bfloat16)
        pbs.append((ptb, do))
    gb = g.astype(jnp.bfloat16)
    delta = delta + jnp.sum((gb.astype(jnp.float32) - g) * ov, axis=1, keepdims=True) / lv
    dp = dot(gb, v_video, NT)
    ds_ref[:, :VIDK] = (e * (dp - delta)).astype(jnp.bfloat16)
    ds = ds_ref[...]
    dq_ref[...] = (dot(ds, k_ref[...], NN) * SCALE).astype(jnp.bfloat16)
    dk = dot(ds, q, TN)
    dv = jnp.concatenate([dot(eb, gb, TN)] + [dot(ptb, do, TN) for ptb, do in pbs], axis=0)

    @pl.when(step == 0)
    def _():
        dk_acc[...] = dk
        dv_acc[...] = dv

    @pl.when(step > 0)
    def _():
        dk_acc[...] += dk
        dv_acc[...] += dv

    @pl.when(step == last)
    def _():
        dk_ref[...] = (dk_acc[...] * SCALE).astype(jnp.bfloat16)
        dv_ref[...] = dv_acc[...].astype(jnp.bfloat16)


def attention(bias, q, do, k, v, block=256):
    nq = q.shape[0]
    per = do.shape[2]
    nk = k.shape[0]
    full = lambda *shape: pl.BlockSpec(shape, lambda i: (0,) * len(shape))
    return pl.pallas_call(
        attn_kernel,
        grid=(nq // block,),
        in_specs=[
            full(2, TXTK),
            pl.BlockSpec((block, HD), lambda i: (i, 0)),
            pl.BlockSpec((block // per, 2, per, HD), lambda i: (i, 0, 0, 0)),
            full(nk, HD),
            full(nk, HD),
        ],
        out_specs=[
            pl.BlockSpec((block, HD), lambda i: (i, 0)),
            full(nk, HD),
            full(nk, HD),
        ],
        out_shape=[
            jax.ShapeDtypeStruct((nq, HD), jnp.bfloat16),
            jax.ShapeDtypeStruct((nk, HD), jnp.bfloat16),
            jax.ShapeDtypeStruct((nk, HD), jnp.bfloat16),
        ],
        scratch_shapes=[
            pltpu.VMEM((nk, HD), jnp.float32),
            pltpu.VMEM((nk, HD), jnp.float32),
            pltpu.VMEM((block, nk), jnp.bfloat16),
        ],
        compiler_params=pltpu.CompilerParams(vmem_limit_bytes=48 * 1024 * 1024),
        cost_estimate=pl.CostEstimate(flops=12 * nq * nk * HD, bytes_accessed=4 * nk * HD * 2, transcendentals=nq * nk),
    )(bias, q, do, k, v)


def swap(a, axis):
    return lax.ppermute(a, axis, [(0, 1), (1, 0)])


def x_swap(a, r):
    if r == 1:
        return swap(a, "xlo")
    if r == 2:
        return swap(a, "cfg")
    return lax.ppermute(a, ("cfg", "xlo"), [(i, 3 - i) for i in range(4)])


def y_swap(a, r):
    return lax.ppermute(a, "y", [(i, i ^ r) for i in range(4)])


def cols(a, start, width):
    return lax.dynamic_slice_in_dim(a, start, width, axis=a.ndim - 1)


def own_head(a, y):
    return cols(a, y * HD, HD)


def shared_head(a, y):
    return cols(a, (4 + y // 2) * HD, HD)


def half_rows(a, y):
    return lax.dynamic_slice_in_dim(a, (y % 2) * (TOK // 2), TOK // 2, axis=a.ndim - 2)


def flat(*parts):
    return jnp.concatenate([part.reshape(-1, HD) for part in parts], axis=0)


def project_kernel(place_ref, *refs):
    y, c = place_ref[0], place_ref[1]
    w_refs, a_refs = refs[:8], refs[8:13]
    out_ref, w_all, a_all, sems = refs[13:]
    copies = []
    for other in range(2):
        for r in range(4):
            row = pl.multiple_of(((y ^ r) * 2 + (c ^ other)) * WROWS, WROWS)
            copies.append((w_refs[other * 4 + r], w_all.at[pl.ds(row, WROWS)]))
    row = 0
    for a_ref in a_refs:
        count = a_ref.shape[0]
        copies.append((a_ref, a_all.at[pl.ds(row, count)]))
        row += count
    started = [
        pltpu.make_async_copy(src, dst, sems.at[i]) for i, (src, dst) in enumerate(copies)
    ]
    for copy in started:
        copy.start()
    for copy in started:
        copy.wait()
    out_ref[...] = dot(a_all[...], w_all[...], NT).astype(jnp.bfloat16)


def project(place, w_pieces, a_pieces):
    rows = sum(a.shape[0] for a in a_pieces)
    width = w_pieces[0].shape[1]
    count = len(w_pieces) * w_pieces[0].shape[0]
    pieces = len(w_pieces) + len(a_pieces)
    return pl.pallas_call(
        project_kernel,
        in_specs=[pl.BlockSpec(memory_space=pltpu.SMEM)]
        + [pl.BlockSpec(memory_space=pl.ANY)] * pieces,
        out_specs=pl.BlockSpec(memory_space=pltpu.VMEM),
        out_shape=jax.ShapeDtypeStruct((rows, count), jnp.bfloat16),
        scratch_shapes=[
            pltpu.VMEM((count, width), jnp.bfloat16),
            pltpu.VMEM((rows, width), jnp.bfloat16),
            pltpu.SemaphoreType.DMA((pieces,)),
        ],
        compiler_params=pltpu.CompilerParams(vmem_limit_bytes=40 * 1024 * 1024),
        cost_estimate=pl.CostEstimate(
            flops=2 * rows * count * width,
            bytes_accessed=2 * (rows + count) * width + 2 * rows * count,
            transcendentals=0,
        ),
    )(place, *w_pieces, *a_pieces)


def local(q_video, k_video, v_video, k_text, v_text, text_len, guide_index, gate, adjoint, w_out):
    h = lax.axis_index("cfg")
    l = lax.axis_index("xlo")
    y = lax.axis_index("y")
    c = lax.axis_index("core")
    x = 2 * h + l
    q, k, v = q_video[0], k_video[0], v_video[0]
    kt, vt = k_text[0, 0], v_text[0, 0]

    guidance = 1.5 + guide_index[0].astype(jnp.float32)
    pass_weight = jnp.where(h == 0, guidance, 1.0 - guidance)
    scaled = (gate[0][None, :] * pass_weight * adjoint[0, 0].astype(jnp.float32)).astype(
        jnp.bfloat16
    )
    scaled1 = x_swap(scaled, 1)
    scaled3 = x_swap(scaled, 3)
    half = TOK // 2
    scaled2a = x_swap(scaled3[:half], 1)
    scaled2b = x_swap(scaled1[half:], 3)

    w_z = lax.all_gather(w_out, "fsdp", axis=0, tiled=True)
    w_own = [w_z] + [y_swap(w_z, r) for r in (1, 2, 3)]
    w_other = [swap(piece, "core") for piece in w_own]

    def text_rows(r):
        parts = [cols(a, (x ^ r) * XW, XW) for a in (kt, vt)]
        return [part[:, i * XH : (i + 1) * XH] for part in parts for i in range(2)]

    def video_rows(r, place):
        return [cols(a, (x ^ r) * XW + place * XH, XH) for a in (q, k, v)]

    got1 = x_swap(jnp.concatenate(video_rows(1, 0) + text_rows(1), axis=0), 1)
    got3 = x_swap(jnp.concatenate(video_rows(3, 1) + text_rows(3), axis=0), 3)
    got2 = x_swap(jnp.concatenate(text_rows(2), axis=0), 2)

    def video_at(i):
        own = cols((q, k, v)[i], x * XW, XW)
        rows = slice(i * TOK, (i + 1) * TOK)
        other = jnp.concatenate([got1[rows], got3[rows]], axis=1)
        return jnp.stack([own, other])

    q6, k6, v6 = video_at(0), video_at(1), video_at(2)

    def text_at(i):
        own = cols((kt, vt)[i], x * XW, XW)
        parts = [own]
        for got, start in ((got1, 3 * TOK), (got2, 0), (got3, 3 * TOK)):
            row = start + 2 * i * TT
            parts.append(jnp.concatenate([got[row : row + TT], got[row + TT : row + 2 * TT]], axis=1))
        return jnp.stack(parts)

    kt6, vt6 = text_at(0), text_at(1)

    def message(yd):
        return flat(
            own_head(k6, yd),
            own_head(v6, yd),
            own_head(kt6, yd),
            own_head(vt6, yd),
            shared_head(k6, yd),
            shared_head(v6, yd),
            shared_head(kt6, yd),
            shared_head(vt6, yd),
            own_head(q6, yd),
            half_rows(shared_head(q6, yd), yd),
        )

    arrived = jnp.stack([message(y)] + [y_swap(message(y ^ r), r) for r in (1, 2, 3)])
    kv_rows = 2 * (4 * TOK + 8 * TT)
    other_kv = swap(arrived[:, :kv_rows], "core")
    both = jnp.stack([arrived[:, :kv_rows], other_kv])

    def keys_values(head):
        start = head * (kv_rows // 2)
        out = []
        for i in range(2):
            video = both[:, :, start + i * 2 * TOK : start + (i + 1) * 2 * TOK]
            row = start + 4 * TOK + i * 4 * TT
            text = [both[:, :, row + p * 2 * TT : row + (p + 1) * 2 * TT] for p in range(2)]
            out.append(flat(video, *text))
        return out

    k_a, v_a = keys_values(0)
    k_b, v_b = keys_values(1)
    q_a = arrived[:, kv_rows : kv_rows + 2 * TOK].reshape(-1, HD)
    q_b = arrived[:, kv_rows + 2 * TOK :].reshape(-1, HD)

    lc = jnp.arange(2, dtype=jnp.int32)
    at_core = (c ^ lc)[:, None, None, None]
    at_y = (y ^ jnp.arange(4, dtype=jnp.int32))[None, :, None, None]
    at_l = (l ^ lc)[None, None, :, None]
    position = ((at_l * 4 + at_y) * 2 + at_core) * TT + jnp.arange(TT, dtype=jnp.int32)
    position = position.reshape(1, -1)
    lens = jnp.where(h == 0, text_len[:, 0], text_len[::-1, 0])
    bias = jnp.where(position < lens[:, None], 0.0, -jnp.inf).astype(jnp.float32)

    place = jnp.stack([y, c]).astype(jnp.int32)
    adj = project(place, w_own + w_other, [scaled, scaled1, scaled2a, scaled2b, scaled3])
    adj = adj.reshape(4, TOK, XW)

    def adj_b(yd):
        return half_rows(shared_head(adj, yd), yd).reshape(2, TOK, HD)

    def adj_a(yd):
        return own_head(adj, yd).reshape(2, 2 * TOK, HD)

    do_b = jnp.stack([adj_b(y)] + [y_swap(adj_b(y ^ r), r) for r in (1, 2, 3)])
    do_a = jnp.stack([adj_a(y)] + [y_swap(adj_a(y ^ r), r) for r in (1, 2, 3)])

    dq_b, dk_b, dv_b = attention(bias, q_b, do_b, k_b, v_b)
    dq_a, dk_a, dv_a = attention(bias, q_a, do_a, k_a, v_a)

    def split_core(a):
        video = a[:VIDK].reshape(2, 4, 2 * TOK, HD)
        text = a[VIDK:].reshape(2, 2, 4, 2 * TT, HD)
        text = jnp.moveaxis(text, 0, 2)
        return jnp.concatenate([video, text.reshape(2, 4, 4 * TT, HD)], axis=2)

    pieces = [split_core(a) for a in (dk_a, dv_a, dk_b, dv_b)]
    sent = jnp.stack([piece[1] for piece in pieces])
    kept = jnp.stack([piece[0] for piece in pieces])
    came = swap(sent, "core")
    summed = (kept.astype(jnp.float32) + came.astype(jnp.float32)).astype(jnp.bfloat16)
    dq_a = dq_a.reshape(4, 2 * TOK, HD)
    dq_b = dq_b.reshape(4, TOK, HD)

    def back(r):
        return flat(summed[:, r], dq_a[r], dq_b[r])

    returned = jnp.stack([back(0)] + [y_swap(back(r), r) for r in (1, 2, 3)])
    rows = 2 * TOK + 4 * TT

    def order_heads(head_a, head_b):
        parts = [lax.dynamic_index_in_dim(head_a, y ^ j, 0, False) for j in range(4)]
        parts += [lax.dynamic_index_in_dim(head_b, (y // 2) ^ j, 0, False) for j in range(2)]
        return jnp.concatenate(parts, axis=-1)

    def key_value(i):
        head_a = returned[:, i * rows : (i + 1) * rows]
        head_b = returned[:, (2 + i) * rows : (3 + i) * rows].astype(jnp.float32)
        head_b = (head_b[0::2] + head_b[1::2]).astype(jnp.bfloat16)
        return order_heads(head_a, head_b)

    def query():
        head_a = returned[:, 4 * rows : 4 * rows + 2 * TOK]
        head_b = returned[:, 4 * rows + 2 * TOK :].reshape(2, 2, 2, TOK // 2, HD)
        first = lax.dynamic_index_in_dim(head_b, y % 2, 1, False)
        second = lax.dynamic_index_in_dim(head_b, 1 - y % 2, 1, False)
        head_b = jnp.stack([first, second], axis=2).reshape(2, 2 * TOK, HD)
        return order_heads(head_a, head_b)

    dq6 = query()
    dk6, dv6 = key_value(0), key_value(1)
    own_rows = [dq6[:TOK], dk6[:TOK], dv6[:TOK]]
    far_rows = [dq6[TOK:], dk6[TOK : 2 * TOK], dv6[TOK : 2 * TOK]]

    def text_of(r):
        return [a[2 * TOK + r * TT : 2 * TOK + (r + 1) * TT] for a in (dk6, dv6)]

    final = jnp.stack(
        [
            jnp.concatenate(own_rows + text_of(0), axis=0),
            x_swap(jnp.concatenate(far_rows + text_of(1), axis=0), 1),
            x_swap(jnp.concatenate(own_rows + text_of(2), axis=0), 2),
            x_swap(jnp.concatenate(far_rows + text_of(3), axis=0), 3),
        ]
    )

    def whole(start, count):
        part = final[:, start : start + count]
        return jnp.concatenate(
            [lax.dynamic_index_in_dim(part, x ^ j, 0, False) for j in range(4)], axis=1
        )

    return (
        whole(0, TOK)[None],
        whole(TOK, TOK)[None],
        whole(2 * TOK, TOK)[None],
        whole(3 * TOK, TT)[None, None],
        whole(3 * TOK + TT, TT)[None, None],
    )


def solution(mesh):
    devices = mesh.devices
    fine = jax.sharding.Mesh(
        devices.reshape(2, 2, 4, 2, devices.shape[-1]), ("cfg", "xlo", "y", "core", "fsdp")
    )
    seq = ("xlo", "y", "core")
    video = P("fsdp", seq, None)
    per_pass = P("cfg", "fsdp", seq, None)
    placed = (
        video,
        video,
        video,
        per_pass,
        per_pass,
        P(None, "fsdp"),
        P("fsdp"),
        P("fsdp", None),
        per_pass,
        P(("cfg",) + seq + ("fsdp",), None),
    )
    return jax.shard_map(
        local,
        mesh=fine,
        in_specs=placed,
        out_specs=(video, video, video, per_pass, per_pass),
        check_vma=False,
    )
```

time: 422 us -> 213 us (0.50)
  matrix products: 96.3 us -> 0 us
  waiting for transfers between devices: 161 us -> 95.7 us
  local copies, waits for them, and re-layouts: 78.8 us -> 23.7 us
  Pallas kernels: 0 us -> 26.3 us
  blocking collectives: 0 us -> 14.5 us
  between operations: 15 us -> 2.56 us
  starting transfers between devices: 46.7 us -> 36.8 us
  other arithmetic: 19.8 us -> 13 us
    all_to_all x11 -> x0, waiting for transfers between devices: 103 us -> none  [the longest x1 18.5 us: local(): lax.all_to_all(query_sent, 'seq', split_axis=1, concat_axis=0, tiled=True)]
    dot_general x57 -> x0, matrix products: 96.3 us -> none  [the longest x8 18.1 us: score_block(): jnp.einsum('qd,kd->qk', query_part, keys_video, preferred_element_type=jn...]
    ppermute x0 -> x31, waiting for transfers between devices: none -> 95.7 us  [the longest x15 48.8 us: y_swap(): return lax.ppermute(a, 'y', [(i, i ^ r) for i in range(4)])]
    psum x1 -> x0, waiting for transfers between devices: 57.2 us -> none  [local(): lax.psum(returned[0][:, :model_width], 'cfg').astype(jnp.float32)]
    all_to_all x11 -> x0, starting transfers between devices: 46.7 us -> none  [the longest x1 5.59 us: local(): lax.all_to_all(text_key_sent, 'seq', split_axis=1, concat_axis=0, tiled=T...]
    ppermute x0 -> x31, starting transfers between devices: none -> 36.8 us  [the longest x15 21.9 us: y_swap(): return lax.ppermute(a, 'y', [(i, i ^ r) for i in range(4)])]
    pallas_call x0 -> x3, Pallas kernels: none -> 26.3 us  [the longest x2 20.9 us: attention(): pl.pallas_call(attn_kernel, grid=(nq // block,), in_specs=[full(2, TXTK),...]
    all_to_all x13 -> x0, local copies, waits for them, and re-layouts: 16.1 us -> none  [the longest x1 2.98 us: local(): lax.all_to_all(value_sent, 'seq', split_axis=1, concat_axis=0, tiled=True)]
  transfers between devices with their start and end apart: 13 -> 31, of which waited for: 11 -> 16; matrix products, arithmetic and copies ran while one was open for 21% -> 11% of each run, Pallas kernels for 0% -> 3%
where the time goes in v1:
time: 213 us
  waiting for transfers between devices  95.7 us (45%)
  starting transfers between devices  36.8 us (17%)
  Pallas kernels  26.3 us (12%)
  local copies, waits for them, and re-layouts  23.7 us (11%)
  blocking collectives  14.5 us (7%)
  other arithmetic  13 us (6%)
  between operations  2.56 us (1%)
    ppermute x15, waiting for transfers between devices, y_swap(): return lax.ppermute(a, 'y', [(i, i ^ r) for i in range(4)])  48.8 us
    ppermute x4, waiting for transfers between devices, x_swap(): return lax.ppermute(a, ('cfg', 'xlo'), [(i, 3 - i) for i in range(4)])  30.8 us
    ppermute x15, starting transfers between devices, y_swap(): return lax.ppermute(a, 'y', [(i, i ^ r) for i in range(4)])  21.9 us
    pallas_call x2, Pallas kernels, attention(): pl.pallas_call(attn_kernel, grid=(nq // block,), in_specs=[full(2, TXTK),...  20.9 us
    ppermute x12, waiting for transfers between devices, swap(): return lax.ppermute(a, axis, [(0, 1), (1, 0)])  16 us
    all_gather x1, blocking collectives, local(): w_z = lax.all_gather(w_out, 'fsdp', axis=0, tiled=True)  14.5 us
    unnamed x103, local copies, waits for them, and re-layouts  12.4 us
    ppermute x4, starting transfers between devices, x_swap(): return lax.ppermute(a, ('cfg', 'xlo'), [(i, 3 - i) for i in range(4)])  9.06 us
  transfers between devices with their start and end apart: 31, of which 16 were waited for; matrix products, arithmetic and copies ran while one was open for 11% of the time, Pallas kernels for 3%

profile of v1, /device:TPU:0, one launch (start us, length us, event | category | flops | bytes accessed | tf_op | source)
XLA Modules:
  0.0 212.6 jit_solution(5299827210352758547)
XLA Ops:
  0.7 14.5 %all_gather.3.refs_0_ = bf16[96,3072]{1,0:T(8,128)(2,1)S(1)} all-gather(bf16[24,3072]{1,0:T(8,128)(2,1)} %param.19), channel_id=1, replica_groups=mesh['cfg'=2,'xlo'=2,'y'=4,'core'=2,'fsdp'=4] {'fsdp'}, dimensions={0}, use_global_device_ids=true | all-gather | bytes 737280 | tf_op jit(solution)/shard_map/all_gather | solution.py:230
  16.8 2.9 %collective-permute-start.7 = (bf16[96,3072]{1,0:T(8,128)(2,1)S(1)}, bf16[96,3072]{1,0:T(8,128)(2,1)}, u32[]{:S(2)}, u32[]{:S(2)}) collective-permute-start(bf16[96,3072]{1,0:T(8,128)(2,1)S(1)} %all_gather.3.refs_0_), channel_id=1, source_target_pairs={{0,16},{8,24},{16,0},{24,8},{1,17},{9,25},{17,1},{25,9},{2,18},{10... | collective-permute-start | bytes 1769480 | tf_op jit(solution)/shard_map/ppermute | solution.py:138
  26.1 2.8 %collective-permute-start.1 = (bf16[448,384]{1,0:T(8,128)(2,1)}, bf16[448,384]{1,0:T(8,128)(2,1)S(1)}, u32[]{:S(2)}, u32[]{:S(2)}) collective-permute-start(bf16[448,384]{1,0:T(8,128)(2,1)} %constant_dynamic-update-slice_fusion.7), channel_id=1, source_target_pairs={{0,96},{32,64},{64,32},{96,0},{1,97},{33,65},{65,33},{97,1},{2,98}... | collective-permute-start | bytes 1032200 | tf_op jit(solution)/shard_map/ppermute | solution.py:134
  37.8 2.3 %collective-permute-done.2 = bf16[64,384]{1,0:T(8,128)(2,1)} collective-permute-done((bf16[64,384]{1,0:T(8,128)(2,1)}, bf16[64,384]{1,0:T(8,128)(2,1)}, u32[]{:S(2)}, u32[]{:S(2)}) %collective-permute-start.2) | collective-permute-done | bytes 49184 | tf_op jit(solution)/shard_map/ppermute | solution.py:126
  44.1 2.1 collective-permute-start.4
  48.4 14.0 %collective-permute-done.5 = bf16[1664,128]{1,0:T(8,128)(2,1)S(1)} collective-permute-done((bf16[1664,128]{1,0:T(8,128)(2,1)S(1)}, bf16[1664,128]{1,0:T(8,128)(2,1)S(1)}, u32[]{:S(2)}, u32[]{:S(2)}) %collective-permute-start.5) | collective-permute-done | bytes 426016 | tf_op jit(solution)/shard_map/ppermute | solution.py:138
  63.9 2.1 collective-permute-start.14
  68.7 9.7 %collective-permute-done.8.refs_3_ = bf16[96,3072]{1,0:T(8,128)(2,1)} collective-permute-done((bf16[96,3072]{1,0:T(8,128)(2,1)S(1)}, bf16[96,3072]{1,0:T(8,128)(2,1)}, u32[]{:S(2)}, u32[]{:S(2)}) %collective-permute-start.8) | collective-permute-done | bytes 589856 | tf_op jit(solution)/shard_map/ppermute | solution.py:138
  78.4 3.1 %collective-permute-done.13.refs_9_ = bf16[128,3072]{1,0:T(8,128)(2,1)S(1)} collective-permute-done((bf16[128,3072]{1,0:T(8,128)(2,1)S(1)}, bf16[128,3072]{1,0:T(8,128)(2,1)S(1)}, u32[]{:S(2)}, u32[]{:S(2)}) %collective-permute-start.13) | collective-permute-done | bytes 786464 | tf_op jit(solution)/shard_map/ppermute | solution.py:126
  81.5 2.7 %collective-permute-done.14.refs_12_ = bf16[128,3072]{1,0:T(8,128)(2,1)S(1)} collective-permute-done((bf16[128,3072]{1,0:T(8,128)(2,1)S(1)}, bf16[128,3072]{1,0:T(8,128)(2,1)S(1)}, u32[]{:S(2)}, u32[]{:S(2)}) %collective-permute-start.14) | collective-permute-done | bytes 786464 | tf_op jit(solution)/shard_map/ppermute | solution.py:134
  87.9 2.1 collective-permute-start.16
  92.0 7.0 %collective-permute-done.15.refs_10_ = bf16[64,3072]{1,0:T(8,128)(2,1)} collective-permute-done((bf16[64,3072]{1,0:T(8,128)(2,1)}, bf16[64,3072]{1,0:T(8,128)(2,1)}, u32[]{:S(2)}, u32[]{:S(2)}) %collective-permute-start.15) | collective-permute-done | bytes 393248 | tf_op jit(solution)/shard_map/ppermute | solution.py:126
  99.0 2.0 collective-permute-done.16.refs_11_
  101.0 5.5 %shard_map.137 = bf16[512,768]{1,0:T(8,128)(2,1)S(1)} custom-call(s32[2]{0:T(128)S(1)} %pad_add_fusion.place_ref, bf16[96,3072]{1,0:T(8,128)(2,1)S(1)} %all_gather.3.refs_0_, bf16[96,3072]{1,0:T(8,128)(2,1)S(1)} %collective-permute-done.6.refs_1_, bf16[96,3072]{1,0:T(8,128)(2,1)} %collective-permute-done.7.refs_2_, ...), custom_call_target="tpu_custom_call" | custom-call | flops 2415919104 | bytes 8650752 | tf_op jit(solution)/shard_map/pallas_call | solution.py:190
  106.8 2.9 %collective-permute-start.23 = (bf16[2,128,128]{2,1,0:T(8,128)(2,1)S(1)}, bf16[2,128,128]{2,1,0:T(8,128)(2,1)S(1)}, u32[]{:S(2)}, u32[]{:S(2)}) collective-permute-start(bf16[2,128,128]{2,1,0:T(8,128)(2,1)S(1)} %bitcast.381), channel_id=1, source_target_pairs={{0,24},{8,16},{16,8},{24,0},{1,25},{9,17},{17,9},{25,1},{2,26},{10... | collective-permute-start | bytes 196616 | tf_op jit(solution)/shard_map/ppermute | solution.py:138
  111.0 2.9 %collective-permute-start.19 = (bf16[2,256,128]{2,1,0:T(8,128)(2,1)S(1)}, bf16[2,256,128]{2,1,0:T(8,128)(2,1)S(1)}, u32[]{:S(2)}, u32[]{:S(2)}) collective-permute-start(bf16[2,256,128]{2,1,0:T(8,128)(2,1)S(1)} %bitcast.357), channel_id=1, source_target_pairs={{0,24},{8,16},{16,8},{24,0},{1,25},{9,17},{17,9},{25,1},{2,26},{10... | collective-permute-start | bytes 393224 | tf_op jit(solution)/shard_map/ppermute | solution.py:138
  118.9 2.1 collective-permute-done.18
  124.5 7.0 %shard_map.139 = (bf16[512,128]{1,0:T(8,128)(2,1)S(1)}, bf16[2560,128]{1,0:T(8,128)(2,1)S(1)}, bf16[2560,128]{1,0:T(8,128)(2,1)S(1)}) custom-call(f32[2,256]{1,0:T(2,128)S(1)} %compare_select_fusion.bias_ref, bf16[512,128]{1,0:T(8,128)(2,1)S(1)} %bitcast.259, bf16[4,2,128,128]{3,2,1,0:T(8,128)(2,1)S(1)} %pad_maximum_fusion.18.do_ref, ...), custom_call_target="tpu_custom_call" | custom-call | flops 2013265920 | bytes 2621440 | tf_op jit(solution)/shard_map/pallas_call | solution.py:95
  131.7 13.9 %shard_map.138 = (bf16[1024,128]{1,0:T(8,128)(2,1)S(1)}, bf16[2560,128]{1,0:T(8,128)(2,1)S(1)}, bf16[2560,128]{1,0:T(8,128)(2,1)S(1)}) custom-call(f32[2,256]{1,0:T(2,128)S(1)} %compare_select_fusion.bias_ref, bf16[1024,128]{1,0:T(8,128)(2,1)S(1)} %bitcast.258, bf16[4,2,256,128]{3,2,1,0:T(8,128)(2,1)S(1)} %pad_maximum_fusion.7.do_ref, ...), custom_call_target="tpu_custom_call" | custom-call | flops 4026531840 | bytes 2621440 | tf_op jit(solution)/shard_map/pallas_call | solution.py:95
  146.2 2.8 %collective-permute-done.24 = bf16[4,4,320,128]{3,2,1,0:T(8,128)(2,1)S(1)} collective-permute-done((bf16[4,4,320,128]{3,2,1,0:T(8,128)(2,1)S(1)}, bf16[4,4,320,128]{3,2,1,0:T(8,128)(2,1)S(1)}, u32[]{:S(2)}, u32[]{:S(2)}) %collective-permute-start.24) | collective-permute-done | bytes 1310752 | tf_op jit(solution)/shard_map/ppermute | solution.py:126
  151.8 2.2 %collective-permute-start.25 = (bf16[1664,128]{1,0:T(8,128)(2,1)S(1)}, bf16[1664,128]{1,0:T(8,128)(2,1)S(1)}, u32[]{:S(2)}, u32[]{:S(2)}) collective-permute-start(bf16[1664,128]{1,0:T(8,128)(2,1)S(1)} %pad_maximum_fusion.8), channel_id=1, source_target_pairs={{0,8},{8,0},{16,24},{24,16},{1,9},{9,1},{17,25},{25,17},{2,10},{10... | collective-permute-start | bytes 1277960 | tf_op jit(solution)/shard_map/ppermute | solution.py:138
  154.1 17.8 %collective-permute-done.27 = bf16[1664,128]{1,0:T(8,128)(2,1)S(1)} collective-permute-done((bf16[1664,128]{1,0:T(8,128)(2,1)S(1)}, bf16[1664,128]{1,0:T(8,128)(2,1)S(1)}, u32[]{:S(2)}, u32[]{:S(2)}) %collective-permute-start.27) | collective-permute-done | bytes 426016 | tf_op jit(solution)/shard_map/ppermute | solution.py:138
  176.6 2.1 collective-permute-start.30
  180.7 26.1 %collective-permute-done.30 = bf16[416,768]{1,0:T(8,128)(2,1)S(1)} collective-permute-done((bf16[416,768]{1,0:T(8,128)(2,1)S(1)}, bf16[416,768]{1,0:T(8,128)(2,1)S(1)}, u32[]{:S(2)}, u32[]{:S(2)}) %collective-permute-start.30) | collective-permute-done | bytes 639008 | tf_op jit(solution)/shard_map/ppermute | solution.py:134
  (259 shorter events, 57.4 us)
Async XLA Ops:
  15.2 51.1 %collective-permute-start.6 = (bf16[96,3072]{1,0:T(8,128)(2,1)S(1)}, bf16[96,3072]{1,0:T(8,128)(2,1)S(1)}, u32[]{:S(2)}, u32[]{:S(2)}) collective-permute-start(bf16[96,3072]{1,0:T(8,128)(2,1)S(1)} %all_gather.3.refs_0_), channel_id=1, source_target_pairs={{0,8},{8,0},{16,24},{24,16},{1,9},{9,1},{17,25},{25,17},{2,10},{10... | collective-permute-start | bytes 1769480 | tf_op jit(solution)/shard_map/ppermute | solution.py:138
  16.8 49.6 %collective-permute-start.7 = (bf16[96,3072]{1,0:T(8,128)(2,1)S(1)}, bf16[96,3072]{1,0:T(8,128)(2,1)}, u32[]{:S(2)}, u32[]{:S(2)}) collective-permute-start(bf16[96,3072]{1,0:T(8,128)(2,1)S(1)} %all_gather.3.refs_0_), channel_id=1, source_target_pairs={{0,16},{8,24},{16,0},{24,8},{1,17},{9,25},{17,1},{25,9},{2,18},{10... | collective-permute-start | bytes 1769480 | tf_op jit(solution)/shard_map/ppermute | solution.py:138
  26.1 14.8 %collective-permute-start.1 = (bf16[448,384]{1,0:T(8,128)(2,1)}, bf16[448,384]{1,0:T(8,128)(2,1)S(1)}, u32[]{:S(2)}, u32[]{:S(2)}) collective-permute-start(bf16[448,384]{1,0:T(8,128)(2,1)} %constant_dynamic-update-slice_fusion.7), channel_id=1, source_target_pairs={{0,96},{32,64},{64,32},{96,0},{1,97},{33,65},{65,33},{97,1},{2,98}... | collective-permute-start | bytes 1032200 | tf_op jit(solution)/shard_map/ppermute | solution.py:134
  31.3 9.7 %collective-permute-start = (bf16[448,384]{1,0:T(8,128)(2,1)}, bf16[448,384]{1,0:T(8,128)(2,1)}, u32[]{:S(2)}, u32[]{:S(2)}) collective-permute-start(bf16[448,384]{1,0:T(8,128)(2,1)} %constant_dynamic-update-slice_fusion), channel_id=1, source_target_pairs={{0,32},{32,0},{1,33},{33,1},{2,34},{34,2},{3,35},{35,3},{4,36},{36... | collective-permute-start | bytes 1032200 | tf_op jit(solution)/shard_map/ppermute | solution.py:126
  32.1 8.0 %collective-permute-start.2 = (bf16[64,384]{1,0:T(8,128)(2,1)}, bf16[64,384]{1,0:T(8,128)(2,1)}, u32[]{:S(2)}, u32[]{:S(2)}) collective-permute-start(bf16[64,384]{1,0:T(8,128)(2,1)} %pad_maximum_fusion.27), channel_id=1, source_target_pairs={{0,64},{64,0},{1,65},{65,1},{2,66},{66,2},{3,67},{67,3},{4,68},{68... | collective-permute-start | bytes 147464 | tf_op jit(solution)/shard_map/ppermute | solution.py:126
  43.7 18.8 %collective-permute-start.5 = (bf16[1664,128]{1,0:T(8,128)(2,1)S(1)}, bf16[1664,128]{1,0:T(8,128)(2,1)S(1)}, u32[]{:S(2)}, u32[]{:S(2)}) collective-permute-start(bf16[1664,128]{1,0:T(8,128)(2,1)S(1)} %constant_dynamic-update-slice_fusion.44), channel_id=1, source_target_pairs={{0,24},{8,16},{16,8},{24,0},{1,25},{9,17},{17,9},{25,1},{2,26},{10... | collective-permute-start | bytes 1277960 | tf_op jit(solution)/shard_map/ppermute | solution.py:138
  44.1 18.7 %collective-permute-start.4 = (bf16[1664,128]{1,0:T(8,128)(2,1)S(1)}, bf16[1664,128]{1,0:T(8,128)(2,1)S(1)}, u32[]{:S(2)}, u32[]{:S(2)}) collective-permute-start(bf16[1664,128]{1,0:T(8,128)(2,1)S(1)} %constant_dynamic-update-slice_fusion.34), channel_id=1, source_target_pairs={{0,16},{8,24},{16,0},{24,8},{1,17},{9,25},{17,1},{25,9},{2,18},{10... | collective-permute-start | bytes 1277960 | tf_op jit(solution)/shard_map/ppermute | solution.py:138
  46.3 17.6 %collective-permute-start.3 = (bf16[1664,128]{1,0:T(8,128)(2,1)S(1)}, bf16[1664,128]{1,0:T(8,128)(2,1)S(1)}, u32[]{:S(2)}, u32[]{:S(2)}) collective-permute-start(bf16[1664,128]{1,0:T(8,128)(2,1)S(1)} %constant_dynamic-update-slice_fusion.24), channel_id=1, source_target_pairs={{0,8},{8,0},{16,24},{24,16},{1,9},{9,1},{17,25},{25,17},{2,10},{10... | collective-permute-start | bytes 1277960 | tf_op jit(solution)/shard_map/ppermute | solution.py:138
  62.5 16.0 %collective-permute-start.8 = (bf16[96,3072]{1,0:T(8,128)(2,1)S(1)}, bf16[96,3072]{1,0:T(8,128)(2,1)}, u32[]{:S(2)}, u32[]{:S(2)}) collective-permute-start(bf16[96,3072]{1,0:T(8,128)(2,1)S(1)} %all_gather.3.refs_0_), channel_id=1, source_target_pairs={{0,24},{8,16},{16,8},{24,0},{1,25},{9,17},{17,9},{25,1},{2,26},{10... | collective-permute-start | bytes 1769480 | tf_op jit(solution)/shard_map/ppermute | solution.py:138
  62.8 18.8 %collective-permute-start.13 = (bf16[128,3072]{1,0:T(8,128)(2,1)S(1)}, bf16[128,3072]{1,0:T(8,128)(2,1)S(1)}, u32[]{:S(2)}, u32[]{:S(2)}) collective-permute-start(bf16[128,3072]{1,0:T(8,128)(2,1)S(1)} %fusion.8.refs_8_), channel_id=1, source_target_pairs={{0,32},{32,0},{1,33},{33,1},{2,34},{34,2},{3,35},{35,3},{4,36},{36... | collective-permute-start | bytes 2359304 | tf_op jit(solution)/shard_map/ppermute | solution.py:126
  63.9 20.3 %collective-permute-start.14 = (bf16[128,3072]{1,0:T(8,128)(2,1)S(1)}, bf16[128,3072]{1,0:T(8,128)(2,1)S(1)}, u32[]{:S(2)}, u32[]{:S(2)}) collective-permute-start(bf16[128,3072]{1,0:T(8,128)(2,1)S(1)} %fusion.8.refs_8_), channel_id=1, source_target_pairs={{0,96},{32,64},{64,32},{96,0},{1,97},{33,65},{65,33},{97,1},{2,98}... | collective-permute-start | bytes 2359304 | tf_op jit(solution)/shard_map/ppermute | solution.py:134
  66.3 20.0 %collective-permute-start.9 = (bf16[96,3072]{1,0:T(8,128)(2,1)S(1)}, bf16[96,3072]{1,0:T(8,128)(2,1)S(1)}, u32[]{:S(2)}, u32[]{:S(2)}) collective-permute-start(bf16[96,3072]{1,0:T(8,128)(2,1)S(1)} %all_gather.3.refs_0_), channel_id=1, source_target_pairs={{0,4},{4,0},{1,5},{5,1},{2,6},{6,2},{3,7},{7,3},{8,12},{12,8},{9,1... | collective-permute-start | bytes 1769480 | tf_op jit(solution)/shard_map/ppermute | solution.py:126
  66.4 20.7 %collective-permute-start.10 = (bf16[96,3072]{1,0:T(8,128)(2,1)S(1)}, bf16[96,3072]{1,0:T(8,128)(2,1)S(1)}, u32[]{:S(2)}, u32[]{:S(2)}) collective-permute-start(bf16[96,3072]{1,0:T(8,128)(2,1)S(1)} %collective-permute-done.6.refs_1_), channel_id=1, source_target_pairs={{0,4},{4,0},{1,5},{5,1},{2,6},{6,2},{3,7},{7,3},{8,12},{12,8},{9,1... | collective-permute-start | bytes 1769480 | tf_op jit(solution)/shard_map/ppermute | solution.py:126
  78.4 13.6 %collective-permute-start.11 = (bf16[96,3072]{1,0:T(8,128)(2,1)}, bf16[96,3072]{1,0:T(8,128)(2,1)}, u32[]{:S(2)}, u32[]{:S(2)}) collective-permute-start(bf16[96,3072]{1,0:T(8,128)(2,1)} %collective-permute-done.7.refs_2_), channel_id=1, source_target_pairs={{0,4},{4,0},{1,5},{5,1},{2,6},{6,2},{3,7},{7,3},{8,12},{12,8},{9,1... | collective-permute-start | bytes 1769480 | tf_op jit(solution)/shard_map/ppermute | solution.py:126
  81.5 10.5 %collective-permute-start.12 = (bf16[96,3072]{1,0:T(8,128)(2,1)}, bf16[96,3072]{1,0:T(8,128)(2,1)}, u32[]{:S(2)}, u32[]{:S(2)}) collective-permute-start(bf16[96,3072]{1,0:T(8,128)(2,1)} %collective-permute-done.8.refs_3_), channel_id=1, source_target_pairs={{0,4},{4,0},{1,5},{5,1},{2,6},{6,2},{3,7},{7,3},{8,12},{12,8},{9,1... | collective-permute-start | bytes 1769480 | tf_op jit(solution)/shard_map/ppermute | solution.py:126
  84.2 37.8 %collective-permute-start.20 = (bf16[4,1280,128]{2,1,0:T(8,128)(2,1)}, bf16[4,1280,128]{2,1,0:T(8,128)(2,1)}, u32[]{:S(2)}, u32[]{:S(2)}) collective-permute-start(bf16[4,1280,128]{2,1,0:T(8,128)(2,1)} %get-tuple-element.38), channel_id=1, source_target_pairs={{0,4},{4,0},{1,5},{5,1},{2,6},{6,2},{3,7},{7,3},{8,12},{12,8},{9,1... | collective-permute-start | bytes 3932168 | tf_op jit(solution)/shard_map/ppermute | solution.py:126
  87.1 11.8 %collective-permute-start.15 = (bf16[64,3072]{1,0:T(8,128)(2,1)}, bf16[64,3072]{1,0:T(8,128)(2,1)}, u32[]{:S(2)}, u32[]{:S(2)}) collective-permute-start(bf16[64,3072]{1,0:T(8,128)(2,1)} %slice.455), channel_id=1, source_target_pairs={{0,32},{32,0},{1,33},{33,1},{2,34},{34,2},{3,35},{35,3},{4,36},{36... | collective-permute-start | bytes 1179656 | tf_op jit(solution)/shard_map/ppermute | solution.py:126
  87.9 13.1 %collective-permute-start.16 = (bf16[64,3072]{1,0:T(8,128)(2,1)}, bf16[64,3072]{1,0:T(8,128)(2,1)}, u32[]{:S(2)}, u32[]{:S(2)}) collective-permute-start(bf16[64,3072]{1,0:T(8,128)(2,1)} %slice.456), channel_id=1, source_target_pairs={{0,96},{32,64},{64,32},{96,0},{1,97},{33,65},{65,33},{97,1},{2,98}... | collective-permute-start | bytes 1179656 | tf_op jit(solution)/shard_map/ppermute | solution.py:134
  149.6 22.3 %collective-permute-start.27 = (bf16[1664,128]{1,0:T(8,128)(2,1)S(1)}, bf16[1664,128]{1,0:T(8,128)(2,1)S(1)}, u32[]{:S(2)}, u32[]{:S(2)}) collective-permute-start(bf16[1664,128]{1,0:T(8,128)(2,1)S(1)} %pad_maximum_fusion.10), channel_id=1, source_target_pairs={{0,24},{8,16},{16,8},{24,0},{1,25},{9,17},{17,9},{25,1},{2,26},{10... | collective-permute-start | bytes 1277960 | tf_op jit(solution)/shard_map/ppermute | solution.py:138
  151.0 20.9 %collective-permute-start.26 = (bf16[1664,128]{1,0:T(8,128)(2,1)S(1)}, bf16[1664,128]{1,0:T(8,128)(2,1)S(1)}, u32[]{:S(2)}, u32[]{:S(2)}) collective-permute-start(bf16[1664,128]{1,0:T(8,128)(2,1)S(1)} %pad_maximum_fusion.9), channel_id=1, source_target_pairs={{0,16},{8,24},{16,0},{24,8},{1,17},{9,25},{17,1},{25,9},{2,18},{10... | collective-permute-start | bytes 1277960 | tf_op jit(solution)/shard_map/ppermute | solution.py:138
  151.8 20.8 %collective-permute-start.25 = (bf16[1664,128]{1,0:T(8,128)(2,1)S(1)}, bf16[1664,128]{1,0:T(8,128)(2,1)S(1)}, u32[]{:S(2)}, u32[]{:S(2)}) collective-permute-start(bf16[1664,128]{1,0:T(8,128)(2,1)S(1)} %pad_maximum_fusion.8), channel_id=1, source_target_pairs={{0,8},{8,0},{16,24},{24,16},{1,9},{9,1},{17,25},{25,17},{2,10},{10... | collective-permute-start | bytes 1277960 | tf_op jit(solution)/shard_map/ppermute | solution.py:138
  176.6 30.2 %collective-permute-start.30 = (bf16[416,768]{1,0:T(8,128)(2,1)S(1)}, bf16[416,768]{1,0:T(8,128)(2,1)S(1)}, u32[]{:S(2)}, u32[]{:S(2)}) collective-permute-start(bf16[416,768]{1,0:T(8,128)(2,1)S(1)} %get-tuple-element.71), channel_id=1, source_target_pairs={{0,96},{32,64},{64,32},{96,0},{1,97},{33,65},{65,33},{97,1},{2,98}... | collective-permute-start | bytes 1916936 | tf_op jit(solution)/shard_map/ppermute | solution.py:134
  178.7 28.1 %collective-permute-start.29 = (bf16[416,768]{1,0:T(8,128)(2,1)}, bf16[416,768]{1,0:T(8,128)(2,1)S(1)}, u32[]{:S(2)}, u32[]{:S(2)}) collective-permute-start(bf16[416,768]{1,0:T(8,128)(2,1)} %get-tuple-element.72), channel_id=1, source_target_pairs={{0,64},{64,0},{1,65},{65,1},{2,66},{66,2},{3,67},{67,3},{4,68},{68... | collective-permute-start | bytes 1916936 | tf_op jit(solution)/shard_map/ppermute | solution.py:126
  178.7 29.0 %collective-permute-start.28 = (bf16[416,768]{1,0:T(8,128)(2,1)}, bf16[416,768]{1,0:T(8,128)(2,1)S(1)}, u32[]{:S(2)}, u32[]{:S(2)}) collective-permute-start(bf16[416,768]{1,0:T(8,128)(2,1)} %get-tuple-element.73), channel_id=1, source_target_pairs={{0,32},{32,0},{1,33},{33,1},{2,34},{34,2},{3,35},{35,3},{4,36},{36... | collective-permute-start | bytes 1916936 | tf_op jit(solution)/shard_map/ppermute | solution.py:126
  (25 other events, 246.3 us)

commit v2 on v1

v2 whole, which is shorter than its diff:
```python
import math

import jax
import jax.numpy as jnp
from jax import lax
from jax.experimental import pallas as pl
from jax.experimental.pallas import tpu as pltpu
from jax.sharding import PartitionSpec as P

HD = 128
TOK = 128
TT = 16
XH = 6
XW = XH * HD
WROWS = 96
SCALE = 1.0 / math.sqrt(HD)
EXP2 = SCALE * math.log2(math.e)
VIDK = 2048
TXTK = 256
BLOCK = 256

NT = ((1,), (1,))
NN = ((1,), (0,))
TN = ((0,), (0,))

K_A, V_A, K_B, V_B = 0, 2 * TOK, 4 * TOK, 6 * TOK
TK_A, TV_A, TK_B, TV_B = (8 * TOK + i * 4 * TT for i in range(4))
Q_A = 8 * TOK + 16 * TT
Q_B = Q_A + 2 * TOK
MSG = Q_B + TOK
OWN = 3 * TOK + 2 * TT
NEAR = 3 * TOK // 2 + 2 * TT
BACK_KV = 4 * TOK + 8 * TT


def dot(a, b, dims):
    return lax.dot_general(a, b, (dims, ((), ())), preferred_element_type=jnp.float32)


def vmem_specs(count):
    return [pl.BlockSpec(memory_space=pltpu.VMEM)] * count


SMEM = pl.BlockSpec(memory_space=pltpu.SMEM)
MIB = 1024 * 1024


def params(mib):
    return pltpu.CompilerParams(vmem_limit_bytes=mib * MIB)


COST = pl.CostEstimate(flops=0, bytes_accessed=0, transcendentals=0)


def whole(a):
    shape = a.shape
    return pl.BlockSpec(shape, lambda *_: (0,) * len(shape))


def lanes(start, count):
    return pl.ds(pl.multiple_of(start, HD), count)


def run_copies(copies, sems):
    started = [pltpu.make_async_copy(src, dst, sems.at[i]) for i, (src, dst) in enumerate(copies)]
    for copy in started:
        copy.start()
    for copy in started:
        copy.wait()


def swap(a, axis):
    return lax.ppermute(a, axis, [(0, 1), (1, 0)])


def x_swap(a, r):
    if r == 1:
        return swap(a, "xlo")
    if r == 2:
        return swap(a, "cfg")
    return lax.ppermute(a, ("cfg", "xlo"), [(i, 3 - i) for i in range(4)])


def ring_swap(a, axis, r):
    return lax.ppermute(a, axis, [(i, i ^ r) for i in range(4)])


def bf16(*shape):
    return jax.ShapeDtypeStruct(shape, jnp.bfloat16)


def cut_x_kernel(at_ref, *refs):
    del at_ref
    blocks, outs = refs[:17], refs[17:]
    for out, first, count in zip(outs, (0, 5, 10, 15), (5, 5, 5, 2)):
        row = 0
        for block in blocks[first : first + count]:
            out[row : row + block.shape[0]] = block[...]
            row += block.shape[0]


def cut_x(at, q, k, v, kt, vt):
    half = TOK // 2

    def block(rows, r, index):
        return pl.BlockSpec((rows, XW), lambda i, at_ref: (index, at_ref[0] ^ r))

    def same(a):
        return pl.BlockSpec(a.shape, lambda i, at_ref: (0, 0))

    specs, arrays = [], []
    for rows, r, index in ((TOK, 0, 0), (half, 1, 0), (half, 3, 1)):
        specs += [block(rows, r, index)] * 3 + [block(TT, r, 0)] * 2
        arrays += [q, k, v, kt, vt]
    specs += [block(TT, 2, 0)] * 2
    arrays += [kt, vt]
    shapes = [bf16(OWN, XW), bf16(NEAR, XW), bf16(NEAR, XW), bf16(2 * TT, XW)]
    return pl.pallas_call(
        cut_x_kernel,
        grid_spec=pltpu.PrefetchScalarGridSpec(
            num_scalar_prefetch=1,
            grid=(1,),
            in_specs=specs,
            out_specs=[same(a) for a in shapes],
        ),
        out_shape=shapes,
        compiler_params=params(60),
        cost_estimate=COST,
    )(at, *arrays)


def cut_y_kernel(at_ref, own, got1, got2, got3, *outs):
    y = at_ref[1]
    half = TOK // 2
    quarter = TOK // 4
    for r, out in enumerate(outs):
        yd = y ^ r
        head_a = lanes(yd * HD, HD)
        head_b = lanes((4 + yd // 2) * HD, HD)
        for row, tensor, head in (
            (K_A, 1, head_a),
            (V_A, 2, head_a),
            (K_B, 1, head_b),
            (V_B, 2, head_b),
            (Q_A, 0, head_a),
        ):
            out[row : row + TOK] = own[tensor * TOK : (tensor + 1) * TOK, head]
            rows = slice(tensor * half, (tensor + 1) * half)
            out[row + TOK : row + TOK + half] = got1[rows, head]
            out[row + TOK + half : row + 2 * TOK] = got3[rows, head]
        for row, tensor, head in (
            (TK_A, 0, head_a),
            (TV_A, 1, head_a),
            (TK_B, 0, head_b),
            (TV_B, 1, head_b),
        ):
            for s, (src, first) in enumerate(
                ((own, 3 * TOK), (got1, 3 * half), (got2, 0), (got3, 3 * half))
            ):
                start = first + tensor * TT
                out[row + s * TT : row + (s + 1) * TT] = src[start : start + TT, head]
        skip = (yd % 2) * quarter
        for i, (src, first) in enumerate(((own, 0), (own, half), (got1, 0), (got3, 0))):
            rows = pl.ds(pl.multiple_of(first + skip, quarter), quarter)
            out[Q_B + i * quarter : Q_B + (i + 1) * quarter] = src[rows, head_b]


def cut_y(at, own, got1, got2, got3):
    arrays = (own, got1, got2, got3)
    shapes = [bf16(MSG, HD)] * 4
    return pl.pallas_call(
        cut_y_kernel,
        in_specs=[SMEM] + [whole(a) for a in arrays],
        out_specs=[whole(a) for a in shapes],
        out_shape=shapes,
        compiler_params=params(8),
        cost_estimate=COST,
    )(at, *arrays)


def project_kernel(at_ref, *refs):
    y, c = at_ref[1], at_ref[2]
    w_refs, a_refs, outs = refs[:8], refs[8:13], refs[13:17]
    w_all, a_all, out = refs[17:]
    for i, ref in enumerate(w_refs):
        row = pl.multiple_of(((y ^ (i % 4)) * 2 + (c ^ (i // 4))) * WROWS, WROWS)
        w_all[pl.ds(row, WROWS)] = ref[...]
    row = 0
    for ref in a_refs:
        a_all[row : row + ref.shape[0]] = ref[...]
        row += ref.shape[0]
    out[...] = dot(a_all[...], w_all[...], NT).astype(jnp.bfloat16)
    quarter = TOK // 4
    for r in range(4):
        yd = y ^ r
        outs[r][: 4 * TOK] = out[:, lanes(yd * HD, HD)]
        head_b = lanes((4 + yd // 2) * HD, HD)
        skip = (yd % 2) * quarter
        for i in range(8):
            rows = pl.ds(pl.multiple_of(i * 2 * quarter + skip, quarter), quarter)
            outs[r][4 * TOK + i * quarter : 4 * TOK + (i + 1) * quarter] = out[rows, head_b]


def project(at, weights, adjoints):
    width = weights[0].shape[1]
    rows = 4 * TOK
    return pl.pallas_call(
        project_kernel,
        in_specs=[SMEM] + vmem_specs(13),
        out_specs=vmem_specs(4),
        out_shape=[bf16(rows + rows // 2, HD)] * 4,
        scratch_shapes=[
            pltpu.VMEM((XW, width), jnp.bfloat16),
            pltpu.VMEM((rows, width), jnp.bfloat16),
            pltpu.VMEM((rows, XW), jnp.bfloat16),
        ],
        compiler_params=params(16),
        cost_estimate=COST,
    )(at, *weights, *adjoints)


def forward_kernel(bias_ref, *refs):
    msgs = refs[:8]
    e_ref, p_ref, o_ref, w_ref, k_all, v_all, q_ref, q_all = refs[8:]
    step = pl.program_id(0)
    run = 2 * TT

    @pl.when(step == 0)
    def _():
        for head, (k_at, v_at, tk_at, tv_at) in enumerate(
            ((K_A, V_A, TK_A, TV_A), (K_B, V_B, TK_B, TV_B))
        ):
            for i, msg in enumerate(msgs):
                video = slice(i * 2 * TOK, (i + 1) * 2 * TOK)
                k_all[head, video] = msg[k_at : k_at + 2 * TOK]
                v_all[head, video] = msg[v_at : v_at + 2 * TOK]
                for p in range(2):
                    row = VIDK + p * TXTK + i * run
                    k_all[head, row : row + run] = msg[tk_at + p * run : tk_at + (p + 1) * run]
                    v_all[head, row : row + run] = msg[tv_at + p * run : tv_at + (p + 1) * run]
        for r in range(4):
            q_all[r * 2 * TOK : (r + 1) * 2 * TOK] = msgs[r][Q_A : Q_A + 2 * TOK]
            q_all[8 * TOK + r * TOK : 8 * TOK + (r + 1) * TOK] = msgs[r][Q_B : Q_B + TOK]

    head = step // 4
    q = q_all[pl.ds(pl.multiple_of(step * BLOCK, BLOCK), BLOCK)]
    q_ref[...] = q
    s = dot(q, k_all[head, :VIDK], NT)
    mv = jnp.max(s, axis=1, keepdims=True)
    e = jnp.exp2((s - mv) * EXP2)
    lv = jnp.sum(e, axis=1, keepdims=True)
    eb = e.astype(jnp.bfloat16)
    e_ref[...] = eb
    ov = dot(eb, v_all[head, :VIDK], NN)
    o_ref[2] = ov / lv
    for p in range(2):
        text = slice(VIDK + p * TXTK, VIDK + (p + 1) * TXTK)
        st = dot(q, k_all[head, text], NT) + bias_ref[p : p + 1, :]
        m = jnp.maximum(mv, jnp.max(st, axis=1, keepdims=True))
        a = jnp.exp2((mv - m) * EXP2)
        et = jnp.exp2((st - m) * EXP2)
        inv = 1.0 / (a * lv + jnp.sum(et, axis=1, keepdims=True))
        w = a * inv
        pt = (et * inv).astype(jnp.bfloat16)
        p_ref[p] = pt
        w_ref[p] = jnp.broadcast_to(w, w_ref.shape[1:])
        o_ref[p] = w * ov + dot(pt, v_all[head, text], NN)


def attention_forward(bias, own, other):
    keys = VIDK + 2 * TXTK
    rows = 12 * TOK
    arrays = (bias, *own, *other)
    heads = bf16(2, keys, HD)

    def stacked(count, width):
        return pl.BlockSpec((count, BLOCK, width), lambda i: (0, i, 0))

    return pl.pallas_call(
        forward_kernel,
        grid=(rows // BLOCK,),
        in_specs=[whole(a) for a in arrays],
        out_specs=[
            pl.BlockSpec((BLOCK, VIDK), lambda i: (i, 0)),
            stacked(2, TXTK),
            stacked(3, HD),
            stacked(2, HD),
            whole(heads),
            whole(heads),
            pl.BlockSpec((BLOCK, HD), lambda i: (i, 0)),
        ],
        out_shape=[
            bf16(rows, VIDK),
            bf16(2, rows, TXTK),
            jax.ShapeDtypeStruct((3, rows, HD), jnp.float32),
            jax.ShapeDtypeStruct((2, rows, HD), jnp.float32),
            heads,
            heads,
            bf16(rows, HD),
        ],
        scratch_shapes=[pltpu.VMEM((rows, HD), jnp.bfloat16)],
        compiler_params=params(24),
        cost_estimate=COST,
    )(*arrays)


def backward_kernel(shape, *refs):
    parts, first, final, count, do_at = shape
    e_ref, p_ref, o_ref, w_ref, q_ref, k_ref, v_ref = refs[:7]
    dos, refs = refs[7 : 7 + parts], refs[7 + parts :]
    if not first:
        dk_in, dv_in, refs = refs[0], refs[1], refs[2:]
    out0, out1, dqs = refs[0], refs[1], refs[2 : 2 + parts]
    ds_all, dk_acc, dv_acc = refs[2 + parts :]
    step = pl.program_id(0)
    last = pl.num_programs(0) - 1
    per_step = BLOCK // count
    run = 2 * TT

    @pl.when(step == 0)
    def _():
        dk_acc[...] = jnp.zeros_like(dk_acc) if first else dk_in[...]
        dv_acc[...] = jnp.zeros_like(dv_acc) if first else dv_in[...]

    def adjoint(p):
        rows = slice(do_at + p * count, do_at + (p + 1) * count)
        value = jnp.concatenate([ref[rows] for ref in dos[:per_step]], axis=0)
        for i in range(1, parts // per_step):
            group = dos[i * per_step : (i + 1) * per_step]
            other = jnp.concatenate([ref[rows] for ref in group], axis=0)
            value = jnp.where(step == i, other, value)
        return value

    q = q_ref[...]
    v_video = v_ref[:VIDK]
    g = jnp.zeros(q.shape, jnp.float32)
    delta = jnp.zeros((BLOCK, 1), jnp.float32)
    for p in range(2):
        text = slice(VIDK + p * TXTK, VIDK + (p + 1) * TXTK)
        do = adjoint(p)
        do32 = do.astype(jnp.float32)
        w = w_ref[p]
        row_delta = jnp.sum(do32 * o_ref[p], axis=1, keepdims=True)
        g = g + w * do32
        delta = delta + w[:, :1] * row_delta
        pt = p_ref[p]
        ds_text = pt.astype(jnp.float32) * (dot(do, v_ref[text], NT) - row_delta)
        ds_all[:, text] = ds_text.astype(jnp.bfloat16)
        dv_acc[text] += dot(pt, do, TN)
    gb = g.astype(jnp.bfloat16)
    delta = delta + jnp.sum((gb.astype(jnp.float32) - g) * o_ref[2], axis=1, keepdims=True)
    e = e_ref[...]
    ds_video = e.astype(jnp.float32) * (dot(gb, v_video, NT) - delta)
    ds_all[:, :VIDK] = ds_video.astype(jnp.bfloat16)
    dv_acc[:VIDK] += dot(e, gb, TN)
    ds = ds_all[...]
    dk_acc[...] += dot(ds, q, TN)
    dq = (dot(ds, k_ref[...], NN) * SCALE).astype(jnp.bfloat16)
    for r in range(parts):

        @pl.when(step == r // per_step)
        def _():
            start = (r % per_step) * count
            dqs[r][...] = dq[start : start + count]

    @pl.when(step == last)
    def _():
        if not final:
            out0[...] = dk_acc[...]
            out1[...] = dv_acc[...]
            return
        for i in range(8):
            out = (out0, out1)[i // 4].at[i % 4]
            for j, acc, factor in ((0, dk_acc, SCALE), (1, dv_acc, 1.0)):
                video = acc[i * 2 * TOK : (i + 1) * 2 * TOK] * factor
                out[j * 2 * TOK : (j + 1) * 2 * TOK] = video.astype(jnp.bfloat16)
                for p in range(2):
                    src = VIDK + p * TXTK + i * run
                    dst = 4 * TOK + j * 2 * run + p * run
                    out[dst : dst + run] = (acc[src : src + run] * factor).astype(jnp.bfloat16)


def attention_backward(stored, dos, shared, start=0, sums=None, final=True):
    e, p, o, w, k, v, q = stored
    parts = len(dos)
    count = TOK if shared else 2 * TOK
    do_at = 4 * TOK if shared else 0
    steps = parts * count // BLOCK
    head = 1 if shared else 0
    skip = (8 * TOK if shared else 0) // BLOCK + start * count // BLOCK
    keys = VIDK + 2 * TXTK
    shape = (parts, sums is None, final, count, do_at)

    def kernel(*refs):
        backward_kernel(shape, *refs)

    def stacked(depth, width):
        return pl.BlockSpec((depth, BLOCK, width), lambda i: (0, i + skip, 0))

    def rows_of(width):
        return pl.BlockSpec((BLOCK, width), lambda i: (i + skip, 0))

    keys_of = pl.BlockSpec((None, keys, HD), lambda i: (head, 0, 0))
    sum_shape = jax.ShapeDtypeStruct((keys, HD), jnp.float32)
    sums = [] if sums is None else list(sums)
    results = pl.pallas_call(
        kernel,
        grid=(steps,),
        in_specs=[rows_of(VIDK), stacked(2, TXTK), stacked(3, HD), stacked(2, HD), rows_of(HD)]
        + [keys_of, keys_of]
        + vmem_specs(parts + len(sums)),
        out_specs=vmem_specs(2 + parts),
        out_shape=([bf16(4, BACK_KV, HD)] * 2 if final else [sum_shape] * 2)
        + [bf16(count, HD)] * parts,
        scratch_shapes=[
            pltpu.VMEM((BLOCK, keys), jnp.bfloat16),
            pltpu.VMEM((keys, HD), jnp.float32),
            pltpu.VMEM((keys, HD), jnp.float32),
        ],
        compiler_params=params(18),
        cost_estimate=COST,
    )(e, p, o, w, q, k, v, *dos, *sums)
    return results[0], results[1], results[2:]


def add_cores_kernel(kept, came, *refs):
    dqs, outs = refs[:4], refs[4:]
    for r, out in enumerate(outs):
        total = kept[r].astype(jnp.float32) + came[r].astype(jnp.float32)
        out[:BACK_KV] = total.astype(jnp.bfloat16)
        out[BACK_KV:] = dqs[r][...]


def add_cores(kept, came, dqs):
    count = dqs[0].shape[0]
    return pl.pallas_call(
        add_cores_kernel,
        in_specs=vmem_specs(6),
        out_specs=vmem_specs(4),
        out_shape=[bf16(BACK_KV + count, HD)] * 4,
        compiler_params=params(8),
        cost_estimate=COST,
    )(kept, came, *dqs)


def merge_y_kernel(shared, at_ref, *refs):
    y = at_ref[1]
    got, outs = refs[:4], refs[4:]
    quarter = TOK // 4

    def put(out, row, head, value):
        out[row : row + value.shape[0], head] = value

    def part(r, rows):
        if not shared:
            return got[r][rows]
        total = got[r][rows].astype(jnp.float32) + got[r + 1][rows].astype(jnp.float32)
        return total.astype(jnp.bfloat16)

    for r in (0, 2) if shared else range(4):
        head = lanes(((y // 2) ^ (r // 2)) * HD, HD) if shared else lanes((y ^ r) * HD, HD)
        for j in range(2):
            for par in range(2):
                first = (2 * j + par) * TOK
                value = part(r, slice(first, first + TOK))
                for s in (par, par + 2):
                    if (s, par) in ((0, 0), (2, 0), (1, 1), (3, 1)):
                        put(outs[s], (1 + j) * TOK, head, value)
            for s in range(4):
                first = 4 * TOK + j * 4 * TT + s * TT
                value = part(r, slice(first, first + TT))
                put(outs[s], 3 * TOK + j * TT, head, value)
        for par in range(2):
            if not shared:
                value = got[r][BACK_KV + par * TOK : BACK_KV + (par + 1) * TOK]
                for s in (par, par + 2):
                    put(outs[s], 0, head, value)
                continue
            for rr in (r, r + 1):
                skip = ((y ^ rr) % 2) * quarter
                for i in range(2):
                    first = BACK_KV + par * 2 * quarter + i * quarter
                    value = got[rr][first : first + quarter]
                    rows = pl.ds(pl.multiple_of(i * 2 * quarter + skip, quarter), quarter)
                    for s in (par, par + 2):
                        outs[s][rows, head] = value


def merge_y(at, got, shared):
    width = (2 if shared else 4) * HD

    def kernel(*refs):
        merge_y_kernel(shared, *refs)

    return pl.pallas_call(
        kernel,
        in_specs=[SMEM] + vmem_specs(4),
        out_specs=vmem_specs(4),
        out_shape=[bf16(3 * TOK + 2 * TT, width)] * 4,
        compiler_params=params(8),
        cost_estimate=COST,
    )(at, *got)


def merge_x_kernel(at_ref, *refs):
    x = at_ref[0]
    parts_a, parts_b, outs = refs[:4], refs[4:8], refs[8:13]
    for r in range(4):
        for part, first in ((parts_a[r], 0), (parts_b[r], 4 * HD)):
            col = lanes((x ^ r) * XW + first, part.shape[1])
            row = 0
            for out in outs:
                count = out.shape[0]
                out[:, col] = part[row : row + count]
                row += count


def merge_x(at, parts_a, parts_b):
    shapes = [bf16(TOK, 4 * XW)] * 3 + [bf16(TT, 4 * XW)] * 2
    return pl.pallas_call(
        merge_x_kernel,
        in_specs=[SMEM] + vmem_specs(8),
        out_specs=[whole(a) for a in shapes],
        out_shape=shapes,
        compiler_params=params(16),
        cost_estimate=COST,
    )(at, *parts_a, *parts_b)


def local(q_video, k_video, v_video, k_text, v_text, text_len, guide_index, gate, adjoint, w_out):
    h = lax.axis_index("cfg")
    l = lax.axis_index("xlo")
    y = lax.axis_index("y")
    c = lax.axis_index("core")
    z = lax.axis_index("fsdp")
    x = 2 * h + l
    at = jnp.stack([x, y, c]).astype(jnp.int32)

    w_y = jnp.stack([w_out] + [ring_swap(w_out, "y", r) for r in (1, 2, 3)])
    w_z1, w_z3 = ring_swap(w_y, "fsdp", 1), ring_swap(w_y, "fsdp", 3)
    w_parts = [w_y, w_z1, ring_swap(w_z3[:2], "fsdp", 1), ring_swap(w_z1[2:], "fsdp", 3), w_z3]

    own, to1, to3, to2 = cut_x(at, q_video[0], k_video[0], v_video[0], k_text[0, 0], v_text[0, 0])
    got1, got2, got3 = x_swap(to1, 1), x_swap(to2, 2), x_swap(to3, 3)

    guidance = 1.5 + guide_index[0].astype(jnp.float32)
    pass_weight = jnp.where(h == 0, guidance, 1.0 - guidance)
    scaled = (gate[0][None, :] * pass_weight * adjoint[0, 0].astype(jnp.float32)).astype(
        jnp.bfloat16
    )
    scaled, got1, got3 = lax.optimization_barrier((scaled, got1, got3))
    scaled1, scaled3 = x_swap(scaled, 1), x_swap(scaled, 3)
    half = TOK // 2
    adjoints = [scaled, scaled1, x_swap(scaled3[:half], 1), x_swap(scaled1[half:], 3), scaled3]
    messages = cut_y(at, own, got1, got2, got3)
    arrived = [messages[0]] + [ring_swap(messages[r], "y", r) for r in (1, 2, 3)]
    w_z = jnp.concatenate(w_parts, axis=0).reshape(4, *w_y.shape)
    w_z = [lax.dynamic_index_in_dim(w_z, z ^ j, 0, False) for j in range(4)]
    w_own = [jnp.concatenate([part[r] for part in w_z], axis=0) for r in range(4)]
    other = [swap(message, "core") for message in arrived]
    weights = w_own + [swap(piece, "core") for piece in w_own]

    two = jnp.arange(2, dtype=jnp.int32)
    at_core = (c ^ two)[:, None, None, None]
    at_y = (y ^ jnp.arange(4, dtype=jnp.int32))[None, :, None, None]
    at_l = (l ^ two)[None, None, :, None]
    position = ((at_l * 4 + at_y) * 2 + at_core) * TT + jnp.arange(TT, dtype=jnp.int32)
    position = position.reshape(1, -1)
    lens = jnp.where(h == 0, text_len[:, 0], text_len[::-1, 0])
    bias = jnp.where(position < lens[:, None], 0.0, -jnp.inf).astype(jnp.float32)

    to_y = project(at, weights, adjoints)
    dos = [to_y[0]] + [ring_swap(to_y[r], "y", r) for r in (1, 2, 3)]
    other, to_y = lax.optimization_barrier((other, to_y))
    stored = attention_forward(bias, arrived, other)
    dos, stored = lax.optimization_barrier((dos, stored))

    def x_back(parts):
        return [parts[0]] + [x_swap(parts[r], r) for r in (1, 2, 3)]

    def y_back(totals):
        return [totals[0]] + [ring_swap(totals[r], "y", r) for r in (1, 2, 3)]

    dk_sum, dv_sum, dq_0 = attention_backward(stored, dos[:1], False, 0, final=False)
    kept_b, sent_b, dq_b = attention_backward(stored, dos, True)
    totals_b = add_cores(kept_b, swap(sent_b, "core"), dq_b)
    dk_sum, totals_b = lax.optimization_barrier((dk_sum, totals_b))
    got_b = y_back(totals_b)
    kept_a, sent_a, dq_123 = attention_backward(stored, dos[1:], False, 1, (dk_sum, dv_sum))
    sent_a, got_b[1], got_b[3] = lax.optimization_barrier((sent_a, got_b[1], got_b[3]))
    came_a = swap(sent_a, "core")
    came_a, got_b = lax.optimization_barrier((came_a, got_b))
    totals_a = add_cores(kept_a, came_a, dq_0 + dq_123)
    parts_b = x_back(merge_y(at, got_b, True))
    got_a = y_back(totals_a)
    got_a, parts_b = lax.optimization_barrier((got_a, parts_b))
    parts_a = x_back(merge_y(at, got_a, False))
    dq, dk, dv, dkt, dvt = merge_x(at, parts_a, parts_b)
    return dq[None], dk[None], dv[None], dkt[None, None], dvt[None, None]


def solution(mesh):
    devices = mesh.devices
    fine = jax.sharding.Mesh(
        devices.reshape(2, 2, 4, 2, devices.shape[-1]), ("cfg", "xlo", "y", "core", "fsdp")
    )
    seq = ("xlo", "y", "core")
    video = P("fsdp", seq, None)
    per_pass = P("cfg", "fsdp", seq, None)
    placed = (
        video,
        video,
        video,
        per_pass,
        per_pass,
        P(None, "fsdp"),
        P("fsdp"),
        P("fsdp", None),
        per_pass,
        P(("cfg",) + seq + ("fsdp",), None),
    )
    return jax.shard_map(
        local,
        mesh=fine,
        in_specs=placed,
        out_specs=(video, video, video, per_pass, per_pass),
        check_vma=False,
    )
```

time: 213 us -> 166 us (0.78)
  waiting for transfers between devices: 95.7 us -> 66.9 us
  blocking collectives: 14.5 us -> 0 us
  local copies, waits for them, and re-layouts: 23.7 us -> 9.95 us
  starting transfers between devices: 36.8 us -> 49.4 us
  other arithmetic: 13 us -> 1.97 us
  Pallas kernels: 26.3 us -> 35.8 us
    ppermute x15 -> x19, waiting for transfers between devices: 48.8 us -> 28.6 us  [ring_swap(): return lax.ppermute(a, axis, [(i, i ^ r) for i in range(4)])]
    ppermute x4 -> x5, waiting for transfers between devices: 30.8 us -> 15.1 us  [x_swap(): return lax.ppermute(a, ('cfg', 'xlo'), [(i, 3 - i) for i in range(4)])]
    all_gather x1 -> x0, blocking collectives: 14.5 us -> none  [local(): w_z = lax.all_gather(w_out, 'fsdp', axis=0, tiled=True)]
    pallas_call x3 -> x12, Pallas kernels: 26.3 us -> 35.8 us  [the longest x3 11.4 us: attention_backward(): pl.pallas_call(kernel, grid=(steps,), in_specs=[rows_of(VIDK), stacked(2,...]
    ppermute x12 -> x18, starting transfers between devices: 5.8 us -> 14 us  [swap(): return lax.ppermute(a, axis, [(0, 1), (1, 0)])]
    ppermute x15 -> x19, starting transfers between devices: 21.9 us -> 29.1 us  [ring_swap(): return lax.ppermute(a, axis, [(i, i ^ r) for i in range(4)])]
    ppermute x12 -> x18, waiting for transfers between devices: 16 us -> 23.2 us  [swap(): return lax.ppermute(a, axis, [(0, 1), (1, 0)])]
    slice x22 -> x4, local copies, waits for them, and re-layouts: 6.42 us -> 0.1 us  [the longest x1 0.03 us: local(): scaled3[:half]]
  transfers between devices with their start and end apart: 31 -> 42, of which waited for: 16 -> 15; matrix products, arithmetic and copies ran while one was open for 11% -> 4% of each run, Pallas kernels for 3% -> 17%
where the time goes in v2:
time: 166 us
  waiting for transfers between devices  66.9 us (40%)
  starting transfers between devices  49.4 us (30%)
  Pallas kernels  35.8 us (22%)
  local copies, waits for them, and re-layouts  9.95 us (6%)
  other arithmetic  1.97 us (1%)
  between operations  1.76 us (1%)
    ppermute x19, starting transfers between devices, ring_swap(): return lax.ppermute(a, axis, [(i, i ^ r) for i in range(4)])  29.1 us
    ppermute x19, waiting for transfers between devices, ring_swap(): return lax.ppermute(a, axis, [(i, i ^ r) for i in range(4)])  28.6 us
    ppermute x18, waiting for transfers between devices, swap(): return lax.ppermute(a, axis, [(0, 1), (1, 0)])  23.2 us
    ppermute x5, waiting for transfers between devices, x_swap(): return lax.ppermute(a, ('cfg', 'xlo'), [(i, 3 - i) for i in range(4)])  15.1 us
    ppermute x18, starting transfers between devices, swap(): return lax.ppermute(a, axis, [(0, 1), (1, 0)])  14 us
    pallas_call x3, Pallas kernels, attention_backward(): pl.pallas_call(kernel, grid=(steps,), in_specs=[rows_of(VIDK), stacked(2,...  11.4 us
    pallas_call x1, Pallas kernels, attention_forward(): pl.pallas_call(forward_kernel, grid=(rows // BLOCK,), in_specs=[whole(a)...  10.8 us
    unnamed x45, local copies, waits for them, and re-layouts  8.75 us
  transfers between devices with their start and end apart: 42, of which 15 were waited for; matrix products, arithmetic and copies ran while one was open for 4% of the time, Pallas kernels for 17%

profile of v2, /device:TPU:0, one launch (start us, length us, event | category | flops | bytes accessed | tf_op | source)
XLA Modules:
  0.0 165.8 jit_solution(7748908709102341041)
XLA Ops:
  5.9 3.3 %shard_map.137 = (bf16[416,768]{1,0:T(8,128)(2,1)}, bf16[224,768]{1,0:T(8,128)(2,1)}, bf16[224,768]{1,0:T(8,128)(2,1)}, bf16[32,768]{1,0:T(8,128)(2,1)}) custom-call(s32[3]{0:T(128)} %pad_add_fusion.at_ref.refs_0_, bf16[128,3072]{1,0:T(8,128)(2,1)} %bitcast.61, bf16[128,3072]{1,0:T(8,128)(2,1)} %bitcast.64, bf16[128,3072]{1,0:T(8,128)(2,1)} %bitcast.67, ...), custom_call_target="tpu_custom_call" | custom-call | tf_op jit(solution)/shard_map/pallas_call | solution.py:118
  9.2 3.1 %collective-permute-start.20 = (bf16[32,768]{1,0:T(8,128)(2,1)}, bf16[32,768]{1,0:T(8,128)(2,1)S(1)}, u32[]{:S(2)}, u32[]{:S(2)}) collective-permute-start(bf16[32,768]{1,0:T(8,128)(2,1)} %get-tuple-element.107), channel_id=1, source_target_pairs={{0,64},{64,0},{1,65},{65,1},{2,66},{66,2},{3,67},{67,3},{4,68},{68... | collective-permute-start | bytes 147464 | tf_op jit(solution)/shard_map/ppermute | solution.py:73
  15.8 4.1 %collective-permute-start.4 = (bf16[4,24,3072]{2,1,0:T(8,128)(2,1)S(1)}, bf16[4,24,3072]{2,1,0:T(8,128)(2,1)S(1)}, u32[]{:S(2)}, u32[]{:S(2)}) collective-permute-start(bf16[4,24,3072]{2,1,0:T(8,128)(2,1)S(1)} %pad_maximum_fusion), channel_id=1, source_target_pairs={{0,3},{1,2},{2,1},{3,0},{4,7},{5,6},{6,5},{7,4},{8,11},{9,10},{10,... | collective-permute-start | bytes 1769480 | tf_op jit(solution)/shard_map/ppermute | solution.py:85
  22.0 3.3 %collective-permute-done.12.got3 = bf16[224,768]{1,0:T(8,128)(2,1)S(1)} collective-permute-done((bf16[224,768]{1,0:T(8,128)(2,1)}, bf16[224,768]{1,0:T(8,128)(2,1)S(1)}, u32[]{:S(2)}, u32[]{:S(2)}) %collective-permute-start.12) | collective-permute-done | bytes 344096 | tf_op jit(solution)/shard_map/ppermute | solution.py:81
  28.7 3.4 %collective-permute-done.4 = bf16[4,24,3072]{2,1,0:T(8,128)(2,1)S(1)} collective-permute-done((bf16[4,24,3072]{2,1,0:T(8,128)(2,1)S(1)}, bf16[4,24,3072]{2,1,0:T(8,128)(2,1)S(1)}, u32[]{:S(2)}, u32[]{:S(2)}) %collective-permute-start.4) | collective-permute-done | bytes 589856 | tf_op jit(solution)/shard_map/ppermute | solution.py:85
  32.1 2.5 %collective-permute-start.22 = (bf16[1664,128]{1,0:T(8,128)(2,1)S(1)}, bf16[1664,128]{1,0:T(8,128)(2,1)S(1)}, u32[]{:S(2)}, u32[]{:S(2)}) collective-permute-start(bf16[1664,128]{1,0:T(8,128)(2,1)S(1)} %get-tuple-element.111), channel_id=1, source_target_pairs={{0,16},{8,24},{16,0},{24,8},{1,17},{9,25},{17,1},{25,9},{2,18},{10... | collective-permute-start | bytes 1277960 | tf_op jit(solution)/shard_map/ppermute | solution.py:85
  34.9 6.6 %collective-permute-done.5 = bf16[2,24,3072]{2,1,0:T(8,128)(2,1)S(1)} collective-permute-done((bf16[2,24,3072]{2,1,0:T(8,128)(2,1)S(1)}, bf16[2,24,3072]{2,1,0:T(8,128)(2,1)S(1)}, u32[]{:S(2)}, u32[]{:S(2)}) %collective-permute-start.5) | collective-permute-done | bytes 294944 | tf_op jit(solution)/shard_map/ppermute | solution.py:85
  41.5 3.0 %collective-permute-start.6 = (bf16[2,24,3072]{2,1,0:T(8,128)(2,1)S(1)}, bf16[2,24,3072]{2,1,0:T(8,128)(2,1)S(1)}, u32[]{:S(2)}, u32[]{:S(2)}) collective-permute-start(bf16[2,24,3072]{2,1,0:T(8,128)(2,1)S(1)} %slice.97), channel_id=1, source_target_pairs={{0,3},{1,2},{2,1},{3,0},{4,7},{5,6},{6,5},{7,4},{8,11},{9,10},{10,... | collective-permute-start | bytes 884744 | tf_op jit(solution)/shard_map/ppermute | solution.py:85
  44.5 5.0 %collective-permute-done.6 = bf16[2,24,3072]{2,1,0:T(8,128)(2,1)S(1)} collective-permute-done((bf16[2,24,3072]{2,1,0:T(8,128)(2,1)S(1)}, bf16[2,24,3072]{2,1,0:T(8,128)(2,1)S(1)}, u32[]{:S(2)}, u32[]{:S(2)}) %collective-permute-start.6) | collective-permute-done | bytes 294944 | tf_op jit(solution)/shard_map/ppermute | solution.py:85
  53.4 5.4 %collective-permute-done.23.refs_3_ = bf16[1664,128]{1,0:T(8,128)(2,1)S(1)} collective-permute-done((bf16[1664,128]{1,0:T(8,128)(2,1)S(1)}, bf16[1664,128]{1,0:T(8,128)(2,1)S(1)}, u32[]{:S(2)}, u32[]{:S(2)}) %collective-permute-start.23) | collective-permute-done | bytes 426016 | tf_op jit(solution)/shard_map/ppermute | solution.py:85
  58.8 2.4 %collective-permute-start.16 = (bf16[64,3072]{1,0:T(8,128)(2,1)S(1)}, bf16[64,3072]{1,0:T(8,128)(2,1)S(1)}, u32[]{:S(2)}, u32[]{:S(2)}) collective-permute-start(bf16[64,3072]{1,0:T(8,128)(2,1)S(1)} %slice.99), channel_id=1, source_target_pairs={{0,96},{32,64},{64,32},{96,0},{1,97},{33,65},{65,33},{97,1},{2,98}... | collective-permute-start | bytes 1179656 | tf_op jit(solution)/shard_map/ppermute | solution.py:81
  63.0 4.8 %collective-permute-done.16.refs_11_ = bf16[64,3072]{1,0:T(8,128)(2,1)S(1)} collective-permute-done((bf16[64,3072]{1,0:T(8,128)(2,1)S(1)}, bf16[64,3072]{1,0:T(8,128)(2,1)S(1)}, u32[]{:S(2)}, u32[]{:S(2)}) %collective-permute-start.16) | collective-permute-done | bytes 393248 | tf_op jit(solution)/shard_map/ppermute | solution.py:81
  75.7 4.6 %shard_map.138 = (bf16[768,128]{1,0:T(8,128)(2,1)S(1)}, bf16[768,128]{1,0:T(8,128)(2,1)S(1)}, bf16[768,128]{1,0:T(8,128)(2,1)S(1)}, bf16[768,128]{1,0:T(8,128)(2,1)S(1)}) custom-call(s32[3]{0:T(128)S(1)} %copy-done.13, bf16[96,3072]{1,0:T(8,128)(2,1)S(1)} %pad_maximum_fusion.1.refs_0_, bf16[96,3072]{1,0:T(8,128)(2,1)S(1)} %pad_maximum_fusion.2.refs_1_, ...), custom_call_target="tpu_custom_call" | custom-call | tf_op jit(solution)/shard_map/pallas_call | solution.py:207
  80.4 2.6 %collective-permute-start.18 = (bf16[768,128]{1,0:T(8,128)(2,1)S(1)}, bf16[768,128]{1,0:T(8,128)(2,1)S(1)}, u32[]{:S(2)}, u32[]{:S(2)}) collective-permute-start(bf16[768,128]{1,0:T(8,128)(2,1)S(1)} %get-tuple-element.103), channel_id=1, source_target_pairs={{0,16},{8,24},{16,0},{24,8},{1,17},{9,25},{17,1},{25,9},{2,18},{10... | collective-permute-start | bytes 589832 | tf_op jit(solution)/shard_map/ppermute | solution.py:85
  85.1 10.8 %shard_map.140 = (bf16[1536,2048]{1,0:T(8,128)(2,1)S(1)}, bf16[2,1536,256]{2,1,0:T(8,128)(2,1)S(1)}, f32[3,1536,128]{2,1,0:T(8,128)S(1)}, f32[2,1536,128]{2,1,0:...) custom-call(f32[2,256]{1,0:T(2,128)S(1)} %compare_select_fusion.bias, ...), custom_call_target="tpu_custom_call" | custom-call | tf_op jit(solution)/shard_map/pallas_call | solution.py:279
  96.0 4.0 %shard_map.142 = (bf16[4,640,128]{2,1,0:T(8,128)(2,1)S(1)}, bf16[4,640,128]{2,1,0:T(8,128)(2,1)S(1)}, bf16[128,128]{1,0:T(8,128)(2,1)S(1)}, bf16[128,128]{1,0:T(...) custom-call(bf16[1536,2048]{1,0:T(8,128)(2,1)S(1)} %get-tuple-element.124.refs_0_, ...), custom_call_target="tpu_custom_call" | custom-call | tf_op jit(solution)/shard_map/pallas_call | solution.py:406
  103.7 5.8 %shard_map.144 = (bf16[4,640,128]{2,1,0:T(8,128)(2,1)S(1)}, bf16[4,640,128]{2,1,0:T(8,128)(2,1)S(1)}, bf16[256,128]{1,0:T(8,128)(2,1)S(1)}, bf16[256,128]{1,0:T(8,128)(2,1)S(1)}, bf16[256,128]{1,0:T(8,128)(2,1)S(1)}) custom-call(bf16[1536,2048]{1,0:T(8,128)(2,1)S(1)} %get-tuple-element.124.refs_0_, bf16[2,1536,256]{2,1,0:T(8,128)(2,1)S(1)} %get-tuple-element.125.refs_1_, ...), custom_call_target="tpu_custom_call" | custom-call | tf_op jit(solution)/shard_map/pallas_call | solution.py:406
  112.5 7.0 %collective-permute-done.32.refs_3_ = bf16[768,128]{1,0:T(8,128)(2,1)S(1)} collective-permute-done((bf16[768,128]{1,0:T(8,128)(2,1)S(1)}, bf16[768,128]{1,0:T(8,128)(2,1)S(1)}, u32[]{:S(2)}, u32[]{:S(2)}) %collective-permute-start.32) | collective-permute-done | bytes 196640 | tf_op jit(solution)/shard_map/ppermute | solution.py:85
  125.2 3.8 %collective-permute-start.37 = (bf16[416,256]{1,0:T(8,128)(2,1)S(1)}, bf16[416,256]{1,0:T(8,128)(2,1)S(1)}, u32[]{:S(2)}, u32[]{:S(2)}) collective-permute-start(bf16[416,256]{1,0:T(8,128)(2,1)S(1)} %get-tuple-element.172), channel_id=1, source_target_pairs={{0,64},{64,0},{1,65},{65,1},{2,66},{66,2},{3,67},{67,3},{4,68},{68... | collective-permute-start | bytes 638984 | tf_op jit(solution)/shard_map/ppermute | solution.py:73
  129.9 3.7 %collective-permute-done.37.refs_6_ = bf16[416,256]{1,0:T(8,128)(2,1)S(1)} collective-permute-done((bf16[416,256]{1,0:T(8,128)(2,1)S(1)}, bf16[416,256]{1,0:T(8,128)(2,1)S(1)}, u32[]{:S(2)}, u32[]{:S(2)}) %collective-permute-start.37) | collective-permute-done | bytes 213024 | tf_op jit(solution)/shard_map/ppermute | solution.py:73
  133.6 4.5 %collective-permute-done.38.refs_7_ = bf16[416,256]{1,0:T(8,128)(2,1)S(1)} collective-permute-done((bf16[416,256]{1,0:T(8,128)(2,1)S(1)}, bf16[416,256]{1,0:T(8,128)(2,1)S(1)}, u32[]{:S(2)}, u32[]{:S(2)}) %collective-permute-start.38) | collective-permute-done | bytes 213024 | tf_op jit(solution)/shard_map/ppermute | solution.py:81
  143.7 8.0 %collective-permute-done.39.refs_1_ = bf16[416,512]{1,0:T(8,128)(2,1)S(1)} collective-permute-done((bf16[416,512]{1,0:T(8,128)(2,1)S(1)}, bf16[416,512]{1,0:T(8,128)(2,1)S(1)}, u32[]{:S(2)}, u32[]{:S(2)}) %collective-permute-start.39) | collective-permute-done | bytes 426016 | tf_op jit(solution)/shard_map/ppermute | solution.py:73
  151.7 9.3 %collective-permute-done.40.refs_2_ = bf16[416,512]{1,0:T(8,128)(2,1)S(1)} collective-permute-done((bf16[416,512]{1,0:T(8,128)(2,1)S(1)}, bf16[416,512]{1,0:T(8,128)(2,1)S(1)}, u32[]{:S(2)}, u32[]{:S(2)}) %collective-permute-start.40) | collective-permute-done | bytes 426016 | tf_op jit(solution)/shard_map/ppermute | solution.py:73
  161.0 2.6 %collective-permute-done.41.refs_3_ = bf16[416,512]{1,0:T(8,128)(2,1)S(1)} collective-permute-done((bf16[416,512]{1,0:T(8,128)(2,1)S(1)}, bf16[416,512]{1,0:T(8,128)(2,1)S(1)}, u32[]{:S(2)}, u32[]{:S(2)}) %collective-permute-start.41) | collective-permute-done | bytes 426016 | tf_op jit(solution)/shard_map/ppermute | solution.py:81
  (141 shorter events, 50.5 us)
Async XLA Ops:
  0.6 14.5 %collective-permute-start = (bf16[24,3072]{1,0:T(8,128)(2,1)}, bf16[24,3072]{1,0:T(8,128)(2,1)S(1)}, u32[]{:S(2)}, u32[]{:S(2)}) collective-permute-start(bf16[24,3072]{1,0:T(8,128)(2,1)} %param.19), channel_id=1, source_target_pairs={{0,8},{8,0},{16,24},{24,16},{1,9},{9,1},{17,25},{25,17},{2,10},{10... | collective-permute-start | bytes 442376 | tf_op jit(solution)/shard_map/ppermute | solution.py:85
  2.4 13.4 %collective-permute-start.2 = (bf16[24,3072]{1,0:T(8,128)(2,1)}, bf16[24,3072]{1,0:T(8,128)(2,1)S(1)}, u32[]{:S(2)}, u32[]{:S(2)}) collective-permute-start(bf16[24,3072]{1,0:T(8,128)(2,1)} %param.19), channel_id=1, source_target_pairs={{0,24},{8,16},{16,8},{24,0},{1,25},{9,17},{17,9},{25,1},{2,26},{10... | collective-permute-start | bytes 442376 | tf_op jit(solution)/shard_map/ppermute | solution.py:85
  9.2 16.9 %collective-permute-start.20 = (bf16[32,768]{1,0:T(8,128)(2,1)}, bf16[32,768]{1,0:T(8,128)(2,1)S(1)}, u32[]{:S(2)}, u32[]{:S(2)}) collective-permute-start(bf16[32,768]{1,0:T(8,128)(2,1)} %get-tuple-element.107), channel_id=1, source_target_pairs={{0,64},{64,0},{1,65},{65,1},{2,66},{66,2},{3,67},{67,3},{4,68},{68... | collective-permute-start | bytes 147464 | tf_op jit(solution)/shard_map/ppermute | solution.py:73
  15.8 16.3 %collective-permute-start.4 = (bf16[4,24,3072]{2,1,0:T(8,128)(2,1)S(1)}, bf16[4,24,3072]{2,1,0:T(8,128)(2,1)S(1)}, u32[]{:S(2)}, u32[]{:S(2)}) collective-permute-start(bf16[4,24,3072]{2,1,0:T(8,128)(2,1)S(1)} %pad_maximum_fusion), channel_id=1, source_target_pairs={{0,3},{1,2},{2,1},{3,0},{4,7},{5,6},{6,5},{7,4},{8,11},{9,10},{10,... | collective-permute-start | bytes 1769480 | tf_op jit(solution)/shard_map/ppermute | solution.py:85
  19.9 14.8 %collective-permute-start.3 = (bf16[4,24,3072]{2,1,0:T(8,128)(2,1)S(1)}, bf16[4,24,3072]{2,1,0:T(8,128)(2,1)S(1)}, u32[]{:S(2)}, u32[]{:S(2)}) collective-permute-start(bf16[4,24,3072]{2,1,0:T(8,128)(2,1)S(1)} %pad_maximum_fusion), channel_id=1, source_target_pairs={{0,1},{1,0},{2,3},{3,2},{4,5},{5,4},{6,7},{7,6},{8,9},{9,8},{10,11... | collective-permute-start | bytes 1769480 | tf_op jit(solution)/shard_map/ppermute | solution.py:85
  25.3 25.9 %collective-permute-start.14 = (bf16[128,3072]{1,0:T(8,128)(2,1)S(1)}, bf16[128,3072]{1,0:T(8,128)(2,1)S(1)}, u32[]{:S(2)}, u32[]{:S(2)}) collective-permute-start(bf16[128,3072]{1,0:T(8,128)(2,1)S(1)} %fusion.refs_8_), channel_id=1, source_target_pairs={{0,96},{32,64},{64,32},{96,0},{1,97},{33,65},{65,33},{97,1},{2,98}... | collective-permute-start | bytes 2359304 | tf_op jit(solution)/shard_map/ppermute | solution.py:81
  26.1 25.2 %collective-permute-start.13 = (bf16[128,3072]{1,0:T(8,128)(2,1)S(1)}, bf16[128,3072]{1,0:T(8,128)(2,1)S(1)}, u32[]{:S(2)}, u32[]{:S(2)}) collective-permute-start(bf16[128,3072]{1,0:T(8,128)(2,1)S(1)} %fusion.refs_8_), channel_id=1, source_target_pairs={{0,32},{32,0},{1,33},{33,1},{2,34},{34,2},{3,35},{35,3},{4,36},{36... | collective-permute-start | bytes 2359304 | tf_op jit(solution)/shard_map/ppermute | solution.py:73
  27.8 25.0 %collective-permute-start.21 = (bf16[1664,128]{1,0:T(8,128)(2,1)S(1)}, bf16[1664,128]{1,0:T(8,128)(2,1)}, u32[]{:S(2)}, u32[]{:S(2)}) collective-permute-start(bf16[1664,128]{1,0:T(8,128)(2,1)S(1)} %get-tuple-element.110), channel_id=1, source_target_pairs={{0,8},{8,0},{16,24},{24,16},{1,9},{9,1},{17,25},{25,17},{2,10},{10... | collective-permute-start | bytes 1277960 | tf_op jit(solution)/shard_map/ppermute | solution.py:85
  32.1 21.0 %collective-permute-start.22 = (bf16[1664,128]{1,0:T(8,128)(2,1)S(1)}, bf16[1664,128]{1,0:T(8,128)(2,1)S(1)}, u32[]{:S(2)}, u32[]{:S(2)}) collective-permute-start(bf16[1664,128]{1,0:T(8,128)(2,1)S(1)} %get-tuple-element.111), channel_id=1, source_target_pairs={{0,16},{8,24},{16,0},{24,8},{1,17},{9,25},{17,1},{25,9},{2,18},{10... | collective-permute-start | bytes 1277960 | tf_op jit(solution)/shard_map/ppermute | solution.py:85
  51.1 17.4 %collective-permute-start.7 = (bf16[96,3072]{1,0:T(8,128)(2,1)S(1)}, bf16[96,3072]{1,0:T(8,128)(2,1)S(1)}, u32[]{:S(2)}, u32[]{:S(2)}) collective-permute-start(bf16[96,3072]{1,0:T(8,128)(2,1)S(1)} %pad_maximum_fusion.1.refs_0_), channel_id=1, source_target_pairs={{0,4},{4,0},{1,5},{5,1},{2,6},{6,2},{3,7},{7,3},{8,12},{12,8},{9,1... | collective-permute-start | bytes 1769480 | tf_op jit(solution)/shard_map/ppermute | solution.py:73
  52.8 17.2 %collective-permute-start.8 = (bf16[96,3072]{1,0:T(8,128)(2,1)S(1)}, bf16[96,3072]{1,0:T(8,128)(2,1)}, u32[]{:S(2)}, u32[]{:S(2)}) collective-permute-start(bf16[96,3072]{1,0:T(8,128)(2,1)S(1)} %pad_maximum_fusion.2.refs_1_), channel_id=1, source_target_pairs={{0,4},{4,0},{1,5},{5,1},{2,6},{6,2},{3,7},{7,3},{8,12},{12,8},{9,1... | collective-permute-start | bytes 1769480 | tf_op jit(solution)/shard_map/ppermute | solution.py:73
  53.1 17.1 %collective-permute-start.9 = (bf16[96,3072]{1,0:T(8,128)(2,1)S(1)}, bf16[96,3072]{1,0:T(8,128)(2,1)}, u32[]{:S(2)}, u32[]{:S(2)}) collective-permute-start(bf16[96,3072]{1,0:T(8,128)(2,1)S(1)} %pad_maximum_fusion.3.refs_2_), channel_id=1, source_target_pairs={{0,4},{4,0},{1,5},{5,1},{2,6},{6,2},{3,7},{7,3},{8,12},{12,8},{9,1... | collective-permute-start | bytes 1769480 | tf_op jit(solution)/shard_map/ppermute | solution.py:73
  69.4 13.6 %collective-permute-start.25 = (bf16[1664,128]{1,0:T(8,128)(2,1)}, bf16[1664,128]{1,0:T(8,128)(2,1)}, u32[]{:S(2)}, u32[]{:S(2)}) collective-permute-start(bf16[1664,128]{1,0:T(8,128)(2,1)} %collective-permute-done.21.refs_1_), channel_id=1, source_target_pairs={{0,4},{4,0},{1,5},{5,1},{2,6},{6,2},{3,7},{7,3},{8,12},{12,8},{9,1... | collective-permute-start | bytes 1277960 | tf_op jit(solution)/shard_map/ppermute | solution.py:73
  70.1 15.1 %collective-permute-start.26 = (bf16[1664,128]{1,0:T(8,128)(2,1)}, bf16[1664,128]{1,0:T(8,128)(2,1)S(1)}, u32[]{:S(2)}, u32[]{:S(2)}) collective-permute-start(bf16[1664,128]{1,0:T(8,128)(2,1)} %copy-done.7), channel_id=1, source_target_pairs={{0,4},{4,0},{1,5},{5,1},{2,6},{6,2},{3,7},{7,3},{8,12},{12,8},{9,1... | collective-permute-start | bytes 1277960 | tf_op jit(solution)/shard_map/ppermute | solution.py:73
  70.2 15.0 %collective-permute-start.27 = (bf16[1664,128]{1,0:T(8,128)(2,1)}, bf16[1664,128]{1,0:T(8,128)(2,1)S(1)}, u32[]{:S(2)}, u32[]{:S(2)}) collective-permute-start(bf16[1664,128]{1,0:T(8,128)(2,1)} %copy-done.9), channel_id=1, source_target_pairs={{0,4},{4,0},{1,5},{5,1},{2,6},{6,2},{3,7},{7,3},{8,12},{12,8},{9,1... | collective-permute-start | bytes 1277960 | tf_op jit(solution)/shard_map/ppermute | solution.py:73
  80.3 15.7 %collective-permute-start.17 = (bf16[768,128]{1,0:T(8,128)(2,1)S(1)}, bf16[768,128]{1,0:T(8,128)(2,1)S(1)}, u32[]{:S(2)}, u32[]{:S(2)}) collective-permute-start(bf16[768,128]{1,0:T(8,128)(2,1)S(1)} %get-tuple-element.102), channel_id=1, source_target_pairs={{0,8},{8,0},{16,24},{24,16},{1,9},{9,1},{17,25},{25,17},{2,10},{10... | collective-permute-start | bytes 589832 | tf_op jit(solution)/shard_map/ppermute | solution.py:85
  80.4 15.6 %collective-permute-start.18 = (bf16[768,128]{1,0:T(8,128)(2,1)S(1)}, bf16[768,128]{1,0:T(8,128)(2,1)S(1)}, u32[]{:S(2)}, u32[]{:S(2)}) collective-permute-start(bf16[768,128]{1,0:T(8,128)(2,1)S(1)} %get-tuple-element.103), channel_id=1, source_target_pairs={{0,16},{8,24},{16,0},{24,8},{1,17},{9,25},{17,1},{25,9},{2,18},{10... | collective-permute-start | bytes 589832 | tf_op jit(solution)/shard_map/ppermute | solution.py:85
  83.0 13.0 %collective-permute-start.19 = (bf16[768,128]{1,0:T(8,128)(2,1)S(1)}, bf16[768,128]{1,0:T(8,128)(2,1)S(1)}, u32[]{:S(2)}, u32[]{:S(2)}) collective-permute-start(bf16[768,128]{1,0:T(8,128)(2,1)S(1)} %get-tuple-element.104), channel_id=1, source_target_pairs={{0,24},{8,16},{16,8},{24,0},{1,25},{9,17},{17,9},{25,1},{2,26},{10... | collective-permute-start | bytes 589832 | tf_op jit(solution)/shard_map/ppermute | solution.py:85
  120.4 17.6 %collective-permute-start.33 = (bf16[896,128]{1,0:T(8,128)(2,1)S(1)}, bf16[896,128]{1,0:T(8,128)(2,1)S(1)}, u32[]{:S(2)}, u32[]{:S(2)}) collective-permute-start(bf16[896,128]{1,0:T(8,128)(2,1)S(1)} %get-tuple-element.163), channel_id=1, source_target_pairs={{0,8},{8,0},{16,24},{24,16},{1,9},{9,1},{17,25},{25,17},{2,10},{10... | collective-permute-start | bytes 688136 | tf_op jit(solution)/shard_map/ppermute | solution.py:85
  121.0 17.1 %collective-permute-start.34 = (bf16[896,128]{1,0:T(8,128)(2,1)S(1)}, bf16[896,128]{1,0:T(8,128)(2,1)S(1)}, u32[]{:S(2)}, u32[]{:S(2)}) collective-permute-start(bf16[896,128]{1,0:T(8,128)(2,1)S(1)} %get-tuple-element.164), channel_id=1, source_target_pairs={{0,16},{8,24},{16,0},{24,8},{1,17},{9,25},{17,1},{25,9},{2,18},{10... | collective-permute-start | bytes 688136 | tf_op jit(solution)/shard_map/ppermute | solution.py:85
  123.3 14.8 %collective-permute-start.35 = (bf16[896,128]{1,0:T(8,128)(2,1)S(1)}, bf16[896,128]{1,0:T(8,128)(2,1)S(1)}, u32[]{:S(2)}, u32[]{:S(2)}) collective-permute-start(bf16[896,128]{1,0:T(8,128)(2,1)S(1)} %get-tuple-element.165), channel_id=1, source_target_pairs={{0,24},{8,16},{16,8},{24,0},{1,25},{9,17},{17,9},{25,1},{2,26},{10... | collective-permute-start | bytes 688136 | tf_op jit(solution)/shard_map/ppermute | solution.py:85
  138.9 12.8 %collective-permute-start.39 = (bf16[416,512]{1,0:T(8,128)(2,1)S(1)}, bf16[416,512]{1,0:T(8,128)(2,1)S(1)}, u32[]{:S(2)}, u32[]{:S(2)}) collective-permute-start(bf16[416,512]{1,0:T(8,128)(2,1)S(1)} %get-tuple-element.179), channel_id=1, source_target_pairs={{0,32},{32,0},{1,33},{33,1},{2,34},{34,2},{3,35},{35,3},{4,36},{36... | collective-permute-start | bytes 1277960 | tf_op jit(solution)/shard_map/ppermute | solution.py:73
  139.6 21.3 %collective-permute-start.40 = (bf16[416,512]{1,0:T(8,128)(2,1)S(1)}, bf16[416,512]{1,0:T(8,128)(2,1)S(1)}, u32[]{:S(2)}, u32[]{:S(2)}) collective-permute-start(bf16[416,512]{1,0:T(8,128)(2,1)S(1)} %get-tuple-element.180), channel_id=1, source_target_pairs={{0,64},{64,0},{1,65},{65,1},{2,66},{66,2},{3,67},{67,3},{4,68},{68... | collective-permute-start | bytes 1277960 | tf_op jit(solution)/shard_map/ppermute | solution.py:73
  142.0 21.5 %collective-permute-start.41 = (bf16[416,512]{1,0:T(8,128)(2,1)S(1)}, bf16[416,512]{1,0:T(8,128)(2,1)S(1)}, u32[]{:S(2)}, u32[]{:S(2)}) collective-permute-start(bf16[416,512]{1,0:T(8,128)(2,1)S(1)} %get-tuple-element.181), channel_id=1, source_target_pairs={{0,96},{32,64},{64,32},{96,0},{1,97},{33,65},{65,33},{97,1},{2,98}... | collective-permute-start | bytes 1277960 | tf_op jit(solution)/shard_map/ppermute | solution.py:81
  (37 other events, 294.5 us)

commit v3 on v2

--- a/solution.py
+++ b/solution.py
@@ -49,7 +49,7 @@
     return pltpu.CompilerParams(vmem_limit_bytes=mib * MIB)
 
 
-COST = pl.CostEstimate(flops=0, bytes_accessed=0, transcendentals=0)
+COST = pl.CostEstimate(flops=10**6, bytes_accessed=16, transcendentals=0)
 
 
 def whole(a):
@@ -59,14 +59,6 @@
 
 def lanes(start, count):
     return pl.ds(pl.multiple_of(start, HD), count)
-
-
-def run_copies(copies, sems):
-    started = [pltpu.make_async_copy(src, dst, sems.at[i]) for i, (src, dst) in enumerate(copies)]
-    for copy in started:
-        copy.start()
-    for copy in started:
-        copy.wait()
 
 
 def swap(a, axis):
@@ -129,14 +121,13 @@
     )(at, *arrays)
 
 
-def cut_y_kernel(at_ref, own, got1, got2, got3, *outs):
-    y = at_ref[1]
+def cut_y_kernel(own, got1, got2, got3, outs):
     half = TOK // 2
     quarter = TOK // 4
-    for r, out in enumerate(outs):
-        yd = y ^ r
-        head_a = lanes(yd * HD, HD)
-        head_b = lanes((4 + yd // 2) * HD, HD)
+    for yd in range(4):
+        out = outs.at[yd]
+        head_a = slice(yd * HD, (yd + 1) * HD)
+        head_b = slice((4 + yd // 2) * HD, (5 + yd // 2) * HD)
         for row, tensor, head in (
             (K_A, 1, head_a),
             (V_A, 2, head_a),
@@ -161,35 +152,39 @@
                 out[row + s * TT : row + (s + 1) * TT] = src[start : start + TT, head]
         skip = (yd % 2) * quarter
         for i, (src, first) in enumerate(((own, 0), (own, half), (got1, 0), (got3, 0))):
-            rows = pl.ds(pl.multiple_of(first + skip, quarter), quarter)
+            rows = slice(first + skip, first + skip + quarter)
             out[Q_B + i * quarter : Q_B + (i + 1) * quarter] = src[rows, head_b]
 
 
-def cut_y(at, own, got1, got2, got3):
-    arrays = (own, got1, got2, got3)
-    shapes = [bf16(MSG, HD)] * 4
+def cut_y(*arrays):
+    shape = bf16(4, MSG, HD)
     return pl.pallas_call(
         cut_y_kernel,
-        in_specs=[SMEM] + [whole(a) for a in arrays],
-        out_specs=[whole(a) for a in shapes],
-        out_shape=shapes,
+        in_specs=[whole(a) for a in arrays],
+        out_specs=whole(shape),
+        out_shape=shape,
         compiler_params=params(8),
         cost_estimate=COST,
-    )(at, *arrays)
-
-
-def project_kernel(at_ref, *refs):
-    y, c = at_ref[1], at_ref[2]
-    w_refs, a_refs, outs = refs[:8], refs[8:13], refs[13:17]
-    w_all, a_all, out = refs[17:]
-    for i, ref in enumerate(w_refs):
-        row = pl.multiple_of(((y ^ (i % 4)) * 2 + (c ^ (i // 4))) * WROWS, WROWS)
-        w_all[pl.ds(row, WROWS)] = ref[...]
-    row = 0
-    for ref in a_refs:
-        a_all[row : row + ref.shape[0]] = ref[...]
-        row += ref.shape[0]
-    out[...] = dot(a_all[...], w_all[...], NT).astype(jnp.bfloat16)
+    )(*arrays)
+
+
+def project_kernel(at_ref, order, *refs):
+    y = at_ref[1]
+    w_refs, a_refs, outs = refs[:10], refs[10:15], refs[15:19]
+    w_all, a_all, out, sems = refs[19:]
+    copies = []
+    for refs, whole_ref in ((w_refs, w_all), (a_refs, a_all)):
+        row = 0
+        for ref in refs:
+            copies.append((ref, whole_ref.at[pl.ds(row, ref.shape[0])]))
+            row += ref.shape[0]
+    started = [pltpu.make_async_copy(src, dst, sems.at[i]) for i, (src, dst) in enumerate(copies)]
+    for copy in started:
+        copy.start()
+    for copy in started:
+        copy.wait()
+    product = dot(a_all[...], w_all[...], NT).astype(jnp.bfloat16)
+    out[...] = dot(product, order[...], NN).astype(jnp.bfloat16)
     quarter = TOK // 4
     for r in range(4):
         yd = y ^ r
@@ -201,27 +196,29 @@
             outs[r][4 * TOK + i * quarter : 4 * TOK + (i + 1) * quarter] = out[rows, head_b]
 
 
-def project(at, weights, adjoints):
+def project(at, order, weights, adjoints):
     width = weights[0].shape[1]
     rows = 4 * TOK
     return pl.pallas_call(
         project_kernel,
-        in_specs=[SMEM] + vmem_specs(13),
+        in_specs=[SMEM, whole(order)] + [pl.BlockSpec(memory_space=pl.ANY)] * 15,
         out_specs=vmem_specs(4),
         out_shape=[bf16(rows + rows // 2, HD)] * 4,
         scratch_shapes=[
             pltpu.VMEM((XW, width), jnp.bfloat16),
             pltpu.VMEM((rows, width), jnp.bfloat16),
             pltpu.VMEM((rows, XW), jnp.bfloat16),
+            pltpu.SemaphoreType.DMA((15,)),
         ],
-        compiler_params=params(16),
-        cost_estimate=COST,
-    )(at, *weights, *adjoints)
-
-
-def forward_kernel(bias_ref, *refs):
-    msgs = refs[:8]
-    e_ref, p_ref, o_ref, w_ref, k_all, v_all, q_ref, q_all = refs[8:]
+        compiler_params=params(20),
+        cost_estimate=COST,
+    )(at, order, *weights, *adjoints)
+
+
+def forward_kernel(at_ref, bias_ref, own, other, *refs):
+    e_ref, p_ref, o_ref, w_ref, k_all, v_all, q_ref, q_all = refs
+    y = at_ref[1]
+    msgs = [ref.at[y ^ r] for ref in (own, other) for r in range(4)]
     step = pl.program_id(0)
     run = 2 * TT
 
@@ -267,10 +264,10 @@
         o_ref[p] = w * ov + dot(pt, v_all[head, text], NN)
 
 
-def attention_forward(bias, own, other):
+def attention_forward(at, bias, own, other):
     keys = VIDK + 2 * TXTK
     rows = 12 * TOK
-    arrays = (bias, *own, *other)
+    arrays = (bias, own, other)
     heads = bf16(2, keys, HD)
 
     def stacked(count, width):
@@ -279,7 +276,7 @@
     return pl.pallas_call(
         forward_kernel,
         grid=(rows // BLOCK,),
-        in_specs=[whole(a) for a in arrays],
+        in_specs=[SMEM] + [whole(a) for a in arrays],
         out_specs=[
             pl.BlockSpec((BLOCK, VIDK), lambda i: (i, 0)),
             stacked(2, TXTK),
@@ -301,7 +298,7 @@
         scratch_shapes=[pltpu.VMEM((rows, HD), jnp.bfloat16)],
         compiler_params=params(24),
         cost_estimate=COST,
-    )(*arrays)
+    )(at, *arrays)
 
 
 def backward_kernel(shape, *refs):
@@ -536,12 +533,22 @@
     x = 2 * h + l
     at = jnp.stack([x, y, c]).astype(jnp.int32)
 
-    w_y = jnp.stack([w_out] + [ring_swap(w_out, "y", r) for r in (1, 2, 3)])
-    w_z1, w_z3 = ring_swap(w_y, "fsdp", 1), ring_swap(w_y, "fsdp", 3)
-    w_parts = [w_y, w_z1, ring_swap(w_z3[:2], "fsdp", 1), ring_swap(w_z1[2:], "fsdp", 3), w_z3]
+    w_y = [w_out] + [ring_swap(w_out, "y", r) for r in (1, 2, 3)]
+    two, four = jnp.arange(2, dtype=jnp.int32), jnp.arange(4, dtype=jnp.int32)
+    shard = (y ^ four[None, None, :]) * 2 + (c ^ two[:, None, None])
+    shard = shard * 4 + (z ^ four[None, :, None])
+    rows = w_out.shape[0]
+    channel = shard[..., None] * rows + jnp.arange(rows, dtype=jnp.int32)
+    order = channel.reshape(-1, 1) == jnp.arange(XW, dtype=jnp.int32)[None]
+    order = order.astype(jnp.bfloat16)
 
     own, to1, to3, to2 = cut_x(at, q_video[0], k_video[0], v_video[0], k_text[0, 0], v_text[0, 0])
     got1, got2, got3 = x_swap(to1, 1), x_swap(to2, 2), x_swap(to3, 3)
+    got2, w_y = lax.optimization_barrier((got2, jnp.concatenate(w_y, axis=0)))
+    got1, w_y = lax.optimization_barrier((got1, w_y))
+    w_z1, w_z3 = ring_swap(w_y, "fsdp", 1), ring_swap(w_y, "fsdp", 3)
+    half = WROWS // 2
+    w_z2 = [ring_swap(w_z3[:half], "fsdp", 1), ring_swap(w_z1[half:], "fsdp", 3)]
 
     guidance = 1.5 + guide_index[0].astype(jnp.float32)
     pass_weight = jnp.where(h == 0, guidance, 1.0 - guidance)
@@ -552,27 +559,27 @@
     scaled1, scaled3 = x_swap(scaled, 1), x_swap(scaled, 3)
     half = TOK // 2
     adjoints = [scaled, scaled1, x_swap(scaled3[:half], 1), x_swap(scaled1[half:], 3), scaled3]
-    messages = cut_y(at, own, got1, got2, got3)
-    arrived = [messages[0]] + [ring_swap(messages[r], "y", r) for r in (1, 2, 3)]
-    w_z = jnp.concatenate(w_parts, axis=0).reshape(4, *w_y.shape)
-    w_z = [lax.dynamic_index_in_dim(w_z, z ^ j, 0, False) for j in range(4)]
-    w_own = [jnp.concatenate([part[r] for part in w_z], axis=0) for r in range(4)]
-    other = [swap(message, "core") for message in arrived]
-    weights = w_own + [swap(piece, "core") for piece in w_own]
-
-    two = jnp.arange(2, dtype=jnp.int32)
+    messages = cut_y(own, got1, got2, got3)
+    arrived = lax.all_to_all(messages, "y", split_axis=0, concat_axis=0, tiled=True)
+    w_swapped = [swap(piece, "core") for piece in (w_y, w_z1, w_z3)]
+    adjoints, w_z2, w_swapped = lax.optimization_barrier((adjoints, w_z2, w_swapped))
+    w_z2_swapped = [swap(piece, "core") for piece in w_z2]
+    weights = [w_y, w_z1] + w_z2 + [w_z3] + w_swapped[:2] + w_z2_swapped + w_swapped[2:]
+    arrived, weights = lax.optimization_barrier((arrived, weights))
+    other = swap(arrived, "core")
+
     at_core = (c ^ two)[:, None, None, None]
-    at_y = (y ^ jnp.arange(4, dtype=jnp.int32))[None, :, None, None]
+    at_y = (y ^ four)[None, :, None, None]
     at_l = (l ^ two)[None, None, :, None]
     position = ((at_l * 4 + at_y) * 2 + at_core) * TT + jnp.arange(TT, dtype=jnp.int32)
     position = position.reshape(1, -1)
     lens = jnp.where(h == 0, text_len[:, 0], text_len[::-1, 0])
     bias = jnp.where(position < lens[:, None], 0.0, -jnp.inf).astype(jnp.float32)
 
-    to_y = project(at, weights, adjoints)
+    to_y = project(at, order, weights, adjoints)
     dos = [to_y[0]] + [ring_swap(to_y[r], "y", r) for r in (1, 2, 3)]
     other, to_y = lax.optimization_barrier((other, to_y))
-    stored = attention_forward(bias, arrived, other)
+    stored = attention_forward(at, bias, arrived, other)
     dos, stored = lax.optimization_barrier((dos, stored))
 
     def x_back(parts):
@@ -581,20 +588,19 @@
     def y_back(totals):
         return [totals[0]] + [ring_swap(totals[r], "y", r) for r in (1, 2, 3)]
 
-    dk_sum, dv_sum, dq_0 = attention_backward(stored, dos[:1], False, 0, final=False)
+    kept_a, sent_a, dq_a = attention_backward(stored, dos, False)
+    kept_a, dos = lax.optimization_barrier((kept_a, dos))
     kept_b, sent_b, dq_b = attention_backward(stored, dos, True)
-    totals_b = add_cores(kept_b, swap(sent_b, "core"), dq_b)
-    dk_sum, totals_b = lax.optimization_barrier((dk_sum, totals_b))
-    got_b = y_back(totals_b)
-    kept_a, sent_a, dq_123 = attention_backward(stored, dos[1:], False, 1, (dk_sum, dv_sum))
-    sent_a, got_b[1], got_b[3] = lax.optimization_barrier((sent_a, got_b[1], got_b[3]))
     came_a = swap(sent_a, "core")
-    came_a, got_b = lax.optimization_barrier((came_a, got_b))
-    totals_a = add_cores(kept_a, came_a, dq_0 + dq_123)
+    sent_b, came_a = lax.optimization_barrier((sent_b, came_a))
+    came_b = swap(sent_b, "core")
+    got_a = y_back(add_cores(kept_a, came_a, dq_a))
+    total_b = add_cores(kept_b, came_b, dq_b)
+    total_b, got_a = lax.optimization_barrier((total_b, got_a))
+    parts_a = x_back(merge_y(at, got_a, False))
+    got_b = y_back(total_b)
+    got_b, parts_a[1], parts_a[2] = lax.optimization_barrier((got_b, parts_a[1], parts_a[2]))
     parts_b = x_back(merge_y(at, got_b, True))
-    got_a = y_back(totals_a)
-    got_a, parts_b = lax.optimization_barrier((got_a, parts_b))
-    parts_a = x_back(merge_y(at, got_a, False))
     dq, dk, dv, dkt, dvt = merge_x(at, parts_a, parts_b)
     return dq[None], dk[None], dv[None], dkt[None, None], dvt[None, None]
 

time: 166 us -> 156 us (0.940)
  waiting for transfers between devices: 66.9 us -> 55.3 us
  Pallas kernels: 35.8 us -> 39.1 us
  local copies, waits for them, and re-layouts: 9.95 us -> 7.53 us
    ppermute x5, waiting for transfers between devices: 15.1 us -> 4.79 us  [x_swap(): return lax.ppermute(a, ('cfg', 'xlo'), [(i, 3 - i) for i in range(4)])]
    unnamed x45 -> x18, local copies, waits for them, and re-layouts: 8.75 us -> 2.54 us
    ppermute x18 -> x16, waiting for transfers between devices: 23.2 us -> 17.2 us  [swap(): return lax.ppermute(a, axis, [(0, 1), (1, 0)])]
    ppermute x19 -> x16, waiting for transfers between devices: 28.6 us -> 33.3 us  [ring_swap(): return lax.ppermute(a, axis, [(i, i ^ r) for i in range(4)])]
    ppermute x19 -> x16, starting transfers between devices: 29.1 us -> 24.7 us  [ring_swap(): return lax.ppermute(a, axis, [(i, i ^ r) for i in range(4)])]
    all_to_all x0 -> x1, starting transfers between devices: none -> 4.26 us  [local(): lax.all_to_all(messages, 'y', split_axis=0, concat_axis=0, tiled=True)]
    pallas_call x3, Pallas kernels: 17.1 us -> 20.3 us  [the longest x1 10.9 us: attention_forward(): pl.pallas_call(forward_kernel, grid=(rows // BLOCK,), in_specs=[SMEM] + [...]
    slice x2, local copies, waits for them, and re-layouts: 0.04 us -> 2.67 us  [the longest x1 1.69 us: local(): w_z3[:half]]
  transfers between devices with their start and end apart: 42 -> 38, of which waited for: 15 -> 18; matrix products, arithmetic and copies ran while one was open for 4% -> 5% of each run, Pallas kernels for 17% -> 18%
where the time goes in v3:
time: 156 us; the launch traced here: 155 us
  waiting for transfers between devices  55.3 us (35%)
  starting transfers between devices  49.2 us (32%)
  Pallas kernels  39.1 us (25%)
  local copies, waits for them, and re-layouts  7.53 us (5%)
  other arithmetic  2.54 us (2%)
  between operations  1.6 us (1%)
    ppermute x16, waiting for transfers between devices, ring_swap(): return lax.ppermute(a, axis, [(i, i ^ r) for i in range(4)])  33.3 us
    ppermute x16, starting transfers between devices, ring_swap(): return lax.ppermute(a, axis, [(i, i ^ r) for i in range(4)])  24.7 us
    ppermute x16, waiting for transfers between devices, swap(): return lax.ppermute(a, axis, [(0, 1), (1, 0)])  17.2 us
    ppermute x16, starting transfers between devices, swap(): return lax.ppermute(a, axis, [(0, 1), (1, 0)])  13.6 us
    pallas_call x2, Pallas kernels, attention_backward(): pl.pallas_call(kernel, grid=(steps,), in_specs=[rows_of(VIDK), stacked(2,...  11.6 us
    pallas_call x1, Pallas kernels, attention_forward(): pl.pallas_call(forward_kernel, grid=(rows // BLOCK,), in_specs=[SMEM] + [...  10.9 us
    pallas_call x1, Pallas kernels, project(): pl.pallas_call(project_kernel, in_specs=[SMEM, whole(order)] + [pl.BlockS...  7.87 us
    ppermute x5, starting transfers between devices, x_swap(): return lax.ppermute(a, ('cfg', 'xlo'), [(i, 3 - i) for i in range(4)])  6.62 us
  transfers between devices with their start and end apart: 38, of which 18 were waited for; matrix products, arithmetic and copies ran while one was open for 5% of the time, Pallas kernels for 18%

profile of v3, /device:TPU:0, one launch (start us, length us, event | category | flops | bytes accessed | tf_op | source)
XLA Modules:
  0.0 155.2 jit_solution(8887214118418141468)
XLA Ops:
  0.6 3.4 %collective-permute-start.3 = (bf16[24,3072]{1,0:T(8,128)(2,1)}, bf16[24,3072]{1,0:T(8,128)(2,1)S(1)}, u32[]{:S(2)}, u32[]{:S(2)}) collective-permute-start(bf16[24,3072]{1,0:T(8,128)(2,1)} %param.19), channel_id=1, source_target_pairs={{0,16},{8,24},{16,0},{24,8},{1,17},{9,25},{17,1},{25,9},{2,18},{10... | collective-permute-start | bytes 442376 | tf_op jit(solution)/shard_map/ppermute | solution.py:77
  5.7 3.3 %shard_map.137 = (bf16[416,768]{1,0:T(8,128)(2,1)}, bf16[224,768]{1,0:T(8,128)(2,1)}, bf16[224,768]{1,0:T(8,128)(2,1)}, bf16[32,768]{1,0:T(8,128)(2,1)}) custom-call(s32[3]{0:T(128)} %pad_add_fusion.at_ref.refs_0_, bf16[128,3072]{1,0:T(8,128)(2,1)} %bitcast.20, bf16[128,3072]{1,0:T(8,128)(2,1)} %bitcast.23, bf16[128,3072]{1,0:T(8,128)(2,1)} %bitcast.26, ...), custom_call_target="tpu_custom_call" | custom-call | flops 1000000 | bytes 16 | tf_op jit(solution)/shard_map/pallas_call | solution.py:110
  9.0 3.1 %collective-permute-start.1 = (bf16[32,768]{1,0:T(8,128)(2,1)}, bf16[32,768]{1,0:T(8,128)(2,1)S(1)}, u32[]{:S(2)}, u32[]{:S(2)}) collective-permute-start(bf16[32,768]{1,0:T(8,128)(2,1)} %get-tuple-element.116), channel_id=1, source_target_pairs={{0,64},{64,0},{1,65},{65,1},{2,66},{66,2},{3,67},{67,3},{4,68},{68... | collective-permute-start | bytes 147464 | tf_op jit(solution)/shard_map/ppermute | solution.py:65
  15.9 5.9 %collective-permute-done.got1 = bf16[224,768]{1,0:T(8,128)(2,1)S(1)} collective-permute-done((bf16[224,768]{1,0:T(8,128)(2,1)}, bf16[224,768]{1,0:T(8,128)(2,1)S(1)}, u32[]{:S(2)}, u32[]{:S(2)}) %collective-permute-start) | collective-permute-done | bytes 344096 | tf_op jit(solution)/shard_map/ppermute | solution.py:65
  21.8 2.4 %collective-permute-done.5.got3 = bf16[224,768]{1,0:T(8,128)(2,1)S(1)} collective-permute-done((bf16[224,768]{1,0:T(8,128)(2,1)S(1)}, bf16[224,768]{1,0:T(8,128)(2,1)S(1)}, u32[]{:S(2)}, u32[]{:S(2)}) %collective-permute-start.5) | collective-permute-done | bytes 344096 | tf_op jit(solution)/shard_map/ppermute | solution.py:73
  25.4 4.0 %collective-permute-start.11 = (bf16[96,3072]{1,0:T(8,128)(2,1)S(1)}, bf16[96,3072]{1,0:T(8,128)(2,1)}, u32[]{:S(2)}, u32[]{:S(2)}) collective-permute-start(bf16[96,3072]{1,0:T(8,128)(2,1)S(1)} %pad_maximum_fusion.refs_0_), channel_id=1, source_target_pairs={{0,3},{1,2},{2,1},{3,0},{4,7},{5,6},{6,5},{7,4},{8,11},{9,10},{10,... | collective-permute-start | bytes 1769480 | tf_op jit(solution)/shard_map/ppermute | solution.py:77
  31.0 4.3 %all-to-all-start = ((bf16[4,1664,128]{2,1,0:T(8,128)(2,1)}), bf16[4,1664,128]{2,1,0:T(8,128)(2,1)S(1)}, u32[]{:S(2)}, u32[]{:S(2)}) async-start(bf16[4,1664,128]{2,1,0:T(8,128)(2,1)} %shard_map.138), calls=%async_computation | async-start | bytes 3407872 | tf_op jit(solution)/shard_map/all_to_all | solution.py:563
  35.2 5.7 %collective-permute-done.11.refs_4_ = bf16[96,3072]{1,0:T(8,128)(2,1)} collective-permute-done((bf16[96,3072]{1,0:T(8,128)(2,1)S(1)}, bf16[96,3072]{1,0:T(8,128)(2,1)}, u32[]{:S(2)}, u32[]{:S(2)}) %collective-permute-start.11) | collective-permute-done | bytes 589856 | tf_op jit(solution)/shard_map/ppermute | solution.py:77
  49.9 3.0 %collective-permute-start.13 = (bf16[48,3072]{1,0:T(8,128)(2,1)S(1)}, bf16[48,3072]{1,0:T(8,128)(2,1)}, u32[]{:S(2)}, u32[]{:S(2)}) collective-permute-start(bf16[48,3072]{1,0:T(8,128)(2,1)S(1)} %slice.19), channel_id=1, source_target_pairs={{0,3},{1,2},{2,1},{3,0},{4,7},{5,6},{6,5},{7,4},{8,11},{9,10},{10,... | collective-permute-start | bytes 884744 | tf_op jit(solution)/shard_map/ppermute | solution.py:77
  53.0 6.7 %collective-permute-done.13.refs_3_ = bf16[48,3072]{1,0:T(8,128)(2,1)} collective-permute-done((bf16[48,3072]{1,0:T(8,128)(2,1)S(1)}, bf16[48,3072]{1,0:T(8,128)(2,1)}, u32[]{:S(2)}, u32[]{:S(2)}) %collective-permute-start.13) | collective-permute-done | bytes 294944 | tf_op jit(solution)/shard_map/ppermute | solution.py:77
  64.8 7.9 %shard_map.139 = (bf16[768,128]{1,0:T(8,128)(2,1)S(1)}, bf16[768,128]{1,0:T(8,128)(2,1)S(1)}, bf16[768,128]{1,0:T(8,128)(2,1)S(1)}, bf16[768,128]{1,0:T(8,128)(2,1)S(1)}) custom-call(s32[3]{0:T(128)S(1)} %copy-done.3, bf16[768,768]{1,0:T(8,128)(2,1)S(1)} %fusion.order, bf16[96,3072]{1,0:T(8,128)(2,1)S(1)} %pad_maximum_fusion.refs_0_, ...), custom_call_target="tpu_custom_call" | custom-call | flops 1000000 | bytes 16 | tf_op jit(solution)/shard_map/pallas_call | solution.py:202
  73.8 2.9 %collective-permute-start.20 = (bf16[768,128]{1,0:T(8,128)(2,1)S(1)}, bf16[768,128]{1,0:T(8,128)(2,1)S(1)}, u32[]{:S(2)}, u32[]{:S(2)}) collective-permute-start(bf16[768,128]{1,0:T(8,128)(2,1)S(1)} %get-tuple-element.147), channel_id=1, source_target_pairs={{0,16},{8,24},{16,0},{24,8},{1,17},{9,25},{17,1},{25,9},{2,18},{10... | collective-permute-start | bytes 589832 | tf_op jit(solution)/shard_map/ppermute | solution.py:77
  77.5 10.9 %shard_map.140 = (bf16[1536,2048]{1,0:T(8,128)(2,1)S(1)}, bf16[2,1536,256]{2,1,0:T(8,128)(2,1)S(1)}, f32[3,1536,128]{2,1,0:T(8,128)S(1)}, f32[2,1536,128]{2,1,0:...) custom-call(s32[3]{0:T(128)S(1)} %copy-done.3, ...), custom_call_target="tpu_custom_call" | custom-call | flops 1000000 | bytes 16 | tf_op jit(solution)/shard_map/pallas_call | solution.py:276
  88.7 7.6 %shard_map.141 = (bf16[4,640,128]{2,1,0:T(8,128)(2,1)S(1)}, bf16[4,640,128]{2,1,0:T(8,128)(2,1)S(1)}, bf16[256,128]{1,0:T(8,128)(2,1)S(1)}, bf16[256,128]{1,0:T(...) custom-call(bf16[1536,2048]{1,0:T(8,128)(2,1)S(1)} %get-tuple-element.158.refs_0_, ...), custom_call_target="tpu_custom_call" | custom-call | flops 1000000 | bytes 16 | tf_op jit(solution)/shard_map/pallas_call | solution.py:403
  96.4 4.0 %shard_map.142 = (bf16[4,640,128]{2,1,0:T(8,128)(2,1)S(1)}, bf16[4,640,128]{2,1,0:T(8,128)(2,1)S(1)}, bf16[128,128]{1,0:T(8,128)(2,1)S(1)}, bf16[128,128]{1,0:T(...) custom-call(bf16[1536,2048]{1,0:T(8,128)(2,1)S(1)} %get-tuple-element.158.refs_0_, ...), custom_call_target="tpu_custom_call" | custom-call | flops 1000000 | bytes 16 | tf_op jit(solution)/shard_map/pallas_call | solution.py:403
  101.2 3.7 %collective-permute-start.26 = (bf16[896,128]{1,0:T(8,128)(2,1)S(1)}, bf16[896,128]{1,0:T(8,128)(2,1)S(1)}, u32[]{:S(2)}, u32[]{:S(2)}) collective-permute-start(bf16[896,128]{1,0:T(8,128)(2,1)S(1)} %get-tuple-element.194), channel_id=1, source_target_pairs={{0,16},{8,24},{16,0},{24,8},{1,17},{9,25},{17,1},{25,9},{2,18},{10... | collective-permute-start | bytes 688136 | tf_op jit(solution)/shard_map/ppermute | solution.py:77
  106.0 3.6 %collective-permute-done.25.refs_2_ = bf16[896,128]{1,0:T(8,128)(2,1)S(1)} collective-permute-done((bf16[896,128]{1,0:T(8,128)(2,1)S(1)}, bf16[896,128]{1,0:T(8,128)(2,1)S(1)}, u32[]{:S(2)}, u32[]{:S(2)}) %collective-permute-start.25) | collective-permute-done | bytes 229408 | tf_op jit(solution)/shard_map/ppermute | solution.py:77
  109.6 5.8 %collective-permute-done.26.refs_3_ = bf16[896,128]{1,0:T(8,128)(2,1)S(1)} collective-permute-done((bf16[896,128]{1,0:T(8,128)(2,1)S(1)}, bf16[896,128]{1,0:T(8,128)(2,1)S(1)}, u32[]{:S(2)}, u32[]{:S(2)}) %collective-permute-start.26) | collective-permute-done | bytes 229408 | tf_op jit(solution)/shard_map/ppermute | solution.py:77
  115.4 2.6 %collective-permute-done.27.refs_4_ = bf16[896,128]{1,0:T(8,128)(2,1)S(1)} collective-permute-done((bf16[896,128]{1,0:T(8,128)(2,1)S(1)}, bf16[896,128]{1,0:T(8,128)(2,1)S(1)}, u32[]{:S(2)}, u32[]{:S(2)}) %collective-permute-start.27) | collective-permute-done | bytes 229408 | tf_op jit(solution)/shard_map/ppermute | solution.py:77
  126.0 3.0 %collective-permute-done.28.refs_2_ = bf16[768,128]{1,0:T(8,128)(2,1)S(1)} collective-permute-done((bf16[768,128]{1,0:T(8,128)(2,1)S(1)}, bf16[768,128]{1,0:T(8,128)(2,1)S(1)}, u32[]{:S(2)}, u32[]{:S(2)}) %collective-permute-start.28) | collective-permute-done | bytes 196640 | tf_op jit(solution)/shard_map/ppermute | solution.py:77
  131.9 4.0 %collective-permute-done.30.refs_4_ = bf16[768,128]{1,0:T(8,128)(2,1)S(1)} collective-permute-done((bf16[768,128]{1,0:T(8,128)(2,1)S(1)}, bf16[768,128]{1,0:T(8,128)(2,1)S(1)}, u32[]{:S(2)}, u32[]{:S(2)}) %collective-permute-start.30) | collective-permute-done | bytes 196640 | tf_op jit(solution)/shard_map/ppermute | solution.py:77
  135.9 3.7 %collective-permute-done.32.refs_2_ = bf16[416,512]{1,0:T(8,128)(2,1)S(1)} collective-permute-done((bf16[416,512]{1,0:T(8,128)(2,1)S(1)}, bf16[416,512]{1,0:T(8,128)(2,1)S(1)}, u32[]{:S(2)}, u32[]{:S(2)}) %collective-permute-start.32) | collective-permute-done | bytes 426016 | tf_op jit(solution)/shard_map/ppermute | solution.py:65
  140.3 3.0 %collective-permute-start.35 = (bf16[416,256]{1,0:T(8,128)(2,1)S(1)}, bf16[416,256]{1,0:T(8,128)(2,1)S(1)}, u32[]{:S(2)}, u32[]{:S(2)}) collective-permute-start(bf16[416,256]{1,0:T(8,128)(2,1)S(1)} %get-tuple-element.216), channel_id=1, source_target_pairs={{0,64},{64,0},{1,65},{65,1},{2,66},{66,2},{3,67},{67,3},{4,68},{68... | collective-permute-start | bytes 638984 | tf_op jit(solution)/shard_map/ppermute | solution.py:65
  147.4 3.4 %collective-permute-done.35.refs_6_ = bf16[416,256]{1,0:T(8,128)(2,1)S(1)} collective-permute-done((bf16[416,256]{1,0:T(8,128)(2,1)S(1)}, bf16[416,256]{1,0:T(8,128)(2,1)S(1)}, u32[]{:S(2)}, u32[]{:S(2)}) %collective-permute-start.35) | collective-permute-done | bytes 213024 | tf_op jit(solution)/shard_map/ppermute | solution.py:65
  (105 shorter events, 45.8 us)
Async XLA Ops:
  0.6 12.9 %collective-permute-start.3 = (bf16[24,3072]{1,0:T(8,128)(2,1)}, bf16[24,3072]{1,0:T(8,128)(2,1)S(1)}, u32[]{:S(2)}, u32[]{:S(2)}) collective-permute-start(bf16[24,3072]{1,0:T(8,128)(2,1)} %param.19), channel_id=1, source_target_pairs={{0,16},{8,24},{16,0},{24,8},{1,17},{9,25},{17,1},{25,9},{2,18},{10... | collective-permute-start | bytes 442376 | tf_op jit(solution)/shard_map/ppermute | solution.py:77
  4.0 10.9 %collective-permute-start.2 = (bf16[24,3072]{1,0:T(8,128)(2,1)}, bf16[24,3072]{1,0:T(8,128)(2,1)S(1)}, u32[]{:S(2)}, u32[]{:S(2)}) collective-permute-start(bf16[24,3072]{1,0:T(8,128)(2,1)} %param.19), channel_id=1, source_target_pairs={{0,8},{8,0},{16,24},{24,16},{1,9},{9,1},{17,25},{25,17},{2,10},{10... | collective-permute-start | bytes 442376 | tf_op jit(solution)/shard_map/ppermute | solution.py:77
  4.7 10.2 %collective-permute-start.4 = (bf16[24,3072]{1,0:T(8,128)(2,1)}, bf16[24,3072]{1,0:T(8,128)(2,1)}, u32[]{:S(2)}, u32[]{:S(2)}) collective-permute-start(bf16[24,3072]{1,0:T(8,128)(2,1)} %param.19), channel_id=1, source_target_pairs={{0,24},{8,16},{16,8},{24,0},{1,25},{9,17},{17,9},{25,1},{2,26},{10... | collective-permute-start | bytes 442376 | tf_op jit(solution)/shard_map/ppermute | solution.py:77
  14.3 9.9 %collective-permute-start.5 = (bf16[224,768]{1,0:T(8,128)(2,1)S(1)}, bf16[224,768]{1,0:T(8,128)(2,1)S(1)}, u32[]{:S(2)}, u32[]{:S(2)}) collective-permute-start(bf16[224,768]{1,0:T(8,128)(2,1)S(1)} %copy-done.8), channel_id=1, source_target_pairs={{0,96},{32,64},{64,32},{96,0},{1,97},{33,65},{65,33},{97,1},{2,98}... | collective-permute-start | bytes 1032200 | tf_op jit(solution)/shard_map/ppermute | solution.py:73
  24.2 18.6 %collective-permute-start.8 = (bf16[128,3072]{1,0:T(8,128)(2,1)S(1)}, bf16[128,3072]{1,0:T(8,128)(2,1)}, u32[]{:S(2)}, u32[]{:S(2)}) collective-permute-start(bf16[128,3072]{1,0:T(8,128)(2,1)S(1)} %fusion.1.refs_10_), channel_id=1, source_target_pairs={{0,96},{32,64},{64,32},{96,0},{1,97},{33,65},{65,33},{97,1},{2,98}... | collective-permute-start | bytes 2359304 | tf_op jit(solution)/shard_map/ppermute | solution.py:73
  25.3 19.0 %collective-permute-start.7 = (bf16[128,3072]{1,0:T(8,128)(2,1)S(1)}, bf16[128,3072]{1,0:T(8,128)(2,1)}, u32[]{:S(2)}, u32[]{:S(2)}) collective-permute-start(bf16[128,3072]{1,0:T(8,128)(2,1)S(1)} %fusion.1.refs_10_), channel_id=1, source_target_pairs={{0,32},{32,0},{1,33},{33,1},{2,34},{34,2},{3,35},{35,3},{4,36},{36... | collective-permute-start | bytes 2359304 | tf_op jit(solution)/shard_map/ppermute | solution.py:65
  25.4 15.5 %collective-permute-start.11 = (bf16[96,3072]{1,0:T(8,128)(2,1)S(1)}, bf16[96,3072]{1,0:T(8,128)(2,1)}, u32[]{:S(2)}, u32[]{:S(2)}) collective-permute-start(bf16[96,3072]{1,0:T(8,128)(2,1)S(1)} %pad_maximum_fusion.refs_0_), channel_id=1, source_target_pairs={{0,3},{1,2},{2,1},{3,0},{4,7},{5,6},{6,5},{7,4},{8,11},{9,10},{10,... | collective-permute-start | bytes 1769480 | tf_op jit(solution)/shard_map/ppermute | solution.py:77
  29.4 13.1 %collective-permute-start.6 = (bf16[96,3072]{1,0:T(8,128)(2,1)S(1)}, bf16[96,3072]{1,0:T(8,128)(2,1)}, u32[]{:S(2)}, u32[]{:S(2)}) collective-permute-start(bf16[96,3072]{1,0:T(8,128)(2,1)S(1)} %pad_maximum_fusion.refs_0_), channel_id=1, source_target_pairs={{0,1},{1,0},{2,3},{3,2},{4,5},{5,4},{6,7},{7,6},{8,9},{9,8},{10,11... | collective-permute-start | bytes 1769480 | tf_op jit(solution)/shard_map/ppermute | solution.py:77
  29.5 17.6 %collective-permute-start.14 = (bf16[96,3072]{1,0:T(8,128)(2,1)S(1)}, bf16[96,3072]{1,0:T(8,128)(2,1)}, u32[]{:S(2)}, u32[]{:S(2)}) collective-permute-start(bf16[96,3072]{1,0:T(8,128)(2,1)S(1)} %pad_maximum_fusion.refs_0_), channel_id=1, source_target_pairs={{0,4},{4,0},{1,5},{5,1},{2,6},{6,2},{3,7},{7,3},{8,12},{12,8},{9,1... | collective-permute-start | bytes 1769480 | tf_op jit(solution)/shard_map/ppermute | solution.py:65
  31.0 30.1 %all-to-all-start = ((bf16[4,1664,128]{2,1,0:T(8,128)(2,1)}), bf16[4,1664,128]{2,1,0:T(8,128)(2,1)S(1)}, u32[]{:S(2)}, u32[]{:S(2)}) async-start(bf16[4,1664,128]{2,1,0:T(8,128)(2,1)} %shard_map.138), calls=%async_computation | async-start | bytes 3407872 | tf_op jit(solution)/shard_map/all_to_all | solution.py:563
  42.6 17.9 %collective-permute-start.16 = (bf16[96,3072]{1,0:T(8,128)(2,1)}, bf16[96,3072]{1,0:T(8,128)(2,1)}, u32[]{:S(2)}, u32[]{:S(2)}) collective-permute-start(bf16[96,3072]{1,0:T(8,128)(2,1)} %collective-permute-done.11.refs_4_), channel_id=1, source_target_pairs={{0,4},{4,0},{1,5},{5,1},{2,6},{6,2},{3,7},{7,3},{8,12},{12,8},{9,1... | collective-permute-start | bytes 1769480 | tf_op jit(solution)/shard_map/ppermute | solution.py:65
  42.8 17.7 %collective-permute-start.15 = (bf16[96,3072]{1,0:T(8,128)(2,1)}, bf16[96,3072]{1,0:T(8,128)(2,1)}, u32[]{:S(2)}, u32[]{:S(2)}) collective-permute-start(bf16[96,3072]{1,0:T(8,128)(2,1)} %collective-permute-done.6.refs_1_), channel_id=1, source_target_pairs={{0,4},{4,0},{1,5},{5,1},{2,6},{6,2},{3,7},{7,3},{8,12},{12,8},{9,1... | collective-permute-start | bytes 1769480 | tf_op jit(solution)/shard_map/ppermute | solution.py:65
  44.2 15.5 %collective-permute-start.9 = (bf16[64,3072]{1,0:T(8,128)(2,1)S(1)}, bf16[64,3072]{1,0:T(8,128)(2,1)S(1)}, u32[]{:S(2)}, u32[]{:S(2)}) collective-permute-start(bf16[64,3072]{1,0:T(8,128)(2,1)S(1)} %slice.16), channel_id=1, source_target_pairs={{0,32},{32,0},{1,33},{33,1},{2,34},{34,2},{3,35},{35,3},{4,36},{36... | collective-permute-start | bytes 1179656 | tf_op jit(solution)/shard_map/ppermute | solution.py:65
  47.1 12.7 %collective-permute-start.10 = (bf16[64,3072]{1,0:T(8,128)(2,1)S(1)}, bf16[64,3072]{1,0:T(8,128)(2,1)S(1)}, u32[]{:S(2)}, u32[]{:S(2)}) collective-permute-start(bf16[64,3072]{1,0:T(8,128)(2,1)S(1)} %slice.17), channel_id=1, source_target_pairs={{0,96},{32,64},{64,32},{96,0},{1,97},{33,65},{65,33},{97,1},{2,98}... | collective-permute-start | bytes 1179656 | tf_op jit(solution)/shard_map/ppermute | solution.py:73
  62.9 14.7 %collective-permute-start.22 = (bf16[4,1664,128]{2,1,0:T(8,128)(2,1)S(1)}, bf16[4,1664,128]{2,1,0:T(8,128)(2,1)}, u32[]{:S(2)}, u32[]{:S(2)}) collective-permute-start(bf16[4,1664,128]{2,1,0:T(8,128)(2,1)S(1)} %all-to-all-done.own), channel_id=1, source_target_pairs={{0,4},{4,0},{1,5},{5,1},{2,6},{6,2},{3,7},{7,3},{8,12},{12,8},{9,1... | collective-permute-start | bytes 5111816 | tf_op jit(solution)/shard_map/ppermute | solution.py:65
  72.7 15.8 %collective-permute-start.19 = (bf16[768,128]{1,0:T(8,128)(2,1)S(1)}, bf16[768,128]{1,0:T(8,128)(2,1)S(1)}, u32[]{:S(2)}, u32[]{:S(2)}) collective-permute-start(bf16[768,128]{1,0:T(8,128)(2,1)S(1)} %get-tuple-element.146), channel_id=1, source_target_pairs={{0,8},{8,0},{16,24},{24,16},{1,9},{9,1},{17,25},{25,17},{2,10},{10... | collective-permute-start | bytes 589832 | tf_op jit(solution)/shard_map/ppermute | solution.py:77
  73.8 14.7 %collective-permute-start.20 = (bf16[768,128]{1,0:T(8,128)(2,1)S(1)}, bf16[768,128]{1,0:T(8,128)(2,1)S(1)}, u32[]{:S(2)}, u32[]{:S(2)}) collective-permute-start(bf16[768,128]{1,0:T(8,128)(2,1)S(1)} %get-tuple-element.147), channel_id=1, source_target_pairs={{0,16},{8,24},{16,0},{24,8},{1,17},{9,25},{17,1},{25,9},{2,18},{10... | collective-permute-start | bytes 589832 | tf_op jit(solution)/shard_map/ppermute | solution.py:77
  76.7 12.0 %collective-permute-start.21 = (bf16[768,128]{1,0:T(8,128)(2,1)S(1)}, bf16[768,128]{1,0:T(8,128)(2,1)S(1)}, u32[]{:S(2)}, u32[]{:S(2)}) collective-permute-start(bf16[768,128]{1,0:T(8,128)(2,1)S(1)} %get-tuple-element.148), channel_id=1, source_target_pairs={{0,24},{8,16},{16,8},{24,0},{1,25},{9,17},{17,9},{25,1},{2,26},{10... | collective-permute-start | bytes 589832 | tf_op jit(solution)/shard_map/ppermute | solution.py:77
  101.2 14.3 %collective-permute-start.26 = (bf16[896,128]{1,0:T(8,128)(2,1)S(1)}, bf16[896,128]{1,0:T(8,128)(2,1)S(1)}, u32[]{:S(2)}, u32[]{:S(2)}) collective-permute-start(bf16[896,128]{1,0:T(8,128)(2,1)S(1)} %get-tuple-element.194), channel_id=1, source_target_pairs={{0,16},{8,24},{16,0},{24,8},{1,17},{9,25},{17,1},{25,9},{2,18},{10... | collective-permute-start | bytes 688136 | tf_op jit(solution)/shard_map/ppermute | solution.py:77
  104.9 13.1 %collective-permute-start.27 = (bf16[896,128]{1,0:T(8,128)(2,1)S(1)}, bf16[896,128]{1,0:T(8,128)(2,1)S(1)}, u32[]{:S(2)}, u32[]{:S(2)}) collective-permute-start(bf16[896,128]{1,0:T(8,128)(2,1)S(1)} %get-tuple-element.195), channel_id=1, source_target_pairs={{0,24},{8,16},{16,8},{24,0},{1,25},{9,17},{17,9},{25,1},{2,26},{10... | collective-permute-start | bytes 688136 | tf_op jit(solution)/shard_map/ppermute | solution.py:77
  118.8 17.1 %collective-permute-start.31 = (bf16[416,512]{1,0:T(8,128)(2,1)S(1)}, bf16[416,512]{1,0:T(8,128)(2,1)S(1)}, u32[]{:S(2)}, u32[]{:S(2)}) collective-permute-start(bf16[416,512]{1,0:T(8,128)(2,1)S(1)} %get-tuple-element.205), channel_id=1, source_target_pairs={{0,32},{32,0},{1,33},{33,1},{2,34},{34,2},{3,35},{35,3},{4,36},{36... | collective-permute-start | bytes 1277960 | tf_op jit(solution)/shard_map/ppermute | solution.py:65
  119.7 19.9 %collective-permute-start.32 = (bf16[416,512]{1,0:T(8,128)(2,1)S(1)}, bf16[416,512]{1,0:T(8,128)(2,1)S(1)}, u32[]{:S(2)}, u32[]{:S(2)}) collective-permute-start(bf16[416,512]{1,0:T(8,128)(2,1)S(1)} %get-tuple-element.206), channel_id=1, source_target_pairs={{0,64},{64,0},{1,65},{65,1},{2,66},{66,2},{3,67},{67,3},{4,68},{68... | collective-permute-start | bytes 1277960 | tf_op jit(solution)/shard_map/ppermute | solution.py:65
  122.0 23.0 %collective-permute-start.33 = (bf16[416,512]{1,0:T(8,128)(2,1)S(1)}, bf16[416,512]{1,0:T(8,128)(2,1)S(1)}, u32[]{:S(2)}, u32[]{:S(2)}) collective-permute-start(bf16[416,512]{1,0:T(8,128)(2,1)S(1)} %get-tuple-element.209), channel_id=1, source_target_pairs={{0,96},{32,64},{64,32},{96,0},{1,97},{33,65},{65,33},{97,1},{2,98}... | collective-permute-start | bytes 1277960 | tf_op jit(solution)/shard_map/ppermute | solution.py:73
  140.3 10.5 %collective-permute-start.35 = (bf16[416,256]{1,0:T(8,128)(2,1)S(1)}, bf16[416,256]{1,0:T(8,128)(2,1)S(1)}, u32[]{:S(2)}, u32[]{:S(2)}) collective-permute-start(bf16[416,256]{1,0:T(8,128)(2,1)S(1)} %get-tuple-element.216), channel_id=1, source_target_pairs={{0,64},{64,0},{1,65},{65,1},{2,66},{66,2},{3,67},{67,3},{4,68},{68... | collective-permute-start | bytes 638984 | tf_op jit(solution)/shard_map/ppermute | solution.py:65
  (23 other events, 172.3 us)

commit v4 on v3

--- a/solution.py
+++ b/solution.py
@@ -17,7 +17,8 @@
 EXP2 = SCALE * math.log2(math.e)
 VIDK = 2048
 TXTK = 256
-BLOCK = 256
+BLOCK = 512
+BACK = 512
 
 NT = ((1,), (1,))
 NN = ((1,), (0,))
@@ -171,19 +172,31 @@
 def project_kernel(at_ref, order, *refs):
     y = at_ref[1]
     w_refs, a_refs, outs = refs[:10], refs[10:15], refs[15:19]
-    w_all, a_all, out, sems = refs[19:]
-    copies = []
-    for refs, whole_ref in ((w_refs, w_all), (a_refs, a_all)):
-        row = 0
-        for ref in refs:
-            copies.append((ref, whole_ref.at[pl.ds(row, ref.shape[0])]))
-            row += ref.shape[0]
-    started = [pltpu.make_async_copy(src, dst, sems.at[i]) for i, (src, dst) in enumerate(copies)]
-    for copy in started:
-        copy.start()
-    for copy in started:
-        copy.wait()
-    product = dot(a_all[...], w_all[...], NT).astype(jnp.bfloat16)
+    w_all, a_all, out, total, sems = refs[19:]
+    chunks = sems.shape[0]
+    width = w_all.shape[1] // chunks
+    started = []
+    for j in range(chunks):
+        cols = slice(j * width, (j + 1) * width)
+        count = 0
+        for refs, whole_ref in ((w_refs, w_all), (a_refs, a_all)):
+            row = 0
+            for ref in refs:
+                rows = slice(row, row + ref.shape[0])
+                copy = pltpu.make_async_copy(
+                    ref.at[:, cols], whole_ref.at[rows, cols], sems.at[j, count]
+                )
+                copy.start()
+                started.append(copy)
+                row += ref.shape[0]
+                count += 1
+    for j in range(chunks):
+        cols = slice(j * width, (j + 1) * width)
+        for copy in started[j * count : (j + 1) * count]:
+            copy.wait()
+        term = dot(a_all[:, cols], w_all[:, cols], NT)
+        total[...] = term if j == 0 else total[...] + term
+    product = total[...].astype(jnp.bfloat16)
     out[...] = dot(product, order[...], NN).astype(jnp.bfloat16)
     quarter = TOK // 4
     for r in range(4):
@@ -208,7 +221,8 @@
             pltpu.VMEM((XW, width), jnp.bfloat16),
             pltpu.VMEM((rows, width), jnp.bfloat16),
             pltpu.VMEM((rows, XW), jnp.bfloat16),
-            pltpu.SemaphoreType.DMA((15,)),
+            pltpu.VMEM((rows, XW), jnp.float32),
+            pltpu.SemaphoreType.DMA((4, 15)),
         ],
         compiler_params=params(20),
         cost_estimate=COST,
@@ -239,7 +253,7 @@
             q_all[r * 2 * TOK : (r + 1) * 2 * TOK] = msgs[r][Q_A : Q_A + 2 * TOK]
             q_all[8 * TOK + r * TOK : 8 * TOK + (r + 1) * TOK] = msgs[r][Q_B : Q_B + TOK]
 
-    head = step // 4
+    head = step * BLOCK // (8 * TOK)
     q = q_all[pl.ds(pl.multiple_of(step * BLOCK, BLOCK), BLOCK)]
     q_ref[...] = q
     s = dot(q, k_all[head, :VIDK], NT)
@@ -296,7 +310,7 @@
             bf16(rows, HD),
         ],
         scratch_shapes=[pltpu.VMEM((rows, HD), jnp.bfloat16)],
-        compiler_params=params(24),
+        compiler_params=params(32),
         cost_estimate=COST,
     )(at, *arrays)
 
@@ -311,7 +325,7 @@
     ds_all, dk_acc, dv_acc = refs[2 + parts :]
     step = pl.program_id(0)
     last = pl.num_programs(0) - 1
-    per_step = BLOCK // count
+    per_step = BACK // count
     run = 2 * TT
 
     @pl.when(step == 0)
@@ -331,7 +345,7 @@
     q = q_ref[...]
     v_video = v_ref[:VIDK]
     g = jnp.zeros(q.shape, jnp.float32)
-    delta = jnp.zeros((BLOCK, 1), jnp.float32)
+    delta = jnp.zeros((BACK, 1), jnp.float32)
     for p in range(2):
         text = slice(VIDK + p * TXTK, VIDK + (p + 1) * TXTK)
         do = adjoint(p)
@@ -343,15 +357,15 @@
         pt = p_ref[p]
         ds_text = pt.astype(jnp.float32) * (dot(do, v_ref[text], NT) - row_delta)
         ds_all[:, text] = ds_text.astype(jnp.bfloat16)
-        dv_acc[text] += dot(pt, do, TN)
+        dv_acc[:, text] += dot(do, pt, TN)
     gb = g.astype(jnp.bfloat16)
     delta = delta + jnp.sum((gb.astype(jnp.float32) - g) * o_ref[2], axis=1, keepdims=True)
     e = e_ref[...]
     ds_video = e.astype(jnp.float32) * (dot(gb, v_video, NT) - delta)
     ds_all[:, :VIDK] = ds_video.astype(jnp.bfloat16)
-    dv_acc[:VIDK] += dot(e, gb, TN)
+    dv_acc[:, :VIDK] += dot(gb, e, TN)
     ds = ds_all[...]
-    dk_acc[...] += dot(ds, q, TN)
+    dk_acc[...] += dot(q, ds, TN)
     dq = (dot(ds, k_ref[...], NN) * SCALE).astype(jnp.bfloat16)
     for r in range(parts):
 
@@ -366,15 +380,17 @@
             out0[...] = dk_acc[...]
             out1[...] = dv_acc[...]
             return
+        dk = (dk_acc[...] * SCALE).T
+        dv = dv_acc[...].T
         for i in range(8):
             out = (out0, out1)[i // 4].at[i % 4]
-            for j, acc, factor in ((0, dk_acc, SCALE), (1, dv_acc, 1.0)):
-                video = acc[i * 2 * TOK : (i + 1) * 2 * TOK] * factor
+            for j, acc in ((0, dk), (1, dv)):
+                video = acc[i * 2 * TOK : (i + 1) * 2 * TOK]
                 out[j * 2 * TOK : (j + 1) * 2 * TOK] = video.astype(jnp.bfloat16)
                 for p in range(2):
                     src = VIDK + p * TXTK + i * run
                     dst = 4 * TOK + j * 2 * run + p * run
-                    out[dst : dst + run] = (acc[src : src + run] * factor).astype(jnp.bfloat16)
+                    out[dst : dst + run] = acc[src : src + run].astype(jnp.bfloat16)
 
 
 def attention_backward(stored, dos, shared, start=0, sums=None, final=True):
@@ -382,9 +398,9 @@
     parts = len(dos)
     count = TOK if shared else 2 * TOK
     do_at = 4 * TOK if shared else 0
-    steps = parts * count // BLOCK
+    steps = parts * count // BACK
     head = 1 if shared else 0
-    skip = (8 * TOK if shared else 0) // BLOCK + start * count // BLOCK
+    skip = (8 * TOK if shared else 0) // BACK + start * count // BACK
     keys = VIDK + 2 * TXTK
     shape = (parts, sums is None, final, count, do_at)
 
@@ -392,10 +408,10 @@
         backward_kernel(shape, *refs)
 
     def stacked(depth, width):
-        return pl.BlockSpec((depth, BLOCK, width), lambda i: (0, i + skip, 0))
+        return pl.BlockSpec((depth, BACK, width), lambda i: (0, i + skip, 0))
 
     def rows_of(width):
-        return pl.BlockSpec((BLOCK, width), lambda i: (i + skip, 0))
+        return pl.BlockSpec((BACK, width), lambda i: (i + skip, 0))
 
     keys_of = pl.BlockSpec((None, keys, HD), lambda i: (head, 0, 0))
     sum_shape = jax.ShapeDtypeStruct((keys, HD), jnp.float32)
@@ -410,11 +426,11 @@
         out_shape=([bf16(4, BACK_KV, HD)] * 2 if final else [sum_shape] * 2)
         + [bf16(count, HD)] * parts,
         scratch_shapes=[
-            pltpu.VMEM((BLOCK, keys), jnp.bfloat16),
-            pltpu.VMEM((keys, HD), jnp.float32),
-            pltpu.VMEM((keys, HD), jnp.float32),
+            pltpu.VMEM((BACK, keys), jnp.bfloat16),
+            pltpu.VMEM((HD, keys), jnp.float32),
+            pltpu.VMEM((HD, keys), jnp.float32),
         ],
-        compiler_params=params(18),
+        compiler_params=params(26),
         cost_estimate=COST,
     )(e, p, o, w, q, k, v, *dos, *sums)
     return results[0], results[1], results[2:]
@@ -545,7 +561,8 @@
     own, to1, to3, to2 = cut_x(at, q_video[0], k_video[0], v_video[0], k_text[0, 0], v_text[0, 0])
     got1, got2, got3 = x_swap(to1, 1), x_swap(to2, 2), x_swap(to3, 3)
     got2, w_y = lax.optimization_barrier((got2, jnp.concatenate(w_y, axis=0)))
-    got1, w_y = lax.optimization_barrier((got1, w_y))
+    w_y_swapped = swap(w_y, "core")
+    got1, w_y_swapped = lax.optimization_barrier((got1, w_y_swapped))
     w_z1, w_z3 = ring_swap(w_y, "fsdp", 1), ring_swap(w_y, "fsdp", 3)
     half = WROWS // 2
     w_z2 = [ring_swap(w_z3[:half], "fsdp", 1), ring_swap(w_z1[half:], "fsdp", 3)]
@@ -561,7 +578,7 @@
     adjoints = [scaled, scaled1, x_swap(scaled3[:half], 1), x_swap(scaled1[half:], 3), scaled3]
     messages = cut_y(own, got1, got2, got3)
     arrived = lax.all_to_all(messages, "y", split_axis=0, concat_axis=0, tiled=True)
-    w_swapped = [swap(piece, "core") for piece in (w_y, w_z1, w_z3)]
+    w_swapped = [w_y_swapped, swap(w_z1, "core"), swap(w_z3, "core")]
     adjoints, w_z2, w_swapped = lax.optimization_barrier((adjoints, w_z2, w_swapped))
     w_z2_swapped = [swap(piece, "core") for piece in w_z2]
     weights = [w_y, w_z1] + w_z2 + [w_z3] + w_swapped[:2] + w_z2_swapped + w_swapped[2:]
@@ -599,7 +616,7 @@
     total_b, got_a = lax.optimization_barrier((total_b, got_a))
     parts_a = x_back(merge_y(at, got_a, False))
     got_b = y_back(total_b)
-    got_b, parts_a[1], parts_a[2] = lax.optimization_barrier((got_b, parts_a[1], parts_a[2]))
+    got_b, parts_a[1] = lax.optimization_barrier((got_b, parts_a[1]))
     parts_b = x_back(merge_y(at, got_b, True))
     dq, dk, dv, dkt, dvt = merge_x(at, parts_a, parts_b)
     return dq[None], dk[None], dv[None], dkt[None, None], dvt[None, None]

time: 156 us -> 152 us (0.974)
  Pallas kernels: 39.1 us -> 36.6 us
  waiting for transfers between devices: 55.3 us -> 53.1 us
    ppermute x16, waiting for transfers between devices: 17.2 us -> 14.2 us  [swap(): return lax.ppermute(a, axis, [(0, 1), (1, 0)])]
    ppermute x5, waiting for transfers between devices: 4.79 us -> 7.69 us  [x_swap(): return lax.ppermute(a, ('cfg', 'xlo'), [(i, 3 - i) for i in range(4)])]
    ppermute x16, waiting for transfers between devices: 33.3 us -> 31.3 us  [ring_swap(): return lax.ppermute(a, axis, [(i, i ^ r) for i in range(4)])]
  transfers between devices with their start and end apart: 38 -> 38, of which waited for: 18 -> 19; matrix products, arithmetic and copies ran while one was open for 5% -> 5% of each run, Pallas kernels for 18% -> 17%
where the time goes in v4:
time: 152 us; the launch traced here: 151 us
  waiting for transfers between devices  53.1 us (35%)
  starting transfers between devices  49.9 us (33%)
  Pallas kernels  36.6 us (24%)
  local copies, waits for them, and re-layouts  7.53 us (5%)
  other arithmetic  2.78 us (2%)
  between operations  1.53 us (1%)
    ppermute x16, waiting for transfers between devices, ring_swap(): return lax.ppermute(a, axis, [(i, i ^ r) for i in range(4)])  31.3 us
    ppermute x16, starting transfers between devices, ring_swap(): return lax.ppermute(a, axis, [(i, i ^ r) for i in range(4)])  25.7 us
    ppermute x16, starting transfers between devices, swap(): return lax.ppermute(a, axis, [(0, 1), (1, 0)])  14.3 us
    ppermute x16, waiting for transfers between devices, swap(): return lax.ppermute(a, axis, [(0, 1), (1, 0)])  14.2 us
    pallas_call x2, Pallas kernels, attention_backward(): pl.pallas_call(kernel, grid=(steps,), in_specs=[rows_of(VIDK), stacked(2,...  10.6 us
    pallas_call x1, Pallas kernels, attention_forward(): pl.pallas_call(forward_kernel, grid=(rows // BLOCK,), in_specs=[SMEM] + [...  10.1 us
    ppermute x5, waiting for transfers between devices, x_swap(): return lax.ppermute(a, ('cfg', 'xlo'), [(i, 3 - i) for i in range(4)])  7.69 us
    pallas_call x1, Pallas kernels, project(): pl.pallas_call(project_kernel, in_specs=[SMEM, whole(order)] + [pl.BlockS...  7.12 us
  transfers between devices with their start and end apart: 38, of which 19 were waited for; matrix products, arithmetic and copies ran while one was open for 5% of the time, Pallas kernels for 17%

profile of v4, /device:TPU:0, one launch (start us, length us, event | category | flops | bytes accessed | tf_op | source)
XLA Modules:
  0.0 151.4 jit_solution(13262418631611758953)
XLA Ops:
  0.6 3.4 %collective-permute-start.3 = (bf16[24,3072]{1,0:T(8,128)(2,1)}, bf16[24,3072]{1,0:T(8,128)(2,1)S(1)}, u32[]{:S(2)}, u32[]{:S(2)}) collective-permute-start(bf16[24,3072]{1,0:T(8,128)(2,1)} %param.19), channel_id=1, source_target_pairs={{0,16},{8,24},{16,0},{24,8},{1,17},{9,25},{17,1},{25,9},{2,18},{10... | collective-permute-start | bytes 442376 | tf_op jit(solution)/shard_map/ppermute | solution.py:78
  5.7 3.3 %shard_map.137 = (bf16[416,768]{1,0:T(8,128)(2,1)}, bf16[224,768]{1,0:T(8,128)(2,1)}, bf16[224,768]{1,0:T(8,128)(2,1)}, bf16[32,768]{1,0:T(8,128)(2,1)}) custom-call(s32[3]{0:T(128)} %pad_add_fusion.at_ref.refs_0_, bf16[128,3072]{1,0:T(8,128)(2,1)} %bitcast.20, bf16[128,3072]{1,0:T(8,128)(2,1)} %bitcast.23, bf16[128,3072]{1,0:T(8,128)(2,1)} %bitcast.26, ...), custom_call_target="tpu_custom_call" | custom-call | flops 1000000 | bytes 16 | tf_op jit(solution)/shard_map/pallas_call | solution.py:111
  9.0 3.1 %collective-permute-start.1 = (bf16[32,768]{1,0:T(8,128)(2,1)}, bf16[32,768]{1,0:T(8,128)(2,1)S(1)}, u32[]{:S(2)}, u32[]{:S(2)}) collective-permute-start(bf16[32,768]{1,0:T(8,128)(2,1)} %get-tuple-element.115), channel_id=1, source_target_pairs={{0,64},{64,0},{1,65},{65,1},{2,66},{66,2},{3,67},{67,3},{4,68},{68... | collective-permute-start | bytes 147464 | tf_op jit(solution)/shard_map/ppermute | solution.py:66
  16.6 5.2 %collective-permute-done.got1 = bf16[224,768]{1,0:T(8,128)(2,1)S(1)} collective-permute-done((bf16[224,768]{1,0:T(8,128)(2,1)}, bf16[224,768]{1,0:T(8,128)(2,1)S(1)}, u32[]{:S(2)}, u32[]{:S(2)}) %collective-permute-start) | collective-permute-done | bytes 344096 | tf_op jit(solution)/shard_map/ppermute | solution.py:66
  24.9 4.0 %collective-permute-start.12 = (bf16[96,3072]{1,0:T(8,128)(2,1)S(1)}, bf16[96,3072]{1,0:T(8,128)(2,1)}, u32[]{:S(2)}, u32[]{:S(2)}) collective-permute-start(bf16[96,3072]{1,0:T(8,128)(2,1)S(1)} %pad_maximum_fusion.refs_0_), channel_id=1, source_target_pairs={{0,3},{1,2},{2,1},{3,0},{4,7},{5,6},{6,5},{7,4},{8,11},{9,10},{10,... | collective-permute-start | bytes 1769480 | tf_op jit(solution)/shard_map/ppermute | solution.py:78
  30.5 4.2 %all-to-all-start = ((bf16[4,1664,128]{2,1,0:T(8,128)(2,1)}), bf16[4,1664,128]{2,1,0:T(8,128)(2,1)S(1)}, u32[]{:S(2)}, u32[]{:S(2)}) async-start(bf16[4,1664,128]{2,1,0:T(8,128)(2,1)} %shard_map.138), calls=%async_computation | async-start | bytes 3407872 | tf_op jit(solution)/shard_map/all_to_all | solution.py:580
  34.6 6.2 %collective-permute-done.12.refs_4_ = bf16[96,3072]{1,0:T(8,128)(2,1)} collective-permute-done((bf16[96,3072]{1,0:T(8,128)(2,1)S(1)}, bf16[96,3072]{1,0:T(8,128)(2,1)}, u32[]{:S(2)}, u32[]{:S(2)}) %collective-permute-start.12) | collective-permute-done | bytes 589856 | tf_op jit(solution)/shard_map/ppermute | solution.py:78
  49.6 3.0 %collective-permute-start.14 = (bf16[48,3072]{1,0:T(8,128)(2,1)S(1)}, bf16[48,3072]{1,0:T(8,128)(2,1)}, u32[]{:S(2)}, u32[]{:S(2)}) collective-permute-start(bf16[48,3072]{1,0:T(8,128)(2,1)S(1)} %slice.19), channel_id=1, source_target_pairs={{0,3},{1,2},{2,1},{3,0},{4,7},{5,6},{6,5},{7,4},{8,11},{9,10},{10,... | collective-permute-start | bytes 884744 | tf_op jit(solution)/shard_map/ppermute | solution.py:78
  52.6 6.4 %collective-permute-done.14.refs_3_ = bf16[48,3072]{1,0:T(8,128)(2,1)} collective-permute-done((bf16[48,3072]{1,0:T(8,128)(2,1)S(1)}, bf16[48,3072]{1,0:T(8,128)(2,1)}, u32[]{:S(2)}, u32[]{:S(2)}) %collective-permute-start.14) | collective-permute-done | bytes 294944 | tf_op jit(solution)/shard_map/ppermute | solution.py:78
  65.0 7.1 %shard_map.139 = (bf16[768,128]{1,0:T(8,128)(2,1)S(1)}, bf16[768,128]{1,0:T(8,128)(2,1)S(1)}, bf16[768,128]{1,0:T(8,128)(2,1)S(1)}, bf16[768,128]{1,0:T(8,128)(2,1)S(1)}) custom-call(s32[3]{0:T(128)S(1)} %copy-done.5, bf16[768,768]{1,0:T(8,128)(2,1)S(1)} %fusion.order, bf16[96,3072]{1,0:T(8,128)(2,1)S(1)} %pad_maximum_fusion.refs_0_, ...), custom_call_target="tpu_custom_call" | custom-call | flops 1000000 | bytes 16 | tf_op jit(solution)/shard_map/pallas_call | solution.py:215
  73.1 2.9 %collective-permute-start.20 = (bf16[768,128]{1,0:T(8,128)(2,1)S(1)}, bf16[768,128]{1,0:T(8,128)(2,1)S(1)}, u32[]{:S(2)}, u32[]{:S(2)}) collective-permute-start(bf16[768,128]{1,0:T(8,128)(2,1)S(1)} %get-tuple-element.146), channel_id=1, source_target_pairs={{0,16},{8,24},{16,0},{24,8},{1,17},{9,25},{17,1},{25,9},{2,18},{10... | collective-permute-start | bytes 589832 | tf_op jit(solution)/shard_map/ppermute | solution.py:78
  77.0 10.1 %shard_map.140 = (bf16[1536,2048]{1,0:T(8,128)(2,1)S(1)}, bf16[2,1536,256]{2,1,0:T(8,128)(2,1)S(1)}, f32[3,1536,128]{2,1,0:T(8,128)S(1)}, f32[2,1536,128]{2,1,0:...) custom-call(s32[3]{0:T(128)S(1)} %copy-done.5, ...), custom_call_target="tpu_custom_call" | custom-call | flops 1000000 | bytes 16 | tf_op jit(solution)/shard_map/pallas_call | solution.py:290
  88.0 7.4 %shard_map.141 = (bf16[4,640,128]{2,1,0:T(8,128)(2,1)S(1)}, bf16[4,640,128]{2,1,0:T(8,128)(2,1)S(1)}, bf16[256,128]{1,0:T(8,128)(2,1)S(1)}, bf16[256,128]{1,0:T(...) custom-call(bf16[1536,2048]{1,0:T(8,128)(2,1)S(1)} %get-tuple-element.157.refs_0_, ...), custom_call_target="tpu_custom_call" | custom-call | flops 1000000 | bytes 16 | tf_op jit(solution)/shard_map/pallas_call | solution.py:419
  95.5 3.2 %shard_map.142 = (bf16[4,640,128]{2,1,0:T(8,128)(2,1)S(1)}, bf16[4,640,128]{2,1,0:T(8,128)(2,1)S(1)}, bf16[128,128]{1,0:T(8,128)(2,1)S(1)}, bf16[128,128]{1,0:T(...) custom-call(bf16[1536,2048]{1,0:T(8,128)(2,1)S(1)} %get-tuple-element.157.refs_0_, ...), custom_call_target="tpu_custom_call" | custom-call | flops 1000000 | bytes 16 | tf_op jit(solution)/shard_map/pallas_call | solution.py:419
  99.5 2.9 %collective-permute-start.26 = (bf16[896,128]{1,0:T(8,128)(2,1)S(1)}, bf16[896,128]{1,0:T(8,128)(2,1)S(1)}, u32[]{:S(2)}, u32[]{:S(2)}) collective-permute-start(bf16[896,128]{1,0:T(8,128)(2,1)S(1)} %get-tuple-element.193), channel_id=1, source_target_pairs={{0,16},{8,24},{16,0},{24,8},{1,17},{9,25},{17,1},{25,9},{2,18},{10... | collective-permute-start | bytes 688136 | tf_op jit(solution)/shard_map/ppermute | solution.py:78
  104.4 3.6 %collective-permute-done.25.refs_2_ = bf16[896,128]{1,0:T(8,128)(2,1)S(1)} collective-permute-done((bf16[896,128]{1,0:T(8,128)(2,1)S(1)}, bf16[896,128]{1,0:T(8,128)(2,1)S(1)}, u32[]{:S(2)}, u32[]{:S(2)}) %collective-permute-start.25) | collective-permute-done | bytes 229408 | tf_op jit(solution)/shard_map/ppermute | solution.py:78
  108.0 5.0 %collective-permute-done.26.refs_3_ = bf16[896,128]{1,0:T(8,128)(2,1)S(1)} collective-permute-done((bf16[896,128]{1,0:T(8,128)(2,1)S(1)}, bf16[896,128]{1,0:T(8,128)(2,1)S(1)}, u32[]{:S(2)}, u32[]{:S(2)}) %collective-permute-start.26) | collective-permute-done | bytes 229408 | tf_op jit(solution)/shard_map/ppermute | solution.py:78
  116.6 3.3 %collective-permute-start.32 = (bf16[416,512]{1,0:T(8,128)(2,1)S(1)}, bf16[416,512]{1,0:T(8,128)(2,1)S(1)}, u32[]{:S(2)}, u32[]{:S(2)}) collective-permute-start(bf16[416,512]{1,0:T(8,128)(2,1)S(1)} %get-tuple-element.206), channel_id=1, source_target_pairs={{0,64},{64,0},{1,65},{65,1},{2,66},{66,2},{3,67},{67,3},{4,68},{68... | collective-permute-start | bytes 1277960 | tf_op jit(solution)/shard_map/ppermute | solution.py:66
  121.1 3.2 %collective-permute-start.29 = (bf16[768,128]{1,0:T(8,128)(2,1)S(1)}, bf16[768,128]{1,0:T(8,128)(2,1)S(1)}, u32[]{:S(2)}, u32[]{:S(2)}) collective-permute-start(bf16[768,128]{1,0:T(8,128)(2,1)S(1)} %get-tuple-element.202), channel_id=1, source_target_pairs={{0,16},{8,24},{16,0},{24,8},{1,17},{9,25},{17,1},{25,9},{2,18},{10... | collective-permute-start | bytes 589832 | tf_op jit(solution)/shard_map/ppermute | solution.py:78
  128.4 3.6 %collective-permute-done.30.refs_4_ = bf16[768,128]{1,0:T(8,128)(2,1)S(1)} collective-permute-done((bf16[768,128]{1,0:T(8,128)(2,1)S(1)}, bf16[768,128]{1,0:T(8,128)(2,1)S(1)}, u32[]{:S(2)}, u32[]{:S(2)}) %collective-permute-start.30) | collective-permute-done | bytes 196640 | tf_op jit(solution)/shard_map/ppermute | solution.py:78
  133.4 2.7 %collective-permute-start.35 = (bf16[416,256]{1,0:T(8,128)(2,1)S(1)}, bf16[416,256]{1,0:T(8,128)(2,1)S(1)}, u32[]{:S(2)}, u32[]{:S(2)}) collective-permute-start(bf16[416,256]{1,0:T(8,128)(2,1)S(1)} %get-tuple-element.214), channel_id=1, source_target_pairs={{0,64},{64,0},{1,65},{65,1},{2,66},{66,2},{3,67},{67,3},{4,68},{68... | collective-permute-start | bytes 638984 | tf_op jit(solution)/shard_map/ppermute | solution.py:66
  139.6 3.2 %collective-permute-done.33.refs_3_ = bf16[416,512]{1,0:T(8,128)(2,1)S(1)} collective-permute-done((bf16[416,512]{1,0:T(8,128)(2,1)S(1)}, bf16[416,512]{1,0:T(8,128)(2,1)S(1)}, u32[]{:S(2)}, u32[]{:S(2)}) %collective-permute-start.33) | collective-permute-done | bytes 426016 | tf_op jit(solution)/shard_map/ppermute | solution.py:74
  142.8 3.8 %collective-permute-done.35.refs_6_ = bf16[416,256]{1,0:T(8,128)(2,1)S(1)} collective-permute-done((bf16[416,256]{1,0:T(8,128)(2,1)S(1)}, bf16[416,256]{1,0:T(8,128)(2,1)S(1)}, u32[]{:S(2)}, u32[]{:S(2)}) %collective-permute-start.35) | collective-permute-done | bytes 213024 | tf_op jit(solution)/shard_map/ppermute | solution.py:66
  146.6 2.6 %collective-permute-done.36.refs_7_ = bf16[416,256]{1,0:T(8,128)(2,1)S(1)} collective-permute-done((bf16[416,256]{1,0:T(8,128)(2,1)S(1)}, bf16[416,256]{1,0:T(8,128)(2,1)S(1)}, u32[]{:S(2)}, u32[]{:S(2)}) %collective-permute-start.36) | collective-permute-done | bytes 213024 | tf_op jit(solution)/shard_map/ppermute | solution.py:74
  (105 shorter events, 46.5 us)
Async XLA Ops:
  0.6 12.8 %collective-permute-start.3 = (bf16[24,3072]{1,0:T(8,128)(2,1)}, bf16[24,3072]{1,0:T(8,128)(2,1)S(1)}, u32[]{:S(2)}, u32[]{:S(2)}) collective-permute-start(bf16[24,3072]{1,0:T(8,128)(2,1)} %param.19), channel_id=1, source_target_pairs={{0,16},{8,24},{16,0},{24,8},{1,17},{9,25},{17,1},{25,9},{2,18},{10... | collective-permute-start | bytes 442376 | tf_op jit(solution)/shard_map/ppermute | solution.py:78
  4.0 10.0 %collective-permute-start.2 = (bf16[24,3072]{1,0:T(8,128)(2,1)}, bf16[24,3072]{1,0:T(8,128)(2,1)S(1)}, u32[]{:S(2)}, u32[]{:S(2)}) collective-permute-start(bf16[24,3072]{1,0:T(8,128)(2,1)} %param.19), channel_id=1, source_target_pairs={{0,8},{8,0},{16,24},{24,16},{1,9},{9,1},{17,25},{25,17},{2,10},{10... | collective-permute-start | bytes 442376 | tf_op jit(solution)/shard_map/ppermute | solution.py:78
  13.4 10.2 %collective-permute-start.6 = (bf16[224,768]{1,0:T(8,128)(2,1)}, bf16[224,768]{1,0:T(8,128)(2,1)S(1)}, u32[]{:S(2)}, u32[]{:S(2)}) collective-permute-start(bf16[224,768]{1,0:T(8,128)(2,1)} %get-tuple-element.118), channel_id=1, source_target_pairs={{0,96},{32,64},{64,32},{96,0},{1,97},{33,65},{65,33},{97,1},{2,98}... | collective-permute-start | bytes 1032200 | tf_op jit(solution)/shard_map/ppermute | solution.py:74
  23.6 19.6 %collective-permute-start.9 = (bf16[128,3072]{1,0:T(8,128)(2,1)S(1)}, bf16[128,3072]{1,0:T(8,128)(2,1)}, u32[]{:S(2)}, u32[]{:S(2)}) collective-permute-start(bf16[128,3072]{1,0:T(8,128)(2,1)S(1)} %fusion.1.refs_10_), channel_id=1, source_target_pairs={{0,96},{32,64},{64,32},{96,0},{1,97},{33,65},{65,33},{97,1},{2,98}... | collective-permute-start | bytes 2359304 | tf_op jit(solution)/shard_map/ppermute | solution.py:74
  24.9 21.1 %collective-permute-start.8 = (bf16[128,3072]{1,0:T(8,128)(2,1)S(1)}, bf16[128,3072]{1,0:T(8,128)(2,1)}, u32[]{:S(2)}, u32[]{:S(2)}) collective-permute-start(bf16[128,3072]{1,0:T(8,128)(2,1)S(1)} %fusion.1.refs_10_), channel_id=1, source_target_pairs={{0,32},{32,0},{1,33},{33,1},{2,34},{34,2},{3,35},{35,3},{4,36},{36... | collective-permute-start | bytes 2359304 | tf_op jit(solution)/shard_map/ppermute | solution.py:66
  24.9 15.9 %collective-permute-start.12 = (bf16[96,3072]{1,0:T(8,128)(2,1)S(1)}, bf16[96,3072]{1,0:T(8,128)(2,1)}, u32[]{:S(2)}, u32[]{:S(2)}) collective-permute-start(bf16[96,3072]{1,0:T(8,128)(2,1)S(1)} %pad_maximum_fusion.refs_0_), channel_id=1, source_target_pairs={{0,3},{1,2},{2,1},{3,0},{4,7},{5,6},{6,5},{7,4},{8,11},{9,10},{10,... | collective-permute-start | bytes 1769480 | tf_op jit(solution)/shard_map/ppermute | solution.py:78
  29.0 13.6 %collective-permute-start.7 = (bf16[96,3072]{1,0:T(8,128)(2,1)S(1)}, bf16[96,3072]{1,0:T(8,128)(2,1)}, u32[]{:S(2)}, u32[]{:S(2)}) collective-permute-start(bf16[96,3072]{1,0:T(8,128)(2,1)S(1)} %pad_maximum_fusion.refs_0_), channel_id=1, source_target_pairs={{0,1},{1,0},{2,3},{3,2},{4,5},{5,4},{6,7},{7,6},{8,9},{9,8},{10,11... | collective-permute-start | bytes 1769480 | tf_op jit(solution)/shard_map/ppermute | solution.py:78
  30.5 30.0 %all-to-all-start = ((bf16[4,1664,128]{2,1,0:T(8,128)(2,1)}), bf16[4,1664,128]{2,1,0:T(8,128)(2,1)S(1)}, u32[]{:S(2)}, u32[]{:S(2)}) async-start(bf16[4,1664,128]{2,1,0:T(8,128)(2,1)} %shard_map.138), calls=%async_computation | async-start | bytes 3407872 | tf_op jit(solution)/shard_map/all_to_all | solution.py:580
  42.6 16.5 %collective-permute-start.16 = (bf16[96,3072]{1,0:T(8,128)(2,1)}, bf16[96,3072]{1,0:T(8,128)(2,1)}, u32[]{:S(2)}, u32[]{:S(2)}) collective-permute-start(bf16[96,3072]{1,0:T(8,128)(2,1)} %collective-permute-done.12.refs_4_), channel_id=1, source_target_pairs={{0,4},{4,0},{1,5},{5,1},{2,6},{6,2},{3,7},{7,3},{8,12},{12,8},{9,1... | collective-permute-start | bytes 1769480 | tf_op jit(solution)/shard_map/ppermute | solution.py:66
  42.6 16.5 %collective-permute-start.15 = (bf16[96,3072]{1,0:T(8,128)(2,1)}, bf16[96,3072]{1,0:T(8,128)(2,1)}, u32[]{:S(2)}, u32[]{:S(2)}) collective-permute-start(bf16[96,3072]{1,0:T(8,128)(2,1)} %collective-permute-done.7.refs_1_), channel_id=1, source_target_pairs={{0,4},{4,0},{1,5},{5,1},{2,6},{6,2},{3,7},{7,3},{8,12},{12,8},{9,1... | collective-permute-start | bytes 1769480 | tf_op jit(solution)/shard_map/ppermute | solution.py:66
  44.2 14.8 %collective-permute-start.10 = (bf16[64,3072]{1,0:T(8,128)(2,1)S(1)}, bf16[64,3072]{1,0:T(8,128)(2,1)S(1)}, u32[]{:S(2)}, u32[]{:S(2)}) collective-permute-start(bf16[64,3072]{1,0:T(8,128)(2,1)S(1)} %slice.16), channel_id=1, source_target_pairs={{0,32},{32,0},{1,33},{33,1},{2,34},{34,2},{3,35},{35,3},{4,36},{36... | collective-permute-start | bytes 1179656 | tf_op jit(solution)/shard_map/ppermute | solution.py:66
  47.1 12.1 %collective-permute-start.11 = (bf16[64,3072]{1,0:T(8,128)(2,1)S(1)}, bf16[64,3072]{1,0:T(8,128)(2,1)S(1)}, u32[]{:S(2)}, u32[]{:S(2)}) collective-permute-start(bf16[64,3072]{1,0:T(8,128)(2,1)S(1)} %slice.17), channel_id=1, source_target_pairs={{0,96},{32,64},{64,32},{96,0},{1,97},{33,65},{65,33},{97,1},{2,98}... | collective-permute-start | bytes 1179656 | tf_op jit(solution)/shard_map/ppermute | solution.py:74
  62.3 14.7 %collective-permute-start.22 = (bf16[4,1664,128]{2,1,0:T(8,128)(2,1)S(1)}, bf16[4,1664,128]{2,1,0:T(8,128)(2,1)}, u32[]{:S(2)}, u32[]{:S(2)}) collective-permute-start(bf16[4,1664,128]{2,1,0:T(8,128)(2,1)S(1)} %all-to-all-done.own), channel_id=1, source_target_pairs={{0,4},{4,0},{1,5},{5,1},{2,6},{6,2},{3,7},{7,3},{8,12},{12,8},{9,1... | collective-permute-start | bytes 5111816 | tf_op jit(solution)/shard_map/ppermute | solution.py:66
  72.1 15.0 %collective-permute-start.19 = (bf16[768,128]{1,0:T(8,128)(2,1)S(1)}, bf16[768,128]{1,0:T(8,128)(2,1)S(1)}, u32[]{:S(2)}, u32[]{:S(2)}) collective-permute-start(bf16[768,128]{1,0:T(8,128)(2,1)S(1)} %get-tuple-element.145), channel_id=1, source_target_pairs={{0,8},{8,0},{16,24},{24,16},{1,9},{9,1},{17,25},{25,17},{2,10},{10... | collective-permute-start | bytes 589832 | tf_op jit(solution)/shard_map/ppermute | solution.py:78
  73.1 14.0 %collective-permute-start.20 = (bf16[768,128]{1,0:T(8,128)(2,1)S(1)}, bf16[768,128]{1,0:T(8,128)(2,1)S(1)}, u32[]{:S(2)}, u32[]{:S(2)}) collective-permute-start(bf16[768,128]{1,0:T(8,128)(2,1)S(1)} %get-tuple-element.146), channel_id=1, source_target_pairs={{0,16},{8,24},{16,0},{24,8},{1,17},{9,25},{17,1},{25,9},{2,18},{10... | collective-permute-start | bytes 589832 | tf_op jit(solution)/shard_map/ppermute | solution.py:78
  76.0 12.0 %collective-permute-start.21 = (bf16[768,128]{1,0:T(8,128)(2,1)S(1)}, bf16[768,128]{1,0:T(8,128)(2,1)S(1)}, u32[]{:S(2)}, u32[]{:S(2)}) collective-permute-start(bf16[768,128]{1,0:T(8,128)(2,1)S(1)} %get-tuple-element.147), channel_id=1, source_target_pairs={{0,24},{8,16},{16,8},{24,0},{1,25},{9,17},{17,9},{25,1},{2,26},{10... | collective-permute-start | bytes 589832 | tf_op jit(solution)/shard_map/ppermute | solution.py:78
  99.5 13.4 %collective-permute-start.26 = (bf16[896,128]{1,0:T(8,128)(2,1)S(1)}, bf16[896,128]{1,0:T(8,128)(2,1)S(1)}, u32[]{:S(2)}, u32[]{:S(2)}) collective-permute-start(bf16[896,128]{1,0:T(8,128)(2,1)S(1)} %get-tuple-element.193), channel_id=1, source_target_pairs={{0,16},{8,24},{16,0},{24,8},{1,17},{9,25},{17,1},{25,9},{2,18},{10... | collective-permute-start | bytes 688136 | tf_op jit(solution)/shard_map/ppermute | solution.py:78
  102.5 13.1 %collective-permute-start.27 = (bf16[896,128]{1,0:T(8,128)(2,1)S(1)}, bf16[896,128]{1,0:T(8,128)(2,1)S(1)}, u32[]{:S(2)}, u32[]{:S(2)}) collective-permute-start(bf16[896,128]{1,0:T(8,128)(2,1)S(1)} %get-tuple-element.194), channel_id=1, source_target_pairs={{0,24},{8,16},{16,8},{24,0},{1,25},{9,17},{17,9},{25,1},{2,26},{10... | collective-permute-start | bytes 688136 | tf_op jit(solution)/shard_map/ppermute | solution.py:78
  116.3 15.6 %collective-permute-start.31 = (bf16[416,512]{1,0:T(8,128)(2,1)S(1)}, bf16[416,512]{1,0:T(8,128)(2,1)S(1)}, u32[]{:S(2)}, u32[]{:S(2)}) collective-permute-start(bf16[416,512]{1,0:T(8,128)(2,1)S(1)} %get-tuple-element.204), channel_id=1, source_target_pairs={{0,32},{32,0},{1,33},{33,1},{2,34},{34,2},{3,35},{35,3},{4,36},{36... | collective-permute-start | bytes 1277960 | tf_op jit(solution)/shard_map/ppermute | solution.py:66
  116.6 23.0 %collective-permute-start.32 = (bf16[416,512]{1,0:T(8,128)(2,1)S(1)}, bf16[416,512]{1,0:T(8,128)(2,1)S(1)}, u32[]{:S(2)}, u32[]{:S(2)}) collective-permute-start(bf16[416,512]{1,0:T(8,128)(2,1)S(1)} %get-tuple-element.206), channel_id=1, source_target_pairs={{0,64},{64,0},{1,65},{65,1},{2,66},{66,2},{3,67},{67,3},{4,68},{68... | collective-permute-start | bytes 1277960 | tf_op jit(solution)/shard_map/ppermute | solution.py:66
  119.9 22.9 %collective-permute-start.33 = (bf16[416,512]{1,0:T(8,128)(2,1)S(1)}, bf16[416,512]{1,0:T(8,128)(2,1)S(1)}, u32[]{:S(2)}, u32[]{:S(2)}) collective-permute-start(bf16[416,512]{1,0:T(8,128)(2,1)S(1)} %get-tuple-element.207), channel_id=1, source_target_pairs={{0,96},{32,64},{64,32},{96,0},{1,97},{33,65},{65,33},{97,1},{2,98}... | collective-permute-start | bytes 1277960 | tf_op jit(solution)/shard_map/ppermute | solution.py:74
  132.6 10.2 %collective-permute-start.34 = (bf16[416,256]{1,0:T(8,128)(2,1)S(1)}, bf16[416,256]{1,0:T(8,128)(2,1)S(1)}, u32[]{:S(2)}, u32[]{:S(2)}) collective-permute-start(bf16[416,256]{1,0:T(8,128)(2,1)S(1)} %get-tuple-element.213), channel_id=1, source_target_pairs={{0,32},{32,0},{1,33},{33,1},{2,34},{34,2},{3,35},{35,3},{4,36},{36... | collective-permute-start | bytes 638984 | tf_op jit(solution)/shard_map/ppermute | solution.py:66
  133.4 13.2 %collective-permute-start.35 = (bf16[416,256]{1,0:T(8,128)(2,1)S(1)}, bf16[416,256]{1,0:T(8,128)(2,1)S(1)}, u32[]{:S(2)}, u32[]{:S(2)}) collective-permute-start(bf16[416,256]{1,0:T(8,128)(2,1)S(1)} %get-tuple-element.214), channel_id=1, source_target_pairs={{0,64},{64,0},{1,65},{65,1},{2,66},{66,2},{3,67},{67,3},{4,68},{68... | collective-permute-start | bytes 638984 | tf_op jit(solution)/shard_map/ppermute | solution.py:66
  136.1 13.1 %collective-permute-start.36 = (bf16[416,256]{1,0:T(8,128)(2,1)S(1)}, bf16[416,256]{1,0:T(8,128)(2,1)S(1)}, u32[]{:S(2)}, u32[]{:S(2)}) collective-permute-start(bf16[416,256]{1,0:T(8,128)(2,1)S(1)} %get-tuple-element.215), channel_id=1, source_target_pairs={{0,96},{32,64},{64,32},{96,0},{1,97},{33,65},{65,33},{97,1},{2,98}... | collective-permute-start | bytes 638984 | tf_op jit(solution)/shard_map/ppermute | solution.py:74
  (23 other events, 172.6 us)

commit v5 on v4

--- a/solution.py
+++ b/solution.py
@@ -517,27 +517,54 @@
 
 def merge_x_kernel(at_ref, *refs):
     x = at_ref[0]
-    parts_a, parts_b, outs = refs[:4], refs[4:8], refs[8:13]
+    parts, outs = refs[:4], refs[4:]
     for r in range(4):
-        for part, first in ((parts_a[r], 0), (parts_b[r], 4 * HD)):
-            col = lanes((x ^ r) * XW + first, part.shape[1])
-            row = 0
-            for out in outs:
-                count = out.shape[0]
-                out[:, col] = part[row : row + count]
-                row += count
+        col = lanes((x ^ r) * XW, parts[r].shape[1])
+        row = 0
+        for out in outs:
+            count = out.shape[0]
+            out[:, col] = parts[r][row : row + count]
+            row += count
+
+
+def add_shared_kernel(at_ref, *refs):
+    x = at_ref[0]
+    parts, outs, sems = refs[:4], refs[9:14], refs[14]
+    started = []
+    for r in range(4):
+        col = lanes((x ^ r) * XW + 4 * HD, 2 * HD)
+        row = 0
+        for i, out in enumerate(outs):
+            count = out.shape[0]
+            src = parts[r].at[pl.ds(row, count)]
+            copy = pltpu.make_async_copy(src, out.at[:, col], sems.at[r, i])
+            copy.start()
+            started.append(copy)
+            row += count
+    for copy in started:
+        copy.wait()
 
 
 def merge_x(at, parts_a, parts_b):
     shapes = [bf16(TOK, 4 * XW)] * 3 + [bf16(TT, 4 * XW)] * 2
-    return pl.pallas_call(
+    placed = pl.pallas_call(
         merge_x_kernel,
-        in_specs=[SMEM] + vmem_specs(8),
+        in_specs=[SMEM] + vmem_specs(4),
         out_specs=[whole(a) for a in shapes],
         out_shape=shapes,
         compiler_params=params(16),
         cost_estimate=COST,
-    )(at, *parts_a, *parts_b)
+    )(at, *parts_a)
+    return pl.pallas_call(
+        add_shared_kernel,
+        in_specs=[SMEM] + vmem_specs(4) + [pl.BlockSpec(memory_space=pl.ANY)] * 5,
+        out_specs=[pl.BlockSpec(memory_space=pl.ANY)] * 5,
+        out_shape=shapes,
+        input_output_aliases={5 + i: i for i in range(5)},
+        scratch_shapes=[pltpu.SemaphoreType.DMA((4, 5))],
+        compiler_params=params(16),
+        cost_estimate=COST,
+    )(at, *parts_b, *placed)
 
 
 def local(q_video, k_video, v_video, k_text, v_text, text_len, guide_index, gate, adjoint, w_out):
@@ -578,11 +605,11 @@
     adjoints = [scaled, scaled1, x_swap(scaled3[:half], 1), x_swap(scaled1[half:], 3), scaled3]
     messages = cut_y(own, got1, got2, got3)
     arrived = lax.all_to_all(messages, "y", split_axis=0, concat_axis=0, tiled=True)
+    w_z1, w_z2, w_z3 = lax.optimization_barrier((w_z1, w_z2, w_z3))
     w_swapped = [w_y_swapped, swap(w_z1, "core"), swap(w_z3, "core")]
-    adjoints, w_z2, w_swapped = lax.optimization_barrier((adjoints, w_z2, w_swapped))
     w_z2_swapped = [swap(piece, "core") for piece in w_z2]
     weights = [w_y, w_z1] + w_z2 + [w_z3] + w_swapped[:2] + w_z2_swapped + w_swapped[2:]
-    arrived, weights = lax.optimization_barrier((arrived, weights))
+    arrived, adjoints, weights = lax.optimization_barrier((arrived, adjoints, weights))
     other = swap(arrived, "core")
 
     at_core = (c ^ two)[:, None, None, None]

time: 152 us -> 151 us (level)
  waiting for transfers between devices: 53.1 us -> 49.5 us
    ppermute x16, waiting for transfers between devices: 31.3 us -> 25.7 us  [ring_swap(): return lax.ppermute(a, axis, [(i, i ^ r) for i in range(4)])]
    ppermute x5, waiting for transfers between devices: 7.69 us -> 12.1 us  [x_swap(): return lax.ppermute(a, ('cfg', 'xlo'), [(i, 3 - i) for i in range(4)])]
    ppermute x16, waiting for transfers between devices: 14.2 us -> 11.8 us  [swap(): return lax.ppermute(a, axis, [(0, 1), (1, 0)])]
    ppermute x16, starting transfers between devices: 14.3 us -> 12.2 us  [swap(): return lax.ppermute(a, axis, [(0, 1), (1, 0)])]
    ppermute x16, starting transfers between devices: 25.7 us -> 27.2 us  [ring_swap(): return lax.ppermute(a, axis, [(i, i ^ r) for i in range(4)])]
    pallas_call x1 -> x2, Pallas kernels: 2.24 us -> 3.74 us  [the longest x1 2.13 us: merge_x(): pl.pallas_call(merge_x_kernel, in_specs=[SMEM] + vmem_specs(4), out_specs...]
  transfers between devices with their start and end apart: 38 -> 38, of which waited for: 19 -> 19; matrix products, arithmetic and copies ran while one was open for 5% -> 6% of each run, Pallas kernels for 17% -> 19%
where the time goes in v5:
time: 151 us
  starting transfers between devices  50.3 us (33%)
  waiting for transfers between devices  49.5 us (33%)
  Pallas kernels  38.1 us (25%)
  local copies, waits for them, and re-layouts  8.25 us (5%)
  other arithmetic  2.72 us (2%)
  between operations  1.72 us (1%)
    ppermute x16, starting transfers between devices, ring_swap(): return lax.ppermute(a, axis, [(i, i ^ r) for i in range(4)])  27.2 us
    ppermute x16, waiting for transfers between devices, ring_swap(): return lax.ppermute(a, axis, [(i, i ^ r) for i in range(4)])  25.7 us
    ppermute x16, starting transfers between devices, swap(): return lax.ppermute(a, axis, [(0, 1), (1, 0)])  12.2 us
    ppermute x5, waiting for transfers between devices, x_swap(): return lax.ppermute(a, ('cfg', 'xlo'), [(i, 3 - i) for i in range(4)])  12.1 us
    ppermute x16, waiting for transfers between devices, swap(): return lax.ppermute(a, axis, [(0, 1), (1, 0)])  11.8 us
    pallas_call x2, Pallas kernels, attention_backward(): pl.pallas_call(kernel, grid=(steps,), in_specs=[rows_of(VIDK), stacked(2,...  10.6 us
    pallas_call x1, Pallas kernels, attention_forward(): pl.pallas_call(forward_kernel, grid=(rows // BLOCK,), in_specs=[SMEM] + [...  10.1 us
    pallas_call x1, Pallas kernels, project(): pl.pallas_call(project_kernel, in_specs=[SMEM, whole(order)] + [pl.BlockS...  7.13 us
  transfers between devices with their start and end apart: 38, of which 19 were waited for; matrix products, arithmetic and copies ran while one was open for 6% of the time, Pallas kernels for 19%

profile of v5, /device:TPU:0, one launch (start us, length us, event | category | flops | bytes accessed | tf_op | source)
XLA Modules:
  0.0 150.6 jit_solution(2430465819277169305)
XLA Ops:
  0.6 3.4 %collective-permute-start.3 = (bf16[24,3072]{1,0:T(8,128)(2,1)}, bf16[24,3072]{1,0:T(8,128)(2,1)S(1)}, u32[]{:S(2)}, u32[]{:S(2)}) collective-permute-start(bf16[24,3072]{1,0:T(8,128)(2,1)} %param.19), channel_id=1, source_target_pairs={{0,16},{8,24},{16,0},{24,8},{1,17},{9,25},{17,1},{25,9},{2,18},{10... | collective-permute-start | bytes 442376 | tf_op jit(solution)/shard_map/ppermute | solution.py:78
  5.6 3.3 %shard_map.137 = (bf16[416,768]{1,0:T(8,128)(2,1)}, bf16[224,768]{1,0:T(8,128)(2,1)}, bf16[224,768]{1,0:T(8,128)(2,1)}, bf16[32,768]{1,0:T(8,128)(2,1)}) custom-call(s32[3]{0:T(128)} %pad_add_fusion.at_ref.refs_0_, bf16[128,3072]{1,0:T(8,128)(2,1)} %bitcast.20, bf16[128,3072]{1,0:T(8,128)(2,1)} %bitcast.23, bf16[128,3072]{1,0:T(8,128)(2,1)} %bitcast.26, ...), custom_call_target="tpu_custom_call" | custom-call | flops 1000000 | bytes 16 | tf_op jit(solution)/shard_map/pallas_call | solution.py:111
  8.9 3.1 %collective-permute-start.1 = (bf16[32,768]{1,0:T(8,128)(2,1)}, bf16[32,768]{1,0:T(8,128)(2,1)S(1)}, u32[]{:S(2)}, u32[]{:S(2)}) collective-permute-start(bf16[32,768]{1,0:T(8,128)(2,1)} %get-tuple-element.119), channel_id=1, source_target_pairs={{0,64},{64,0},{1,65},{65,1},{2,66},{66,2},{3,67},{67,3},{4,68},{68... | collective-permute-start | bytes 147464 | tf_op jit(solution)/shard_map/ppermute | solution.py:66
  15.2 4.0 %collective-permute-start.12 = (bf16[96,3072]{1,0:T(8,128)(2,1)S(1)}, bf16[96,3072]{1,0:T(8,128)(2,1)}, u32[]{:S(2)}, u32[]{:S(2)}) collective-permute-start(bf16[96,3072]{1,0:T(8,128)(2,1)S(1)} %pad_maximum_fusion.refs_0_), channel_id=1, source_target_pairs={{0,3},{1,2},{2,1},{3,0},{4,7},{5,6},{6,5},{7,4},{8,11},{9,10},{10,... | collective-permute-start | bytes 1769480 | tf_op jit(solution)/shard_map/ppermute | solution.py:78
  26.4 4.0 %all-to-all-start = ((bf16[4,1664,128]{2,1,0:T(8,128)(2,1)}), bf16[4,1664,128]{2,1,0:T(8,128)(2,1)S(1)}, u32[]{:S(2)}, u32[]{:S(2)}) async-start(bf16[4,1664,128]{2,1,0:T(8,128)(2,1)} %shard_map.138), calls=%async_computation | async-start | bytes 3407872 | tf_op jit(solution)/shard_map/all_to_all | solution.py:607
  34.4 2.6 %collective-permute-start.14 = (bf16[48,3072]{1,0:T(8,128)(2,1)S(1)}, bf16[48,3072]{1,0:T(8,128)(2,1)}, u32[]{:S(2)}, u32[]{:S(2)}) collective-permute-start(bf16[48,3072]{1,0:T(8,128)(2,1)S(1)} %slice.19), channel_id=1, source_target_pairs={{0,3},{1,2},{2,1},{3,0},{4,7},{5,6},{6,5},{7,4},{8,11},{9,10},{10,... | collective-permute-start | bytes 884744 | tf_op jit(solution)/shard_map/ppermute | solution.py:78
  37.0 2.9 %collective-permute-done.13.refs_2_ = bf16[48,3072]{1,0:T(8,128)(2,1)} collective-permute-done((bf16[48,3072]{1,0:T(8,128)(2,1)S(1)}, bf16[48,3072]{1,0:T(8,128)(2,1)}, u32[]{:S(2)}, u32[]{:S(2)}) %collective-permute-start.13) | collective-permute-done | bytes 294944 | tf_op jit(solution)/shard_map/ppermute | solution.py:78
  39.9 3.7 %collective-permute-done.14.refs_3_ = bf16[48,3072]{1,0:T(8,128)(2,1)} collective-permute-done((bf16[48,3072]{1,0:T(8,128)(2,1)S(1)}, bf16[48,3072]{1,0:T(8,128)(2,1)}, u32[]{:S(2)}, u32[]{:S(2)}) %collective-permute-start.14) | collective-permute-done | bytes 294944 | tf_op jit(solution)/shard_map/ppermute | solution.py:78
  53.2 4.5 %collective-permute-done.9.refs_12_ = bf16[64,3072]{1,0:T(8,128)(2,1)S(1)} collective-permute-done((bf16[64,3072]{1,0:T(8,128)(2,1)}, bf16[64,3072]{1,0:T(8,128)(2,1)S(1)}, u32[]{:S(2)}, u32[]{:S(2)}) %collective-permute-start.9) | collective-permute-done | bytes 393248 | tf_op jit(solution)/shard_map/ppermute | solution.py:66
  57.7 4.5 %collective-permute-done.10.refs_13_ = bf16[64,3072]{1,0:T(8,128)(2,1)} collective-permute-done((bf16[64,3072]{1,0:T(8,128)(2,1)}, bf16[64,3072]{1,0:T(8,128)(2,1)}, u32[]{:S(2)}, u32[]{:S(2)}) %collective-permute-start.10) | collective-permute-done | bytes 393248 | tf_op jit(solution)/shard_map/ppermute | solution.py:74
  64.8 7.1 %shard_map.139 = (bf16[768,128]{1,0:T(8,128)(2,1)S(1)}, bf16[768,128]{1,0:T(8,128)(2,1)S(1)}, bf16[768,128]{1,0:T(8,128)(2,1)S(1)}, bf16[768,128]{1,0:T(8,128)(2,1)S(1)}) custom-call(s32[3]{0:T(128)S(1)} %copy-done.5, bf16[768,768]{1,0:T(8,128)(2,1)S(1)} %fusion.order, bf16[96,3072]{1,0:T(8,128)(2,1)S(1)} %pad_maximum_fusion.refs_0_, ...), custom_call_target="tpu_custom_call" | custom-call | flops 1000000 | bytes 16 | tf_op jit(solution)/shard_map/pallas_call | solution.py:215
  73.7 2.7 %collective-permute-start.20 = (bf16[768,128]{1,0:T(8,128)(2,1)S(1)}, bf16[768,128]{1,0:T(8,128)(2,1)S(1)}, u32[]{:S(2)}, u32[]{:S(2)}) collective-permute-start(bf16[768,128]{1,0:T(8,128)(2,1)S(1)} %get-tuple-element.149), channel_id=1, source_target_pairs={{0,16},{8,24},{16,0},{24,8},{1,17},{9,25},{17,1},{25,9},{2,18},{10... | collective-permute-start | bytes 589832 | tf_op jit(solution)/shard_map/ppermute | solution.py:78
  76.8 10.1 %shard_map.140 = (bf16[1536,2048]{1,0:T(8,128)(2,1)S(1)}, bf16[2,1536,256]{2,1,0:T(8,128)(2,1)S(1)}, f32[3,1536,128]{2,1,0:T(8,128)S(1)}, f32[2,1536,128]{2,1,0:...) custom-call(s32[3]{0:T(128)S(1)} %copy-done.5, ...), custom_call_target="tpu_custom_call" | custom-call | flops 1000000 | bytes 16 | tf_op jit(solution)/shard_map/pallas_call | solution.py:290
  88.6 7.3 %shard_map.141 = (bf16[4,640,128]{2,1,0:T(8,128)(2,1)S(1)}, bf16[4,640,128]{2,1,0:T(8,128)(2,1)S(1)}, bf16[256,128]{1,0:T(8,128)(2,1)S(1)}, bf16[256,128]{1,0:T(...) custom-call(bf16[1536,2048]{1,0:T(8,128)(2,1)S(1)} %get-tuple-element.160.refs_0_, ...), custom_call_target="tpu_custom_call" | custom-call | flops 1000000 | bytes 16 | tf_op jit(solution)/shard_map/pallas_call | solution.py:419
  96.0 3.2 %shard_map.142 = (bf16[4,640,128]{2,1,0:T(8,128)(2,1)S(1)}, bf16[4,640,128]{2,1,0:T(8,128)(2,1)S(1)}, bf16[128,128]{1,0:T(8,128)(2,1)S(1)}, bf16[128,128]{1,0:T(...) custom-call(bf16[1536,2048]{1,0:T(8,128)(2,1)S(1)} %get-tuple-element.160.refs_0_, ...), custom_call_target="tpu_custom_call" | custom-call | flops 1000000 | bytes 16 | tf_op jit(solution)/shard_map/pallas_call | solution.py:419
  100.1 2.8 %collective-permute-start.26 = (bf16[896,128]{1,0:T(8,128)(2,1)S(1)}, bf16[896,128]{1,0:T(8,128)(2,1)S(1)}, u32[]{:S(2)}, u32[]{:S(2)}) collective-permute-start(bf16[896,128]{1,0:T(8,128)(2,1)S(1)} %get-tuple-element.196), channel_id=1, source_target_pairs={{0,16},{8,24},{16,0},{24,8},{1,17},{9,25},{17,1},{25,9},{2,18},{10... | collective-permute-start | bytes 688136 | tf_op jit(solution)/shard_map/ppermute | solution.py:78
  104.9 3.6 %collective-permute-done.25.refs_2_ = bf16[896,128]{1,0:T(8,128)(2,1)S(1)} collective-permute-done((bf16[896,128]{1,0:T(8,128)(2,1)S(1)}, bf16[896,128]{1,0:T(8,128)(2,1)S(1)}, u32[]{:S(2)}, u32[]{:S(2)}) %collective-permute-start.25) | collective-permute-done | bytes 229408 | tf_op jit(solution)/shard_map/ppermute | solution.py:78
  108.5 4.9 %collective-permute-done.26.refs_3_ = bf16[896,128]{1,0:T(8,128)(2,1)S(1)} collective-permute-done((bf16[896,128]{1,0:T(8,128)(2,1)S(1)}, bf16[896,128]{1,0:T(8,128)(2,1)S(1)}, u32[]{:S(2)}, u32[]{:S(2)}) %collective-permute-start.26) | collective-permute-done | bytes 229408 | tf_op jit(solution)/shard_map/ppermute | solution.py:78
  113.4 2.6 %collective-permute-done.27.refs_4_ = bf16[896,128]{1,0:T(8,128)(2,1)S(1)} collective-permute-done((bf16[896,128]{1,0:T(8,128)(2,1)S(1)}, bf16[896,128]{1,0:T(8,128)(2,1)S(1)}, u32[]{:S(2)}, u32[]{:S(2)}) %collective-permute-start.27) | collective-permute-done | bytes 229408 | tf_op jit(solution)/shard_map/ppermute | solution.py:78
  116.9 2.7 %collective-permute-start.35 = (bf16[416,512]{1,0:T(8,128)(2,1)S(1)}, bf16[416,512]{1,0:T(8,128)(2,1)S(1)}, u32[]{:S(2)}, u32[]{:S(2)}) collective-permute-start(bf16[416,512]{1,0:T(8,128)(2,1)S(1)} %get-tuple-element.217), channel_id=1, source_target_pairs={{0,64},{64,0},{1,65},{65,1},{2,66},{66,2},{3,67},{67,3},{4,68},{68... | collective-permute-start | bytes 1277960 | tf_op jit(solution)/shard_map/ppermute | solution.py:66
  121.5 3.4 %collective-permute-start.29 = (bf16[768,128]{1,0:T(8,128)(2,1)S(1)}, bf16[768,128]{1,0:T(8,128)(2,1)S(1)}, u32[]{:S(2)}, u32[]{:S(2)}) collective-permute-start(bf16[768,128]{1,0:T(8,128)(2,1)S(1)} %get-tuple-element.200), channel_id=1, source_target_pairs={{0,16},{8,24},{16,0},{24,8},{1,17},{9,25},{17,1},{25,9},{2,18},{10... | collective-permute-start | bytes 589832 | tf_op jit(solution)/shard_map/ppermute | solution.py:78
  128.8 3.6 %collective-permute-done.30.refs_4_ = bf16[768,128]{1,0:T(8,128)(2,1)S(1)} collective-permute-done((bf16[768,128]{1,0:T(8,128)(2,1)S(1)}, bf16[768,128]{1,0:T(8,128)(2,1)S(1)}, u32[]{:S(2)}, u32[]{:S(2)}) %collective-permute-start.30) | collective-permute-done | bytes 196640 | tf_op jit(solution)/shard_map/ppermute | solution.py:78
  139.2 3.2 %collective-permute-done.36.refs_3_ = bf16[416,512]{1,0:T(8,128)(2,1)S(1)} collective-permute-done((bf16[416,512]{1,0:T(8,128)(2,1)S(1)}, bf16[416,512]{1,0:T(8,128)(2,1)S(1)}, u32[]{:S(2)}, u32[]{:S(2)}) %collective-permute-start.36) | collective-permute-done | bytes 426016 | tf_op jit(solution)/shard_map/ppermute | solution.py:74
  146.3 2.6 %collective-permute-done.34.refs_3_ = bf16[416,256]{1,0:T(8,128)(2,1)S(1)} collective-permute-done((bf16[416,256]{1,0:T(8,128)(2,1)S(1)}, bf16[416,256]{1,0:T(8,128)(2,1)S(1)}, u32[]{:S(2)}, u32[]{:S(2)}) %collective-permute-start.34) | collective-permute-done | bytes 213024 | tf_op jit(solution)/shard_map/ppermute | solution.py:74
  (106 shorter events, 53.0 us)
Async XLA Ops:
  0.6 12.7 %collective-permute-start.3 = (bf16[24,3072]{1,0:T(8,128)(2,1)}, bf16[24,3072]{1,0:T(8,128)(2,1)S(1)}, u32[]{:S(2)}, u32[]{:S(2)}) collective-permute-start(bf16[24,3072]{1,0:T(8,128)(2,1)} %param.19), channel_id=1, source_target_pairs={{0,16},{8,24},{16,0},{24,8},{1,17},{9,25},{17,1},{25,9},{2,18},{10... | collective-permute-start | bytes 442376 | tf_op jit(solution)/shard_map/ppermute | solution.py:78
  4.0 10.0 %collective-permute-start.2 = (bf16[24,3072]{1,0:T(8,128)(2,1)}, bf16[24,3072]{1,0:T(8,128)(2,1)S(1)}, u32[]{:S(2)}, u32[]{:S(2)}) collective-permute-start(bf16[24,3072]{1,0:T(8,128)(2,1)} %param.19), channel_id=1, source_target_pairs={{0,8},{8,0},{16,24},{24,16},{1,9},{9,1},{17,25},{25,17},{2,10},{10... | collective-permute-start | bytes 442376 | tf_op jit(solution)/shard_map/ppermute | solution.py:78
  12.0 9.7 %collective-permute-start = (bf16[224,768]{1,0:T(8,128)(2,1)}, bf16[224,768]{1,0:T(8,128)(2,1)S(1)}, u32[]{:S(2)}, u32[]{:S(2)}) collective-permute-start(bf16[224,768]{1,0:T(8,128)(2,1)} %get-tuple-element.118), channel_id=1, source_target_pairs={{0,32},{32,0},{1,33},{33,1},{2,34},{34,2},{3,35},{35,3},{4,36},{36... | collective-permute-start | bytes 1032200 | tf_op jit(solution)/shard_map/ppermute | solution.py:66
  13.3 10.2 %collective-permute-start.6 = (bf16[224,768]{1,0:T(8,128)(2,1)}, bf16[224,768]{1,0:T(8,128)(2,1)S(1)}, u32[]{:S(2)}, u32[]{:S(2)}) collective-permute-start(bf16[224,768]{1,0:T(8,128)(2,1)} %get-tuple-element.122), channel_id=1, source_target_pairs={{0,96},{32,64},{64,32},{96,0},{1,97},{33,65},{65,33},{97,1},{2,98}... | collective-permute-start | bytes 1032200 | tf_op jit(solution)/shard_map/ppermute | solution.py:74
  15.2 15.4 %collective-permute-start.12 = (bf16[96,3072]{1,0:T(8,128)(2,1)S(1)}, bf16[96,3072]{1,0:T(8,128)(2,1)}, u32[]{:S(2)}, u32[]{:S(2)}) collective-permute-start(bf16[96,3072]{1,0:T(8,128)(2,1)S(1)} %pad_maximum_fusion.refs_0_), channel_id=1, source_target_pairs={{0,3},{1,2},{2,1},{3,0},{4,7},{5,6},{6,5},{7,4},{8,11},{9,10},{10,... | collective-permute-start | bytes 1769480 | tf_op jit(solution)/shard_map/ppermute | solution.py:78
  19.3 14.1 %collective-permute-start.11 = (bf16[96,3072]{1,0:T(8,128)(2,1)S(1)}, bf16[96,3072]{1,0:T(8,128)(2,1)}, u32[]{:S(2)}, u32[]{:S(2)}) collective-permute-start(bf16[96,3072]{1,0:T(8,128)(2,1)S(1)} %pad_maximum_fusion.refs_0_), channel_id=1, source_target_pairs={{0,1},{1,0},{2,3},{3,2},{4,5},{5,4},{6,7},{7,6},{8,9},{9,8},{10,11... | collective-permute-start | bytes 1769480 | tf_op jit(solution)/shard_map/ppermute | solution.py:78
  23.5 20.7 %collective-permute-start.8 = (bf16[128,3072]{1,0:T(8,128)(2,1)S(1)}, bf16[128,3072]{1,0:T(8,128)(2,1)}, u32[]{:S(2)}, u32[]{:S(2)}) collective-permute-start(bf16[128,3072]{1,0:T(8,128)(2,1)S(1)} %fusion.1.refs_10_), channel_id=1, source_target_pairs={{0,96},{32,64},{64,32},{96,0},{1,97},{33,65},{65,33},{97,1},{2,98}... | collective-permute-start | bytes 2359304 | tf_op jit(solution)/shard_map/ppermute | solution.py:74
  24.9 22.8 %collective-permute-start.7 = (bf16[128,3072]{1,0:T(8,128)(2,1)S(1)}, bf16[128,3072]{1,0:T(8,128)(2,1)}, u32[]{:S(2)}, u32[]{:S(2)}) collective-permute-start(bf16[128,3072]{1,0:T(8,128)(2,1)S(1)} %fusion.1.refs_10_), channel_id=1, source_target_pairs={{0,32},{32,0},{1,33},{33,1},{2,34},{34,2},{3,35},{35,3},{4,36},{36... | collective-permute-start | bytes 2359304 | tf_op jit(solution)/shard_map/ppermute | solution.py:66
  26.4 35.9 %all-to-all-start = ((bf16[4,1664,128]{2,1,0:T(8,128)(2,1)}), bf16[4,1664,128]{2,1,0:T(8,128)(2,1)S(1)}, u32[]{:S(2)}, u32[]{:S(2)}) async-start(bf16[4,1664,128]{2,1,0:T(8,128)(2,1)} %shard_map.138), calls=%async_computation | async-start | bytes 3407872 | tf_op jit(solution)/shard_map/all_to_all | solution.py:607
  43.7 9.5 %collective-permute-start.15 = (bf16[96,3072]{1,0:T(8,128)(2,1)}, bf16[96,3072]{1,0:T(8,128)(2,1)}, u32[]{:S(2)}, u32[]{:S(2)}) collective-permute-start(bf16[96,3072]{1,0:T(8,128)(2,1)} %collective-permute-done.11.refs_1_), channel_id=1, source_target_pairs={{0,4},{4,0},{1,5},{5,1},{2,6},{6,2},{3,7},{7,3},{8,12},{12,8},{9,1... | collective-permute-start | bytes 1769480 | tf_op jit(solution)/shard_map/ppermute | solution.py:66
  46.0 11.7 %collective-permute-start.9 = (bf16[64,3072]{1,0:T(8,128)(2,1)}, bf16[64,3072]{1,0:T(8,128)(2,1)S(1)}, u32[]{:S(2)}, u32[]{:S(2)}) collective-permute-start(bf16[64,3072]{1,0:T(8,128)(2,1)} %slice.16), channel_id=1, source_target_pairs={{0,32},{32,0},{1,33},{33,1},{2,34},{34,2},{3,35},{35,3},{4,36},{36... | collective-permute-start | bytes 1179656 | tf_op jit(solution)/shard_map/ppermute | solution.py:66
  49.5 12.8 %collective-permute-start.10 = (bf16[64,3072]{1,0:T(8,128)(2,1)}, bf16[64,3072]{1,0:T(8,128)(2,1)}, u32[]{:S(2)}, u32[]{:S(2)}) collective-permute-start(bf16[64,3072]{1,0:T(8,128)(2,1)} %slice.17), channel_id=1, source_target_pairs={{0,96},{32,64},{64,32},{96,0},{1,97},{33,65},{65,33},{97,1},{2,98}... | collective-permute-start | bytes 1179656 | tf_op jit(solution)/shard_map/ppermute | solution.py:74
  62.2 14.5 %collective-permute-start.22 = (bf16[4,1664,128]{2,1,0:T(8,128)(2,1)S(1)}, bf16[4,1664,128]{2,1,0:T(8,128)(2,1)}, u32[]{:S(2)}, u32[]{:S(2)}) collective-permute-start(bf16[4,1664,128]{2,1,0:T(8,128)(2,1)S(1)} %all-to-all-done.own), channel_id=1, source_target_pairs={{0,4},{4,0},{1,5},{5,1},{2,6},{6,2},{3,7},{7,3},{8,12},{12,8},{9,1... | collective-permute-start | bytes 5111816 | tf_op jit(solution)/shard_map/ppermute | solution.py:66
  71.9 15.0 %collective-permute-start.19 = (bf16[768,128]{1,0:T(8,128)(2,1)S(1)}, bf16[768,128]{1,0:T(8,128)(2,1)S(1)}, u32[]{:S(2)}, u32[]{:S(2)}) collective-permute-start(bf16[768,128]{1,0:T(8,128)(2,1)S(1)} %get-tuple-element.148), channel_id=1, source_target_pairs={{0,8},{8,0},{16,24},{24,16},{1,9},{9,1},{17,25},{25,17},{2,10},{10... | collective-permute-start | bytes 589832 | tf_op jit(solution)/shard_map/ppermute | solution.py:78
  73.7 13.2 %collective-permute-start.20 = (bf16[768,128]{1,0:T(8,128)(2,1)S(1)}, bf16[768,128]{1,0:T(8,128)(2,1)S(1)}, u32[]{:S(2)}, u32[]{:S(2)}) collective-permute-start(bf16[768,128]{1,0:T(8,128)(2,1)S(1)} %get-tuple-element.149), channel_id=1, source_target_pairs={{0,16},{8,24},{16,0},{24,8},{1,17},{9,25},{17,1},{25,9},{2,18},{10... | collective-permute-start | bytes 589832 | tf_op jit(solution)/shard_map/ppermute | solution.py:78
  76.4 12.2 %collective-permute-start.21 = (bf16[768,128]{1,0:T(8,128)(2,1)S(1)}, bf16[768,128]{1,0:T(8,128)(2,1)S(1)}, u32[]{:S(2)}, u32[]{:S(2)}) collective-permute-start(bf16[768,128]{1,0:T(8,128)(2,1)S(1)} %get-tuple-element.150), channel_id=1, source_target_pairs={{0,24},{8,16},{16,8},{24,0},{1,25},{9,17},{17,9},{25,1},{2,26},{10... | collective-permute-start | bytes 589832 | tf_op jit(solution)/shard_map/ppermute | solution.py:78
  100.1 13.3 %collective-permute-start.26 = (bf16[896,128]{1,0:T(8,128)(2,1)S(1)}, bf16[896,128]{1,0:T(8,128)(2,1)S(1)}, u32[]{:S(2)}, u32[]{:S(2)}) collective-permute-start(bf16[896,128]{1,0:T(8,128)(2,1)S(1)} %get-tuple-element.196), channel_id=1, source_target_pairs={{0,16},{8,24},{16,0},{24,8},{1,17},{9,25},{17,1},{25,9},{2,18},{10... | collective-permute-start | bytes 688136 | tf_op jit(solution)/shard_map/ppermute | solution.py:78
  102.9 13.1 %collective-permute-start.27 = (bf16[896,128]{1,0:T(8,128)(2,1)S(1)}, bf16[896,128]{1,0:T(8,128)(2,1)S(1)}, u32[]{:S(2)}, u32[]{:S(2)}) collective-permute-start(bf16[896,128]{1,0:T(8,128)(2,1)S(1)} %get-tuple-element.197), channel_id=1, source_target_pairs={{0,24},{8,16},{16,8},{24,0},{1,25},{9,17},{17,9},{25,1},{2,26},{10... | collective-permute-start | bytes 688136 | tf_op jit(solution)/shard_map/ppermute | solution.py:78
  116.7 15.6 %collective-permute-start.31 = (bf16[416,512]{1,0:T(8,128)(2,1)S(1)}, bf16[416,512]{1,0:T(8,128)(2,1)S(1)}, u32[]{:S(2)}, u32[]{:S(2)}) collective-permute-start(bf16[416,512]{1,0:T(8,128)(2,1)S(1)} %get-tuple-element.206), channel_id=1, source_target_pairs={{0,32},{32,0},{1,33},{33,1},{2,34},{34,2},{3,35},{35,3},{4,36},{36... | collective-permute-start | bytes 1277960 | tf_op jit(solution)/shard_map/ppermute | solution.py:66
  116.9 22.2 %collective-permute-start.35 = (bf16[416,512]{1,0:T(8,128)(2,1)S(1)}, bf16[416,512]{1,0:T(8,128)(2,1)S(1)}, u32[]{:S(2)}, u32[]{:S(2)}) collective-permute-start(bf16[416,512]{1,0:T(8,128)(2,1)S(1)} %get-tuple-element.217), channel_id=1, source_target_pairs={{0,64},{64,0},{1,65},{65,1},{2,66},{66,2},{3,67},{67,3},{4,68},{68... | collective-permute-start | bytes 1277960 | tf_op jit(solution)/shard_map/ppermute | solution.py:66
  119.6 22.8 %collective-permute-start.36 = (bf16[416,512]{1,0:T(8,128)(2,1)S(1)}, bf16[416,512]{1,0:T(8,128)(2,1)S(1)}, u32[]{:S(2)}, u32[]{:S(2)}) collective-permute-start(bf16[416,512]{1,0:T(8,128)(2,1)S(1)} %get-tuple-element.218), channel_id=1, source_target_pairs={{0,96},{32,64},{64,32},{96,0},{1,97},{33,65},{65,33},{97,1},{2,98}... | collective-permute-start | bytes 1277960 | tf_op jit(solution)/shard_map/ppermute | solution.py:74
  133.0 11.5 %collective-permute-start.32 = (bf16[416,256]{1,0:T(8,128)(2,1)S(1)}, bf16[416,256]{1,0:T(8,128)(2,1)S(1)}, u32[]{:S(2)}, u32[]{:S(2)}) collective-permute-start(bf16[416,256]{1,0:T(8,128)(2,1)S(1)} %get-tuple-element.212), channel_id=1, source_target_pairs={{0,32},{32,0},{1,33},{33,1},{2,34},{34,2},{3,35},{35,3},{4,36},{36... | collective-permute-start | bytes 638984 | tf_op jit(solution)/shard_map/ppermute | solution.py:66
  133.8 12.5 %collective-permute-start.33 = (bf16[416,256]{1,0:T(8,128)(2,1)S(1)}, bf16[416,256]{1,0:T(8,128)(2,1)S(1)}, u32[]{:S(2)}, u32[]{:S(2)}) collective-permute-start(bf16[416,256]{1,0:T(8,128)(2,1)S(1)} %get-tuple-element.213), channel_id=1, source_target_pairs={{0,64},{64,0},{1,65},{65,1},{2,66},{66,2},{3,67},{67,3},{4,68},{68... | collective-permute-start | bytes 638984 | tf_op jit(solution)/shard_map/ppermute | solution.py:66
  135.9 13.0 %collective-permute-start.34 = (bf16[416,256]{1,0:T(8,128)(2,1)S(1)}, bf16[416,256]{1,0:T(8,128)(2,1)S(1)}, u32[]{:S(2)}, u32[]{:S(2)}) collective-permute-start(bf16[416,256]{1,0:T(8,128)(2,1)S(1)} %get-tuple-element.214), channel_id=1, source_target_pairs={{0,96},{32,64},{64,32},{96,0},{1,97},{33,65},{65,33},{97,1},{2,98}... | collective-permute-start | bytes 638984 | tf_op jit(solution)/shard_map/ppermute | solution.py:74
  (23 other events, 181.7 us)
